TPU v7x, 32 devices: a whole 2x2x4 slice. The times are simulated.
32 devices in a mesh: cfg: 8 (over y, x, core), tm: 4 (over z).
Axes of the slice: x: 2, y: 2, z: 4, core: 2. Of those that a mesh axis runs over, the one named last changes fastest.
Arguments:
- targets: float32 [2048, 512], P('cfg', 'tm'), may hold values from -6 to 6
- features: float32 [2048, 64], P('cfg'), may hold values from -6 to 6
- inv_scales: float32 [64], replicated, may hold values from 0.05 to 0.3
- noise: float32 [2048], P('cfg'), may hold values from 0.1 to 1
- time_kernel: float32 [512, 512], P('tm'), may hold values from -1 to 1, as said below
- block_mask: int32 [2048, 4], P('cfg', 'tm'), may hold values from 0 to 1, as said below
Outputs:
- solution_field: float32 [2048, 512], P('cfg', 'tm')
- residual: float32 [2048, 512], P('cfg', 'tm')
Inputs may be any that keep to these rules, and one draw needn't show every extreme that they name: `block_mask`: each configuration observes one contiguous run of blocks that starts at a block of 0 to 1 and has at least one block; some runs start late and some reach the last block. `time_kernel`: symmetric positive definite, with unit diagonal.
All inputs are finite; a program needn't handle non-finite values.
Results may differ from a plain program's by a relative error of at most 0.00026.
Values sent between devices are 32-bit elements; how exact they have to be, the bound alone decides.
No kernel may reach another device: no remote copies, remote signals or barrier semaphores. Data moves between devices by JAX's collectives and lax.ppermute only.
A program may use at most 64 MiB of HBM per device.

v0:
```python
import jax
import jax.numpy as jnp
from jax import lax
from jax.sharding import PartitionSpec as P

BLOCK = 128
ITERS = 2


def matern(left, right):
    cross = jnp.dot(
        left, right.T, precision=lax.Precision.HIGHEST, preferred_element_type=jnp.float32
    )
    dist2 = (
        jnp.sum(left * left, axis=1)[:, None]
        + jnp.sum(right * right, axis=1)[None, :]
        - 2.0 * cross
    )
    scaled_dist = jnp.sqrt(3.0) * jnp.sqrt(jnp.maximum(dist2, 0.0))
    return (1.0 + scaled_dist) * jnp.exp(-scaled_dist)


def body(targets, features, inv_scales, noise, time_kernel, block_mask):
    mask = jnp.repeat(block_mask.astype(jnp.float32), BLOCK, axis=1)
    scaled = features * inv_scales[None, :]
    every = lax.all_gather(scaled, "cfg", axis=0, tiled=True)
    tile = matern(scaled, every)
    residual = mask * targets
    direction = residual
    solution_field = jnp.zeros_like(residual)
    norm_now = lax.psum(jnp.sum(residual * residual), ("cfg", "tm"))
    for step in range(ITERS):
        operate_mixed = jnp.dot(
            tile,
            lax.all_gather(mask * direction, "cfg", axis=0, tiled=True),
            precision=lax.Precision.HIGHEST,
            preferred_element_type=jnp.float32,
        )
        image = (
            mask
            * lax.psum_scatter(
                jnp.dot(
                    time_kernel.T,
                    operate_mixed.T,
                    precision=lax.Precision.HIGHEST,
                    preferred_element_type=jnp.float32,
                ),
                "tm",
                scatter_dimension=0,
                tiled=True,
            ).T
            + noise[:, None] * direction
        )
        curv, cross_term, image_sq = lax.psum(
            (jnp.sum(direction * image), jnp.sum(residual * image), jnp.sum(image * image)),
            ("cfg", "tm"),
        )
        alpha = norm_now / curv
        solution_field = solution_field + alpha * direction
        residual = residual - alpha * image
        norm_next = norm_now - 2.0 * alpha * cross_term + alpha * alpha * image_sq
        direction = residual + norm_next / norm_now * direction
        norm_now = norm_next
    return (solution_field, residual)


def solution(mesh):
    return jax.shard_map(
        body,
        mesh=mesh,
        in_specs=(P("cfg", "tm"), P("cfg", None), P(), P("cfg"), P("tm", None), P("cfg", "tm")),
        out_specs=(P("cfg", "tm"), P("cfg", "tm")),
        check_vma=False,
    )
```

profile of v0, /device:TPU:0, one launch (start us, length us, event | category | flops | bytes accessed | tf_op | source)
XLA Modules:
  0.0 208.2 jit_solution(3787569362566161704)
XLA Ops:
  7.2 0.0 copy-start
  7.2 0.0 all-gather.3.cloned.1.call-start
  7.2 0.7 convert_element_type.5
  7.9 1.7 multiply_multiply_fusion
  9.6 0.0 all-gather.3.cloned.1.call-update
  9.6 0.0 reduce-scatter.3.cloned.1.call-start
  9.7 0.9 multiply_reduce_fusion.5
  10.6 11.3 %all_gather.9 = f32[2048,64]{0,1:T(8,128)S(1)} all-gather(f32[256,64]{0,1:T(8,128)S(1)} %get-tuple-element.9), channel_id=1, replica_groups=mesh['cfg'=8,'tm'=4] {'cfg'}, dimensions={0}, use_global_device_ids=true | all-gather | bytes 589824 | tf_op jit(solution)/shard_map/all_gather | solution.py:26
  21.9 0.1 multiply_reduce_fusion
  22.0 2.9 %exponential_multiply_fusion = f32[256,2048]{1,0:T(8,128)S(1)} fusion(f32[256,64]{0,1:T(8,128)S(1)} %get-tuple-element.9, f32[2048,64]{0,1:T(8,128)S(1)} %all_gather.9, f32[2048]{0:T(1024)S(1)} %multiply_reduce_fusion, f32[256]{0:T(256)S(1)} %get-tuple-element.8), kind=kOutput, calls=%fused_computation.5 | convolution fusion | flops 406847488 | bytes 2696192 | tf_op jit(solution)/shard_map/dot_general | solution.py:11
  24.9 0.0 copy-start.1
  24.9 0.0 copy-start.3
  24.9 11.8 %all-gather.3.cloned.1.call-done = f32[2048,128]{1,0:T(8,128)} async-done(((f32[256,128]{1,0:T(8,128)}), f32[2048,128]{1,0:T(8,128)}) %all-gather.3.cloned.1.call-update) | async-done | bytes 1048592 | tf_op jit(solution)/shard_map/all_gather | solution.py:35
  36.7 3.0 %fusion.4 = f32[256,128]{1,0:T(8,128)S(1)} fusion(f32[256,2048]{1,0:T(8,128)S(1)} %exponential_multiply_fusion, f32[2048,128]{1,0:T(8,128)} %all-gather.3.cloned.1.call-done), kind=kOutput, calls=%fused_computation.23 | convolution fusion | flops 805306368 | bytes 3276800 | tf_op jit(solution)/shard_map/dot_general | solution.py:33
  39.7 0.0 copy-done
  39.8 1.4 convolution_bitcast_fusion.1
  41.1 0.0 reduce-scatter.3.cloned.1.call-update
  41.1 0.0 all-gather.5.cloned.1.call-start
  41.2 21.7 %reduce-scatter.3.cloned.1.call-done = f32[128,256]{0,1:T(8,128)} async-done(((f32[512,256]{0,1:T(8,128)}), f32[128,256]{0,1:T(8,128)}) %reduce-scatter.3.cloned.1.call-update) | async-done | bytes 131088 | tf_op jit(solution)/shard_map/reduce_scatter | solution.py:41
  62.9 0.0 copy-done.1
  62.9 0.0 copy-done.3
  62.9 1.8 multiply_reduce_fusion.2
  64.7 38.8 %all-reduce = (f32[]{:T(128)}, f32[]{:T(128)}, f32[]{:T(128)}) all-reduce(f32[]{:T(128)} %get-tuple-element.4, f32[]{:T(128)} %get-tuple-element.3, f32[]{:T(128)} %get-tuple-element.2), channel_id=1, replica_groups=mesh['cfg'=8,'tm'=4] {'cfg','tm'}, use_global_device_ids=true, to_apply=%region_1.0 | all-reduce | flops 3 | bytes 24 | tf_op jit(solution)/shard_map/psum | solution.py:31
  107.2 1.7 broadcast_multiply_fusion
  109.0 0.0 all-gather.5.cloned.1.call-update
  109.0 0.0 copy-start.2
  109.0 0.0 reduce-scatter.5.cloned.1.call-start
  109.0 23.5 %all-gather.5.cloned.1.call-done = f32[2048,128]{1,0:T(8,128)} async-done(((f32[256,128]{1,0:T(8,128)}), f32[2048,128]{1,0:T(8,128)}) %all-gather.5.cloned.1.call-update) | async-done | bytes 1048592 | tf_op jit(solution)/shard_map/all_gather | solution.py:35
  132.6 3.0 %fusion.5 = f32[256,128]{1,0:T(8,128)S(1)} fusion(f32[256,2048]{1,0:T(8,128)S(1)} %exponential_multiply_fusion, f32[2048,128]{1,0:T(8,128)} %all-gather.5.cloned.1.call-done), kind=kOutput, calls=%fused_computation.24 | convolution fusion | flops 805306368 | bytes 3276800 | tf_op jit(solution)/shard_map/dot_general | solution.py:33
  135.6 1.4 convolution_bitcast_fusion
  137.0 0.0 reduce-scatter.5.cloned.1.call-update
  137.0 21.8 %reduce-scatter.5.cloned.1.call-done = f32[128,256]{0,1:T(8,128)} async-done(((f32[512,256]{0,1:T(8,128)}), f32[128,256]{0,1:T(8,128)}) %reduce-scatter.5.cloned.1.call-update) | async-done | bytes 131088 | tf_op jit(solution)/shard_map/reduce_scatter | solution.py:41
  158.8 0.0 copy-done.2
  158.8 1.7 multiply_reduce_fusion.1
  160.5 38.7 %psum.34 = f32[]{:T(128)} all-reduce(f32[]{:T(128)} %multiply_reduce_fusion.1), channel_id=1, replica_groups=mesh['cfg'=8,'tm'=4] {'cfg','tm'}, use_global_device_ids=true, to_apply=%region_11.0 | all-reduce | flops 1 | bytes 8 | tf_op jit(solution)/shard_map/psum | solution.py:54
  199.9 1.8 multiply_subtract_fusion
Async XLA Ops:
  7.2 32.6 %copy-start = (f32[128,512]{1,0:T(8,128)S(1)}, f32[128,512]{1,0:T(8,128)}, u32[]{:S(2)}) copy-start(f32[128,512]{1,0:T(8,128)} %param.10) | copy-start | bytes 786436
  7.2 29.5 %all-gather.3.cloned.1.call-start = ((), (), s32[]{:S(2)}) async-start(), calls=%async_computation.2 | async-start | bytes 1179648 | tf_op jit(solution)/shard_map/all_gather | solution.py:35
  9.6 53.3 %reduce-scatter.3.cloned.1.call-start = ((), (), s32[]{:S(2)}) async-start(), calls=%async_computation.3 | async-start | bytes 655360 | tf_op jit(solution)/shard_map/reduce_scatter | solution.py:41
  24.9 38.0 %copy-start.1 = (f32[256,128]{1,0:T(8,128)S(1)}, f32[256,128]{1,0:T(8,128)}, u32[]{:S(2)}) copy-start(f32[256,128]{1,0:T(8,128)} %param.6) | copy-start | bytes 393220
  24.9 38.0 %copy-start.3 = (f32[256]{0:T(256)S(1)}, f32[256]{0:T(256)}, u32[]{:S(2)}) copy-start(f32[256]{0:T(256)} %param.9) | copy-start | bytes 3076
  41.1 91.4 %all-gather.5.cloned.1.call-start = ((), (), s32[]{:S(2)}) async-start(), calls=%async_computation.4 | async-start | bytes 1179648 | tf_op jit(solution)/shard_map/all_gather | solution.py:35
  109.0 49.8 %copy-start.2 = (f32[128,256]{0,1:T(8,128)S(1)}, f32[128,256]{0,1:T(8,128)}, u32[]{:S(2)}) copy-start(f32[128,256]{0,1:T(8,128)} %reduce-scatter.3.cloned.1.call-done) | copy-start | bytes 393220
  109.0 49.8 %reduce-scatter.5.cloned.1.call-start = ((), (), s32[]{:S(2)}) async-start(), calls=%async_computation.5 | async-start | bytes 655360 | tf_op jit(solution)/shard_map/reduce_scatter | solution.py:41
Sparse Core Ops, SparseCore 0:
  10.5 26.1 all-gather.2
  41.3 21.6 reduce-scatter.2
  109.1 23.4 all-gather.4
  137.1 21.6 reduce-scatter.4
where the time goes:
time: 209 us; the launch traced here: 208 us
  blocking collectives  88.9 us (43%)
  waiting for transfers between devices  78.9 us (38%)
  between operations  18.2 us (9%)
  matrix products  11.7 us (6%)
  other arithmetic  10.3 us (5%)
    reduce_scatter x2, waiting for transfers between devices, body(): lax.psum_scatter(jnp.dot(time_kernel.T, operate_mixed.T, precision=lax.Pr...  43.5 us
    psum x1, blocking collectives, body(): norm_now = lax.psum(jnp.sum(residual * residual), ('cfg', 'tm'))  38.8 us
    psum x1, blocking collectives, body(): lax.psum((jnp.sum(direction * image), jnp.sum(residual * image), jnp.sum(...  38.7 us
    all_gather x2, waiting for transfers between devices, body(): lax.all_gather(mask * direction, 'cfg', axis=0, tiled=True)  35.3 us
    all_gather x1, blocking collectives, body(): every = lax.all_gather(scaled, 'cfg', axis=0, tiled=True)  11.3 us
    dot_general x2, matrix products, body(): jnp.dot(tile, lax.all_gather(mask * direction, 'cfg', axis=0, tiled=True)...  6.06 us
  transfers between devices with their start and end apart: 4, of which 4 were waited for; matrix products, arithmetic and copies ran while one was open for 2% of the time, Pallas kernels for 0%

commit v1 on v0

v1 whole, which is shorter than its diff:
```python
import jax
import jax.numpy as jnp
from jax import lax
from jax.sharding import PartitionSpec as P

HIGH = lax.Precision.HIGH
HIGHEST = lax.Precision.HIGHEST


def dot(left, right, precision=HIGH):
    return jnp.dot(left, right, precision=precision, preferred_element_type=jnp.float32)


def partners(count, offset):
    return [(index, index ^ offset) for index in range(count)]


def gather_cfg(block, count):
    own = [block] + [lax.ppermute(block, "cfg", partners(count, d)) for d in range(2, count, 2)]
    other = [lax.ppermute(piece, "cfg", partners(count, 1)) for piece in own]
    return [piece for pair in zip(own, other) for piece in pair]


def total(value, count):
    sent = jnp.broadcast_to(value[None, :, None], (count, 8, 128))
    got = lax.all_to_all(sent, ("cfg", "tm"), 0, 0, tiled=True)
    return jnp.sum(got, axis=0)[:, 0]


def matern(left, right_t):
    cross = dot(left, right_t, HIGHEST)
    dist2 = (
        jnp.sum(left * left, axis=1)[:, None]
        + jnp.sum(right_t * right_t, axis=0)[None, :]
        - 2.0 * cross
    )
    scaled_dist = jnp.sqrt(3.0) * jnp.sqrt(jnp.maximum(dist2, 0.0))
    return (1.0 + scaled_dist) * jnp.exp(-scaled_dist)


def solution(mesh):
    cfg, tm = mesh.shape["cfg"], mesh.shape["tm"]
    everyone = cfg * tm

    def body(targets, features, inv_scales, noise, time_kernel, block_mask):
        mask = block_mask.astype(jnp.float32)
        ridge = noise[:, None]
        scaled = features * inv_scales[None, :]
        every_t = jnp.concatenate(gather_cfg(scaled.T, cfg), axis=1)
        residual = mask * targets
        steps = time_kernel.T

        def over_time(field):
            rows = lax.all_gather(field, "tm", axis=0)
            mixed = dot(rows[0], steps[: field.shape[1]])
            for part in range(1, tm):
                mixed = mixed + dot(rows[part], steps[part * field.shape[1] : (part + 1) * field.shape[1]])
            return mixed

        timed = over_time(residual)
        tile = matern(scaled, every_t)

        def over_cfg(field):
            return dot(tile, jnp.concatenate(gather_cfg(field, cfg), axis=0))

        image = mask * over_cfg(timed) + ridge * residual
        second = mask * over_cfg(over_time(image)) + ridge * image
        parts = jnp.stack(
            [
                jnp.sum(residual * residual),
                jnp.sum(residual * image),
                jnp.sum(image * image),
                jnp.sum(image * second),
            ]
            + [jnp.float32(0.0)] * 4
        )
        sums = total(parts, everyone)
        alpha = sums[0] / sums[1]
        norm = sums[0] - 2.0 * alpha * sums[1] + alpha * alpha * sums[2]
        ratio = norm / sums[0]
        keep = 1.0 + ratio
        curv = keep * keep * sums[1] - 2.0 * keep * alpha * sums[2] + alpha * alpha * sums[3]
        beta = norm / curv
        direction = keep * residual - alpha * image
        solution_field = alpha * residual + beta * direction
        left = residual - alpha * image - beta * (keep * image - alpha * second)
        return (solution_field, left)

    return jax.shard_map(
        body,
        mesh=mesh,
        in_specs=(P("cfg", "tm"), P("cfg", None), P(), P("cfg"), P("tm", None), P("cfg", "tm")),
        out_specs=(P("cfg", "tm"), P("cfg", "tm")),
        check_vma=False,
    )
```

time: 209 us -> 98.3 us (0.47)
  waiting for transfers between devices: 78.9 us -> 16.4 us
  blocking collectives: 88.9 us -> 46.5 us
  starting transfers between devices: 0.16 us -> 11.8 us
  between operations: 18.2 us -> 6.78 us
  other arithmetic: 10.3 us -> 2.78 us
  local copies, waits for them, and re-layouts: 0.03 us -> 3.52 us
    psum x2 -> x0, blocking collectives: 77.6 us -> none  [the longest x1 38.8 us: body(): norm_now = lax.psum(jnp.sum(residual * residual), ('cfg', 'tm'))]
    reduce_scatter x2 -> x0, waiting for transfers between devices: 43.5 us -> none  [body(): lax.psum_scatter(jnp.dot(time_kernel.T, operate_mixed.T, precision=lax.Pr...]
    all_gather x2 -> x0, waiting for transfers between devices: 35.3 us -> none  [body(): lax.all_gather(mask * direction, 'cfg', axis=0, tiled=True)]
    all_gather x1 -> x2, blocking collectives: 11.3 us -> 34.1 us  [over_time(): rows = lax.all_gather(field, 'tm', axis=0)]
    ppermute x0 -> x21, waiting for transfers between devices: none -> 16.4 us  [the longest x9 12.6 us: gather_cfg(): lax.ppermute(block, 'cfg', partners(count, d))]
    all_to_all x0 -> x1, blocking collectives: none -> 12.4 us  [total(): got = lax.all_to_all(sent, ('cfg', 'tm'), 0, 0, tiled=True)]
    ppermute x0 -> x21, starting transfers between devices: none -> 11.8 us  [the longest x9 10.4 us: gather_cfg(): lax.ppermute(block, 'cfg', partners(count, d))]
    reduce_sum x3 -> x2, other arithmetic: 3.51 us -> 0.09 us  [the longest x1 0.05 us: matern(): jnp.sum(right_t * right_t, axis=0)[None, :]]
  transfers between devices with their start and end apart: 4 -> 21, of which waited for: 4 -> 12; matrix products, arithmetic and copies ran while one was open for 2% -> 3% of each run, Pallas kernels for 0% -> 0%
where the time goes in v1:
time: 98.3 us; the launch traced here: 97.9 us
  blocking collectives  46.5 us (47%)
  waiting for transfers between devices  16.4 us (17%)
  starting transfers between devices  11.8 us (12%)
  matrix products  10.1 us (10%)
  between operations  6.78 us (7%)
  local copies, waits for them, and re-layouts  3.52 us (4%)
  other arithmetic  2.78 us (3%)
    all_gather x2, blocking collectives, over_time(): rows = lax.all_gather(field, 'tm', axis=0)  34.1 us
    ppermute x9, waiting for transfers between devices, gather_cfg(): lax.ppermute(block, 'cfg', partners(count, d))  12.6 us
    all_to_all x1, blocking collectives, total(): got = lax.all_to_all(sent, ('cfg', 'tm'), 0, 0, tiled=True)  12.4 us
    ppermute x9, starting transfers between devices, gather_cfg(): lax.ppermute(block, 'cfg', partners(count, d))  10.4 us
    dot_general x11, matrix products, dot(): jnp.dot(left, right, precision=precision, preferred_element_type=jnp.floa...  10.1 us
    ppermute x12, waiting for transfers between devices, gather_cfg(): other = [lax.ppermute(piece, 'cfg', partners(count, 1)) for piece in own]  3.79 us
    another operation x1, local copies, waits for them, and re-layouts, body(): jnp.stack([jnp.sum(residual * residual), jnp.sum(residual * image), jnp.s...  2.63 us
  transfers between devices with their start and end apart: 21, of which 12 were waited for; matrix products, arithmetic and copies ran while one was open for 3% of the time, Pallas kernels for 0%

profile of v1, /device:TPU:0, one launch (start us, length us, event | category | flops | bytes accessed | tf_op | source)
XLA Modules:
  0.0 97.9 jit_solution(4996756083297980389)
XLA Ops:
  0.7 0.7 convert_element_type.3
  1.4 1.0 %broadcast_multiply_fusion = f32[256,128]{1,0:T(8,128)S(1)} fusion(f32[256,128]{1,0:T(8,128)} %param.6, f32[256]{0:T(256)S(1)} %bitcast.26), kind=kLoop, calls=%fused_computation.30 | loop fusion | flops 32768 | bytes 263168 | tf_op jit(solution)/shard_map/mul | solution.py:50
  2.4 17.4 %all-gather = f32[1024,128]{1,0:T(8,128)S(1)} all-gather(f32[256,128]{1,0:T(8,128)S(1)} %broadcast_multiply_fusion), channel_id=2, replica_groups=mesh['cfg'=8,'tm'=4] {'tm'}, dimensions={0}, use_global_device_ids=true | all-gather | bytes 655360 | tf_op jit(solution)/shard_map/all_gather | solution.py:54
  19.7 1.1 %fusion.10 = f32[256,128]{1,0:T(8,128)S(1)} fusion(f32[1024,128]{1,0:T(8,128)S(1)} %all-gather, f32[512,128]{0,1:T(8,128)} %bitcast.18), kind=kOutput, calls=%fused_computation.21 | convolution fusion | flops 25165824 | bytes 327680 | tf_op jit(solution)/shard_map/dot_general | solution.py:11
  20.8 1.1 %convolution_add_fusion.5 = f32[256,128]{1,0:T(8,128)S(1)} fusion(f32[256,128]{1,0:T(8,128)S(1)} %fusion.10, f32[1024,128]{1,0:T(8,128)S(1)} %all-gather, f32[512,128]{0,1:T(8,128)} %bitcast.19), kind=kOutput, calls=%fused_computation.7 | convolution fusion | flops 25198592 | bytes 458752 | tf_op jit(solution)/shard_map/dot_general | solution.py:11
  21.9 1.1 %convolution_add_fusion.4 = f32[256,128]{1,0:T(8,128)S(1)} fusion(f32[256,128]{1,0:T(8,128)S(1)} %convolution_add_fusion.5, f32[1024,128]{1,0:T(8,128)S(1)} %all-gather, f32[512,128]{0,1:T(8,128)} %bitcast.20), kind=kOutput, calls=%fused_computation.6 | convolution fusion | flops 25198592 | bytes 458752 | tf_op jit(solution)/shard_map/dot_general | solution.py:11
  23.0 0.2 constant_dynamic-update-slice_fusion.15
  23.2 0.1 collective-permute-start.7
  23.3 1.6 %collective-permute-start.8 = (f32[256,128]{1,0:T(8,128)S(1)}, f32[256,128]{1,0:T(8,128)S(1)}, u32[]{:S(2)}, u32[]{:S(2)}) collective-permute-start(f32[256,128]{1,0:T(8,128)S(1)} %get-tuple-element.15), channel_id=1, source_target_pairs={{0,8},{4,12},{8,0},{12,4},{16,24},{20,28},{24,16},{28,20},{1,9},{5... | collective-permute-start | bytes 393224 | tf_op jit(solution)/shard_map/ppermute | solution.py:19
  24.9 1.5 %collective-permute-start.10 = (f32[256,128]{1,0:T(8,128)S(1)}, f32[256,128]{1,0:T(8,128)S(1)}, u32[]{:S(2)}, u32[]{:S(2)}) collective-permute-start(f32[256,128]{1,0:T(8,128)S(1)} %get-tuple-element.15), channel_id=1, source_target_pairs={{0,16},{4,20},{8,24},{12,28},{16,0},{20,4},{24,8},{28,12},{1,17},{... | collective-permute-start | bytes 393224 | tf_op jit(solution)/shard_map/ppermute | solution.py:19
  26.4 0.1 constant_dynamic-update-slice_fusion.7
  26.6 0.6 collective-permute-start.1
  27.2 0.1 multiply_reduce_fusion.5
  27.2 0.5 collective-permute-done
  27.8 0.5 collective-permute-start.3
  28.3 2.8 %collective-permute-done.1 = f32[64,256]{1,0:T(8,128)S(1)} collective-permute-done((f32[64,256]{1,0:T(8,128)S(1)}, f32[64,256]{1,0:T(8,128)S(1)}, u32[]{:S(2)}, u32[]{:S(2)}) %collective-permute-start.1) | collective-permute-done | bytes 65568 | tf_op jit(solution)/shard_map/ppermute | solution.py:19
  31.1 1.0 collective-permute-done.3
  32.1 1.3 %collective-permute-start.5 = (f32[64,256]{1,0:T(8,128)S(1)}, f32[64,256]{1,0:T(8,128)S(1)}, u32[]{:S(2)}, u32[]{:S(2)}) collective-permute-start(f32[64,256]{1,0:T(8,128)S(1)} %get-tuple-element.7), channel_id=1, source_target_pairs={{0,24},{4,28},{8,16},{12,20},{16,8},{20,12},{24,0},{28,4},{1,25},{... | collective-permute-start | bytes 196616 | tf_op jit(solution)/shard_map/ppermute | solution.py:19
  33.4 3.8 %collective-permute-done.5 = f32[64,256]{1,0:T(8,128)S(1)} collective-permute-done((f32[64,256]{1,0:T(8,128)S(1)}, f32[64,256]{1,0:T(8,128)S(1)}, u32[]{:S(2)}, u32[]{:S(2)}) %collective-permute-start.5) | collective-permute-done | bytes 65568 | tf_op jit(solution)/shard_map/ppermute | solution.py:19
  37.2 1.4 %collective-permute-start.12 = (f32[256,128]{1,0:T(8,128)S(1)}, f32[256,128]{1,0:T(8,128)S(1)}, u32[]{:S(2)}, u32[]{:S(2)}) collective-permute-start(f32[256,128]{1,0:T(8,128)S(1)} %get-tuple-element.15), channel_id=1, source_target_pairs={{0,24},{4,28},{8,16},{12,20},{16,8},{20,12},{24,0},{28,4},{1,25},{... | collective-permute-start | bytes 393224 | tf_op jit(solution)/shard_map/ppermute | solution.py:19
  38.6 1.2 %collective-permute-done.6 = f32[64,256]{1,0:T(8,128)S(1)} collective-permute-done((f32[64,256]{1,0:T(8,128)S(1)}, f32[64,256]{1,0:T(8,128)S(1)}, u32[]{:S(2)}, u32[]{:S(2)}) %collective-permute-start.6) | collective-permute-done | bytes 65568 | tf_op jit(solution)/shard_map/ppermute | solution.py:20
  39.9 3.0 %exponential_multiply_fusion = f32[256,2048]{1,0:T(8,128)S(1)} fusion(f32[64,2048]{1,0:T(8,128)S(1)} %constant_dynamic-update-slice_fusion, f32[2048]{0:T(1024)S(1)} %multiply_reduce_fusion, f32[256]{0:T(256)S(1)} %multiply_reduce_fusion.5, f32[256,64]{0,1:T(8,128)S(1)} %copy-done.2, f32[64]{0:T(128)S(1)} %copy-done.4), kind=kOutput, calls=%fused_computation.1 | convolution fusion | flops 406863872 | bytes 2696448 | tf_op jit(solution)/shard_map/dot_general | solution.py:11
  42.9 0.2 collective-permute-start.9
  43.2 0.4 collective-permute-start.11
  43.5 0.1 collective-permute-start.13
  43.7 0.6 collective-permute-done.9
  44.4 0.2 collective-permute-done.11
  44.6 0.3 collective-permute-done.13
  44.9 1.0 %fusion.1 = f32[256,128]{1,0:T(8,128)S(1)} fusion(f32[256,2048]{1,0:T(8,128)S(1)} %exponential_multiply_fusion, f32[2048,128]{1,0:T(8,128)S(1)} %constant_dynamic-update-slice_fusion.8, f32[256]{0:T(256)S(1)} %copy-done.3, f32[256]{0:T(256)S(1)} %bitcast.27, f32[256,128]{1,0:T(8,128)S(1)} %copy-done), kind=kOutput, calls=%fused_computation.11 | convolution fusion | flops 402784256 | bytes 3409920 | tf_op jit(solution)/shard_map/dot_general | solution.py:11
  45.9 16.8 %all-gather.1 = f32[1024,128]{1,0:T(8,128)S(1)} all-gather(f32[256,128]{1,0:T(8,128)S(1)} %fusion.1), channel_id=3, replica_groups=mesh['cfg'=8,'tm'=4] {'tm'}, dimensions={0}, use_global_device_ids=true | all-gather | bytes 655360 | tf_op jit(solution)/shard_map/all_gather | solution.py:54
  62.7 0.2 fusion.5
  62.9 0.2 convolution_add_fusion.2
  63.2 0.2 convolution_add_fusion.1
  63.4 0.2 constant_dynamic-update-slice_fusion.23
  63.7 1.5 %collective-permute-start.15 = (f32[256,128]{1,0:T(8,128)S(1)}, f32[256,128]{1,0:T(8,128)S(1)}, u32[]{:S(2)}, u32[]{:S(2)}) collective-permute-start(f32[256,128]{1,0:T(8,128)S(1)} %get-tuple-element.17), channel_id=1, source_target_pairs={{0,8},{4,12},{8,0},{12,4},{16,24},{20,28},{24,16},{28,20},{1,9},{5... | collective-permute-start | bytes 393224 | tf_op jit(solution)/shard_map/ppermute | solution.py:19
  65.1 0.7 collective-permute-start.17
  65.8 1.4 %collective-permute-start.19 = (f32[256,128]{1,0:T(8,128)S(1)}, f32[256,128]{1,0:T(8,128)S(1)}, u32[]{:S(2)}, u32[]{:S(2)}) collective-permute-start(f32[256,128]{1,0:T(8,128)S(1)} %get-tuple-element.17), channel_id=1, source_target_pairs={{0,24},{4,28},{8,16},{12,20},{16,8},{20,12},{24,0},{28,4},{1,25},{... | collective-permute-start | bytes 393224 | tf_op jit(solution)/shard_map/ppermute | solution.py:19
  67.2 2.7 %collective-permute-done.15 = f32[256,128]{1,0:T(8,128)S(1)} collective-permute-done((f32[256,128]{1,0:T(8,128)S(1)}, f32[256,128]{1,0:T(8,128)S(1)}, u32[]{:S(2)}, u32[]{:S(2)}) %collective-permute-start.15) | collective-permute-done | bytes 131104 | tf_op jit(solution)/shard_map/ppermute | solution.py:19
  69.9 2.3 %collective-permute-done.17 = f32[256,128]{1,0:T(8,128)S(1)} collective-permute-done((f32[256,128]{1,0:T(8,128)S(1)}, f32[256,128]{1,0:T(8,128)S(1)}, u32[]{:S(2)}, u32[]{:S(2)}) %collective-permute-start.17) | collective-permute-done | bytes 131104 | tf_op jit(solution)/shard_map/ppermute | solution.py:19
  72.3 0.5 collective-permute-start.20
  72.9 0.7 collective-permute-done.18
  73.6 0.2 collective-permute-done.20
  73.8 1.7 %multiply_reduce_fusion.1 = (f32[]{:T(128)}, f32[]{:T(128)}, f32[]{:T(128)}, f32[]{:T(128)}, f32[256,128]{1,0:T(8,128)S(1)}) fusion(f32[256,128]{1,0:T(8,128)S(1)} %fusion.1, f32[256]{0:T(256)S(1)} %copy-done.3, f32[256,2048]{1,0:T(8,128)S(1)} %exponential_multiply_fusion, f32[2048,128]{1,0:T(8,128)S(1)} %constant_dynamic-update-slice_fusion.16, ...), kind=kOutput, calls=%fused_computation.25 | convolution fusion | flops 403046400 | bytes 3541008 | tf_op jit(solution)/shard_map/dot_general | solution.py:11
  75.5 2.6 %stack.19 = f32[8]{0:T(128)S(1)} concatenate(f32[1]{0:T(128)} %bitcast.1, f32[1]{0:T(128)} %bitcast.4, f32[1]{0:T(128)} %bitcast.5, f32[1]{0:T(128)} %bitcast.6, f32[4]{0:T(128)S(1)} %broadcast.8), dimensions={0} | concatenate | bytes 64 | tf_op jit(solution)/shard_map/stack | solution.py:68
  78.1 0.1 broadcast_in_dim.2
  78.2 12.4 %all_to_all.5 = f32[32,8,128]{2,1,0:T(8,128)S(1)} all-to-all(f32[32,8,128]{2,1,0:T(8,128)S(1)} %broadcast_in_dim.2), channel_id=1, replica_groups=mesh['cfg'=8,'tm'=4] {'cfg','tm'}, dimensions={0} | all-to-all | bytes 262144 | tf_op jit(solution)/shard_map/all_to_all | solution.py:26
  90.6 0.6 fusion.22
  97.1 0.8 multiply_subtract_fusion
  (50 shorter events, 0.5 us)
Async XLA Ops:
  0.6 22.4 %copy-start.1 = (f32[128,512]{1,0:T(8,128)S(1)}, f32[128,512]{1,0:T(8,128)}, u32[]{:S(2)}) copy-start(f32[128,512]{1,0:T(8,128)} %param.10) | copy-start | bytes 786436
  0.6 25.8 %copy-start.2 = (f32[256,64]{0,1:T(8,128)S(1)}, f32[256,64]{0,1:T(8,128)}, u32[]{:S(2)}) copy-start(f32[256,64]{0,1:T(8,128)} %param.7) | copy-start | bytes 196612
  0.7 25.8 %copy-start.4 = (f32[64]{0:T(128)S(1)}, f32[64]{0:T(128)}, u32[]{:S(2)}) copy-start(f32[64]{0:T(128)} %param.8) | copy-start | bytes 772
  23.2 20.4 %collective-permute-start.7 = (f32[256,128]{1,0:T(8,128)S(1)}, f32[256,128]{1,0:T(8,128)S(1)}, u32[]{:S(2)}, u32[]{:S(2)}) collective-permute-start(f32[256,128]{1,0:T(8,128)S(1)} %get-tuple-element.15), channel_id=1, source_target_pairs={{0,4},{4,0},{8,12},{12,8},{16,20},{20,16},{24,28},{28,24},{1,5},{5... | collective-permute-start | bytes 393224 | tf_op jit(solution)/shard_map/ppermute | solution.py:20
  23.3 19.6 %collective-permute-start.8 = (f32[256,128]{1,0:T(8,128)S(1)}, f32[256,128]{1,0:T(8,128)S(1)}, u32[]{:S(2)}, u32[]{:S(2)}) collective-permute-start(f32[256,128]{1,0:T(8,128)S(1)} %get-tuple-element.15), channel_id=1, source_target_pairs={{0,8},{4,12},{8,0},{12,4},{16,24},{20,28},{24,16},{28,20},{1,9},{5... | collective-permute-start | bytes 393224 | tf_op jit(solution)/shard_map/ppermute | solution.py:19
  24.9 18.3 %collective-permute-start.10 = (f32[256,128]{1,0:T(8,128)S(1)}, f32[256,128]{1,0:T(8,128)S(1)}, u32[]{:S(2)}, u32[]{:S(2)}) collective-permute-start(f32[256,128]{1,0:T(8,128)S(1)} %get-tuple-element.15), channel_id=1, source_target_pairs={{0,16},{4,20},{8,24},{12,28},{16,0},{20,4},{24,8},{28,12},{1,17},{... | collective-permute-start | bytes 393224 | tf_op jit(solution)/shard_map/ppermute | solution.py:19
  26.5 1.3 %collective-permute-start = (f32[64,256]{1,0:T(8,128)S(1)}, f32[64,256]{1,0:T(8,128)S(1)}, u32[]{:S(2)}, u32[]{:S(2)}) collective-permute-start(f32[64,256]{1,0:T(8,128)S(1)} %get-tuple-element.7), channel_id=1, source_target_pairs={{0,4},{4,0},{8,12},{12,8},{16,20},{20,16},{24,28},{28,24},{1,5},{5... | collective-permute-start | bytes 196616 | tf_op jit(solution)/shard_map/ppermute | solution.py:20
  26.6 4.5 %collective-permute-start.1 = (f32[64,256]{1,0:T(8,128)S(1)}, f32[64,256]{1,0:T(8,128)S(1)}, u32[]{:S(2)}, u32[]{:S(2)}) collective-permute-start(f32[64,256]{1,0:T(8,128)S(1)} %get-tuple-element.7), channel_id=1, source_target_pairs={{0,8},{4,12},{8,0},{12,4},{16,24},{20,28},{24,16},{28,20},{1,9},{5... | collective-permute-start | bytes 196616 | tf_op jit(solution)/shard_map/ppermute | solution.py:19
  27.8 4.3 %collective-permute-start.3 = (f32[64,256]{1,0:T(8,128)S(1)}, f32[64,256]{1,0:T(8,128)S(1)}, u32[]{:S(2)}, u32[]{:S(2)}) collective-permute-start(f32[64,256]{1,0:T(8,128)S(1)} %get-tuple-element.7), channel_id=1, source_target_pairs={{0,16},{4,20},{8,24},{12,28},{16,0},{20,4},{24,8},{28,12},{1,17},{... | collective-permute-start | bytes 196616 | tf_op jit(solution)/shard_map/ppermute | solution.py:19
  31.1 2.3 %collective-permute-start.2 = (f32[64,256]{1,0:T(8,128)S(1)}, f32[64,256]{1,0:T(8,128)S(1)}, u32[]{:S(2)}, u32[]{:S(2)}) collective-permute-start(f32[64,256]{1,0:T(8,128)S(1)} %collective-permute-done.1), channel_id=1, source_target_pairs={{0,4},{4,0},{8,12},{12,8},{16,20},{20,16},{24,28},{28,24},{1,5},{5... | collective-permute-start | bytes 196616 | tf_op jit(solution)/shard_map/ppermute | solution.py:20
  32.1 5.2 %collective-permute-start.5 = (f32[64,256]{1,0:T(8,128)S(1)}, f32[64,256]{1,0:T(8,128)S(1)}, u32[]{:S(2)}, u32[]{:S(2)}) collective-permute-start(f32[64,256]{1,0:T(8,128)S(1)} %get-tuple-element.7), channel_id=1, source_target_pairs={{0,24},{4,28},{8,16},{12,20},{16,8},{20,12},{24,0},{28,4},{1,25},{... | collective-permute-start | bytes 196616 | tf_op jit(solution)/shard_map/ppermute | solution.py:19
  33.3 5.2 %collective-permute-start.4 = (f32[64,256]{1,0:T(8,128)S(1)}, f32[64,256]{1,0:T(8,128)S(1)}, u32[]{:S(2)}, u32[]{:S(2)}) collective-permute-start(f32[64,256]{1,0:T(8,128)S(1)} %collective-permute-done.3), channel_id=1, source_target_pairs={{0,4},{4,0},{8,12},{12,8},{16,20},{20,16},{24,28},{28,24},{1,5},{5... | collective-permute-start | bytes 196616 | tf_op jit(solution)/shard_map/ppermute | solution.py:20
  37.2 6.3 %collective-permute-start.12 = (f32[256,128]{1,0:T(8,128)S(1)}, f32[256,128]{1,0:T(8,128)S(1)}, u32[]{:S(2)}, u32[]{:S(2)}) collective-permute-start(f32[256,128]{1,0:T(8,128)S(1)} %get-tuple-element.15), channel_id=1, source_target_pairs={{0,24},{4,28},{8,16},{12,20},{16,8},{20,12},{24,0},{28,4},{1,25},{... | collective-permute-start | bytes 393224 | tf_op jit(solution)/shard_map/ppermute | solution.py:19
  38.6 1.3 %collective-permute-start.6 = (f32[64,256]{1,0:T(8,128)S(1)}, f32[64,256]{1,0:T(8,128)S(1)}, u32[]{:S(2)}, u32[]{:S(2)}) collective-permute-start(f32[64,256]{1,0:T(8,128)S(1)} %collective-permute-done.5), channel_id=1, source_target_pairs={{0,4},{4,0},{8,12},{12,8},{16,20},{20,16},{24,28},{28,24},{1,5},{5... | collective-permute-start | bytes 196616 | tf_op jit(solution)/shard_map/ppermute | solution.py:20
  39.9 5.0 %copy-start = (f32[256,128]{1,0:T(8,128)S(1)}, f32[256,128]{1,0:T(8,128)}, u32[]{:S(2)}) copy-start(f32[256,128]{1,0:T(8,128)} %param.6) | copy-start | bytes 393220
  39.9 5.0 %copy-start.3 = (f32[256]{0:T(256)S(1)}, f32[256]{0:T(256)}, u32[]{:S(2)}) copy-start(f32[256]{0:T(256)} %param.9) | copy-start | bytes 3076
  42.9 1.4 %collective-permute-start.9 = (f32[256,128]{1,0:T(8,128)S(1)}, f32[256,128]{1,0:T(8,128)S(1)}, u32[]{:S(2)}, u32[]{:S(2)}) collective-permute-start(f32[256,128]{1,0:T(8,128)S(1)} %collective-permute-done.8), channel_id=1, source_target_pairs={{0,4},{4,0},{8,12},{12,8},{16,20},{20,16},{24,28},{28,24},{1,5},{5... | collective-permute-start | bytes 393224 | tf_op jit(solution)/shard_map/ppermute | solution.py:20
  43.2 1.4 %collective-permute-start.11 = (f32[256,128]{1,0:T(8,128)S(1)}, f32[256,128]{1,0:T(8,128)S(1)}, u32[]{:S(2)}, u32[]{:S(2)}) collective-permute-start(f32[256,128]{1,0:T(8,128)S(1)} %collective-permute-done.10), channel_id=1, source_target_pairs={{0,4},{4,0},{8,12},{12,8},{16,20},{20,16},{24,28},{28,24},{1,5},{5... | collective-permute-start | bytes 393224 | tf_op jit(solution)/shard_map/ppermute | solution.py:20
  43.5 1.3 %collective-permute-start.13 = (f32[256,128]{1,0:T(8,128)S(1)}, f32[256,128]{1,0:T(8,128)S(1)}, u32[]{:S(2)}, u32[]{:S(2)}) collective-permute-start(f32[256,128]{1,0:T(8,128)S(1)} %collective-permute-done.12), channel_id=1, source_target_pairs={{0,4},{4,0},{8,12},{12,8},{16,20},{20,16},{24,28},{28,24},{1,5},{5... | collective-permute-start | bytes 393224 | tf_op jit(solution)/shard_map/ppermute | solution.py:20
  63.7 6.3 %collective-permute-start.15 = (f32[256,128]{1,0:T(8,128)S(1)}, f32[256,128]{1,0:T(8,128)S(1)}, u32[]{:S(2)}, u32[]{:S(2)}) collective-permute-start(f32[256,128]{1,0:T(8,128)S(1)} %get-tuple-element.17), channel_id=1, source_target_pairs={{0,8},{4,12},{8,0},{12,4},{16,24},{20,28},{24,16},{28,20},{1,9},{5... | collective-permute-start | bytes 393224 | tf_op jit(solution)/shard_map/ppermute | solution.py:19
  65.1 7.1 %collective-permute-start.17 = (f32[256,128]{1,0:T(8,128)S(1)}, f32[256,128]{1,0:T(8,128)S(1)}, u32[]{:S(2)}, u32[]{:S(2)}) collective-permute-start(f32[256,128]{1,0:T(8,128)S(1)} %get-tuple-element.17), channel_id=1, source_target_pairs={{0,16},{4,20},{8,24},{12,28},{16,0},{20,4},{24,8},{28,12},{1,17},{... | collective-permute-start | bytes 393224 | tf_op jit(solution)/shard_map/ppermute | solution.py:19
  65.8 6.4 %collective-permute-start.19 = (f32[256,128]{1,0:T(8,128)S(1)}, f32[256,128]{1,0:T(8,128)S(1)}, u32[]{:S(2)}, u32[]{:S(2)}) collective-permute-start(f32[256,128]{1,0:T(8,128)S(1)} %get-tuple-element.17), channel_id=1, source_target_pairs={{0,24},{4,28},{8,16},{12,20},{16,8},{20,12},{24,0},{28,4},{1,25},{... | collective-permute-start | bytes 393224 | tf_op jit(solution)/shard_map/ppermute | solution.py:19
  67.2 5.6 %collective-permute-start.14 = (f32[256,128]{1,0:T(8,128)S(1)}, f32[256,128]{1,0:T(8,128)S(1)}, u32[]{:S(2)}, u32[]{:S(2)}) collective-permute-start(f32[256,128]{1,0:T(8,128)S(1)} %get-tuple-element.17), channel_id=1, source_target_pairs={{0,4},{4,0},{8,12},{12,8},{16,20},{20,16},{24,28},{28,24},{1,5},{5... | collective-permute-start | bytes 393224 | tf_op jit(solution)/shard_map/ppermute | solution.py:20
  69.9 2.9 %collective-permute-start.16 = (f32[256,128]{1,0:T(8,128)S(1)}, f32[256,128]{1,0:T(8,128)S(1)}, u32[]{:S(2)}, u32[]{:S(2)}) collective-permute-start(f32[256,128]{1,0:T(8,128)S(1)} %collective-permute-done.15), channel_id=1, source_target_pairs={{0,4},{4,0},{8,12},{12,8},{16,20},{20,16},{24,28},{28,24},{1,5},{5... | collective-permute-start | bytes 393224 | tf_op jit(solution)/shard_map/ppermute | solution.py:20
  72.3 1.3 %collective-permute-start.18 = (f32[256,128]{1,0:T(8,128)S(1)}, f32[256,128]{1,0:T(8,128)S(1)}, u32[]{:S(2)}, u32[]{:S(2)}) collective-permute-start(f32[256,128]{1,0:T(8,128)S(1)} %collective-permute-done.17), channel_id=1, source_target_pairs={{0,4},{4,0},{8,12},{12,8},{16,20},{20,16},{24,28},{28,24},{1,5},{5... | collective-permute-start | bytes 393224 | tf_op jit(solution)/shard_map/ppermute | solution.py:20
  72.3 1.5 %collective-permute-start.20 = (f32[256,128]{1,0:T(8,128)S(1)}, f32[256,128]{1,0:T(8,128)S(1)}, u32[]{:S(2)}, u32[]{:S(2)}) collective-permute-start(f32[256,128]{1,0:T(8,128)S(1)} %collective-permute-done.19), channel_id=1, source_target_pairs={{0,4},{4,0},{8,12},{12,8},{16,20},{20,16},{24,28},{28,24},{1,5},{5... | collective-permute-start | bytes 393224 | tf_op jit(solution)/shard_map/ppermute | solution.py:20

commit v2 on v1

v2 whole, which is shorter than its diff:
```python
import functools

import jax
import jax.numpy as jnp
from jax import lax
from jax.experimental import pallas as pl
from jax.experimental.pallas import tpu as pltpu
from jax.sharding import PartitionSpec as P

HIGH = lax.Precision.HIGH
HIGHEST = lax.Precision.HIGHEST
VMEM = pl.BlockSpec(memory_space=pltpu.VMEM)
SMALL = pltpu.CompilerParams(vmem_limit_bytes=16 * 1024 * 1024)


def dot(left, right, precision=HIGH):
    return jnp.dot(left, right, precision=precision, preferred_element_type=jnp.float32)


def partners(count, offset):
    return [(index, index ^ offset) for index in range(count)]


def gather_cfg(block, count):
    own = [block] + [lax.ppermute(block, "cfg", partners(count, d)) for d in range(2, count, 2)]
    other = [lax.ppermute(piece, "cfg", partners(count, 1)) for piece in own]
    return [piece for pair in zip(own, other) for piece in pair]


def gather_tm(block, count):
    return [block] + [lax.ppermute(block, "tm", partners(count, d)) for d in range(1, count)]


def matern(left, right_t):
    cross = dot(left, right_t, HIGHEST)
    dist2 = (
        jnp.sum(left * left, axis=1)[:, None]
        + jnp.sum(right_t * right_t, axis=0)[None, :]
        - 2.0 * cross
    )
    scaled_dist = jnp.sqrt(3.0) * jnp.sqrt(jnp.maximum(dist2, 0.0))
    return (1.0 + scaled_dist) * jnp.exp(-scaled_dist)


def column(row):
    return jnp.transpose(jnp.broadcast_to(row, (8, row.shape[1])))[:, :1]


def total_of(left, right):
    product = left * right
    return jnp.sum(jnp.sum(product, axis=0, keepdims=True), axis=1, keepdims=True)


def moments_kernel(mixed_ref, mask_ref, noise_ref, image_ref, residual_ref, second_ref, parts_ref):
    image, residual = image_ref[...], residual_ref[...]
    second = column(mask_ref[...]) * mixed_ref[...] + column(noise_ref[...]) * image
    second_ref[...] = second
    place = lax.broadcasted_iota(jnp.int32, parts_ref.shape[1:], 0)
    parts = jnp.zeros(parts_ref.shape[1:], jnp.float32)
    for at, pair in enumerate([(residual, residual), (residual, image), (image, image), (image, second)]):
        parts = jnp.where(place == at, total_of(*pair), parts)
    parts_ref[...] = jnp.broadcast_to(parts[None], parts_ref.shape)


def finish_kernel(parts_ref, residual_ref, image_ref, second_ref, field_ref, left_ref):
    sums = jnp.sum(parts_ref[...], axis=0)
    norm0, first, square, third = (sums[at : at + 1] for at in range(4))
    alpha = norm0 / first
    norm1 = norm0 - 2.0 * alpha * first + alpha * alpha * square
    keep = 1.0 + norm1 / norm0
    curv = keep * keep * first - 2.0 * keep * alpha * square + alpha * alpha * third
    beta = norm1 / curv
    residual, image = residual_ref[...], image_ref[...]
    field_ref[...] = (alpha + beta * keep) * residual - (beta * alpha) * image
    left_ref[...] = residual - (alpha + beta * keep) * image + (beta * alpha) * second_ref[...]


def solution(mesh):
    cfg, tm = mesh.shape["cfg"], mesh.shape["tm"]
    everyone = cfg * tm

    def body(targets, features, inv_scales, noise, time_kernel, block_mask):
        rows, width = targets.shape
        layer = lax.axis_index("tm")
        mask = block_mask.astype(jnp.float32)
        ridge = noise[:, None]
        residual = mask * targets
        scaled = features * inv_scales[None, :]
        every_t = gather_cfg(scaled.T, cfg)
        steps = jnp.concatenate(
            [lax.dynamic_slice(time_kernel, (0, (layer ^ d) * width), (width, width)) for d in range(tm)], axis=1
        )

        def over_time(field):
            whole = jnp.concatenate(gather_tm(field, tm), axis=1)
            return lax.dot_general(
                whole, steps, (((1,), (1,)), ((), ())), precision=HIGH, preferred_element_type=jnp.float32
            )

        timed = over_time(residual)
        tile = matern(scaled, jnp.concatenate(every_t, axis=1))

        def over_cfg(field):
            return dot(tile, jnp.concatenate(gather_cfg(field, cfg), axis=0))

        image = mask * over_cfg(timed) + ridge * residual
        mixed = over_cfg(over_time(image))
        block = jax.ShapeDtypeStruct((rows, width), jnp.float32)
        second, parts = pl.pallas_call(
            moments_kernel,
            out_shape=(block, jax.ShapeDtypeStruct((everyone, 8, width), jnp.float32)),
            in_specs=[VMEM] * 5,
            out_specs=(VMEM, VMEM),
            compiler_params=SMALL,
            name="moments",
        )(mixed, mask.reshape(1, rows), noise.reshape(1, rows), image, residual)
        parts = lax.all_to_all(parts, ("cfg", "tm"), 0, 0, tiled=True)
        return pl.pallas_call(
            finish_kernel,
            out_shape=(block, block),
            in_specs=[VMEM] * 4,
            out_specs=(VMEM, VMEM),
            compiler_params=SMALL,
            name="finish",
        )(parts, residual, image, second)

    return jax.shard_map(
        body,
        mesh=mesh,
        in_specs=(P("cfg", "tm"), P("cfg", None), P(), P("cfg"), P("tm", None), P("cfg", "tm")),
        out_specs=(P("cfg", "tm"), P("cfg", "tm")),
        check_vma=False,
    )
```

time: 98.3 us -> 73.4 us (0.75)
  blocking collectives: 46.5 us -> 14.1 us
  starting transfers between devices: 11.8 us -> 23.8 us
  waiting for transfers between devices: 16.4 us -> 22.4 us
  between operations: 6.78 us -> 0.96 us
  matrix products: 10.1 us -> 5.73 us
  local copies, waits for them, and re-layouts: 3.52 us -> 1.17 us
  Pallas kernels: 0 us -> 1.2 us
    all_gather x2 -> x0, blocking collectives: 34.1 us -> none  [over_time(): rows = lax.all_gather(field, 'tm', axis=0)]
    ppermute x0 -> x6, starting transfers between devices: none -> 10.1 us  [gather_tm(): lax.ppermute(block, 'tm', partners(count, d))]
    ppermute x0 -> x6, waiting for transfers between devices: none -> 9.74 us  [gather_tm(): lax.ppermute(block, 'tm', partners(count, d))]
    dot_general x11 -> x3, matrix products: 10.1 us -> 4.98 us  [dot(): jnp.dot(left, right, precision=precision, preferred_element_type=jnp.floa...]
    another operation x2 -> x0, local copies, waits for them, and re-layouts: 2.63 us -> none  [the longest x1 2.63 us: body(): jnp.stack([jnp.sum(residual * residual), jnp.sum(residual * image), jnp.s...]
    ppermute x9, starting transfers between devices: 10.4 us -> 12.4 us  [gather_cfg(): lax.ppermute(block, 'cfg', partners(count, d))]
    ppermute x9, waiting for transfers between devices: 12.6 us -> 10.5 us  [gather_cfg(): lax.ppermute(block, 'cfg', partners(count, d))]
    all_to_all x1, blocking collectives: 12.4 us -> 14.1 us  [body(): parts = lax.all_to_all(parts, ('cfg', 'tm'), 0, 0, tiled=True)]
  transfers between devices with their start and end apart: 21 -> 27, of which waited for: 12 -> 11; matrix products, arithmetic and copies ran while one was open for 3% -> 9% of each run, Pallas kernels for 0% -> 0%
where the time goes in v2:
time: 73.4 us; the launch traced here: 73 us
  starting transfers between devices  23.8 us (32%)
  waiting for transfers between devices  22.4 us (31%)
  blocking collectives  14.1 us (19%)
  matrix products  5.73 us (8%)
  other arithmetic  3.61 us (5%)
  Pallas kernels  1.2 us (2%)
  local copies, waits for them, and re-layouts  1.17 us (2%)
  between operations  0.96 us (1%)
    all_to_all x1, blocking collectives, body(): parts = lax.all_to_all(parts, ('cfg', 'tm'), 0, 0, tiled=True)  14.1 us
    ppermute x9, starting transfers between devices, gather_cfg(): lax.ppermute(block, 'cfg', partners(count, d))  12.4 us
    ppermute x9, waiting for transfers between devices, gather_cfg(): lax.ppermute(block, 'cfg', partners(count, d))  10.5 us
    ppermute x6, starting transfers between devices, gather_tm(): lax.ppermute(block, 'tm', partners(count, d))  10.1 us
    ppermute x6, waiting for transfers between devices, gather_tm(): lax.ppermute(block, 'tm', partners(count, d))  9.74 us
    dot_general x3, matrix products, dot(): jnp.dot(left, right, precision=precision, preferred_element_type=jnp.floa...  4.98 us
    ppermute x12, waiting for transfers between devices, gather_cfg(): other = [lax.ppermute(piece, 'cfg', partners(count, 1)) for piece in own]  2.13 us
  transfers between devices with their start and end apart: 27, of which 11 were waited for; matrix products, arithmetic and copies ran while one was open for 9% of the time, Pallas kernels for 0%

profile of v2, /device:TPU:0, one launch (start us, length us, event | category | flops | bytes accessed | tf_op | source)
XLA Modules:
  0.0 73.0 jit_solution(13666452501195403141)
XLA Ops:
  0.6 0.0 copy-start.2
  0.6 0.0 copy-start.3
  0.7 0.7 convert_bitcast_fusion
  1.4 1.0 %broadcast_multiply_fusion.residual_ref = f32[256,128]{1,0:T(8,128)S(1)} fusion(f32[256,128]{1,0:T(8,128)} %param.6, f32[256]{0:T(256)S(1)} %bitcast.13), kind=kLoop, calls=%fused_computation.22 | loop fusion | flops 32768 | bytes 263168 | tf_op jit(solution)/shard_map/mul | solution.py:87
  2.4 3.1 %collective-permute-start.7 = (f32[256,128]{1,0:T(8,128)S(1)}, f32[256,128]{1,0:T(8,128)S(1)}, u32[]{:S(2)}, u32[]{:S(2)}) collective-permute-start(f32[256,128]{1,0:T(8,128)S(1)} %broadcast_multiply_fusion.residual_ref), channel_id=1, source_target_pairs={{0,1},{1,0},{2,3},{3,2},{4,5},{5,4},{6,7},{7,6},{8,9},{9,8},{10,11... | collective-permute-start | bytes 393224 | tf_op jit(solution)/shard_map/ppermute | solution.py:31
  5.5 2.6 %collective-permute-start.8 = (f32[256,128]{1,0:T(8,128)S(1)}, f32[256,128]{1,0:T(8,128)S(1)}, u32[]{:S(2)}, u32[]{:S(2)}) collective-permute-start(f32[256,128]{1,0:T(8,128)S(1)} %broadcast_multiply_fusion.residual_ref), channel_id=1, source_target_pairs={{0,2},{1,3},{2,0},{3,1},{4,6},{5,7},{6,4},{7,5},{8,10},{9,11},{10,... | collective-permute-start | bytes 393224 | tf_op jit(solution)/shard_map/ppermute | solution.py:31
  8.1 0.9 %constant_dynamic-update-slice_fusion.7 = (f32[64,2048]{1,0:T(8,128)S(1)}, f32[64,256]{1,0:T(8,128)S(1)}) fusion(f32[256,64]{0,1:T(8,128)} %param.7, f32[64]{0:T(128)} %param.8), kind=kLoop, calls=%fused_computation.33 | loop fusion | flops 16383 | bytes 196864
  9.0 0.1 collective-permute-start
  9.1 1.8 %collective-permute-start.1 = (f32[64,256]{1,0:T(8,128)S(1)}, f32[64,256]{1,0:T(8,128)S(1)}, u32[]{:S(2)}, u32[]{:S(2)}) collective-permute-start(f32[64,256]{1,0:T(8,128)S(1)} %get-tuple-element.7), channel_id=1, source_target_pairs={{0,8},{4,12},{8,0},{12,4},{16,24},{20,28},{24,16},{28,20},{1,9},{5... | collective-permute-start | bytes 196616 | tf_op jit(solution)/shard_map/ppermute | solution.py:25
  10.8 1.0 %constant_dynamic-slice_fusion.3 = (f32[128,128]{1,0:T(8,128)S(1)}, f32[128,128]{1,0:T(8,128)S(1)}, f32[128,128]{1,0:T(8,128)S(1)}, f32[128,128]{1,0:T(8,128)S(1)}) fusion(f32[128,512]{1,0:T(8,128)} %param.10, s32[]{:T(128)S(6)} %select_n.12, s32[]{:T(128)S(6)} %select_n.13, s32[]{:T(128)S(6)} %select_n.15, s32[]{:T(128)S(6)} %select_n.14), kind=kLoop, calls=%fused_computation.54 | loop fusion | bytes 524304 | tf_op jit(solution)/shard_map/dynamic_slice | solution.py:91
  11.8 0.9 %multiply_reduce_fusion.1 = f32[256]{0:T(256)S(1)} fusion(f32[256,64]{0,1:T(8,128)} %param.7, f32[64]{0:T(128)} %param.8), kind=kLoop, calls=%fused_computation.23 | loop fusion | flops 48896 | bytes 66816 | tf_op jit(solution)/shard_map/reduce_sum | solution.py:37
  12.7 1.6 %collective-permute-start.3 = (f32[64,256]{1,0:T(8,128)S(1)}, f32[64,256]{1,0:T(8,128)S(1)}, u32[]{:S(2)}, u32[]{:S(2)}) collective-permute-start(f32[64,256]{1,0:T(8,128)S(1)} %get-tuple-element.7), channel_id=1, source_target_pairs={{0,16},{4,20},{8,24},{12,28},{16,0},{20,4},{24,8},{28,12},{1,17},{... | collective-permute-start | bytes 196616 | tf_op jit(solution)/shard_map/ppermute | solution.py:25
  14.3 1.9 %collective-permute-start.5 = (f32[64,256]{1,0:T(8,128)S(1)}, f32[64,256]{1,0:T(8,128)S(1)}, u32[]{:S(2)}, u32[]{:S(2)}) collective-permute-start(f32[64,256]{1,0:T(8,128)S(1)} %get-tuple-element.7), channel_id=1, source_target_pairs={{0,24},{4,28},{8,16},{12,20},{16,8},{20,12},{24,0},{28,4},{1,25},{... | collective-permute-start | bytes 196616 | tf_op jit(solution)/shard_map/ppermute | solution.py:25
  16.2 0.8 %collective-permute-done.3 = f32[64,256]{1,0:T(8,128)S(1)} collective-permute-done((f32[64,256]{1,0:T(8,128)S(1)}, f32[64,256]{1,0:T(8,128)S(1)}, u32[]{:S(2)}, u32[]{:S(2)}) %collective-permute-start.3) | collective-permute-done | bytes 65568 | tf_op jit(solution)/shard_map/ppermute | solution.py:25
  17.1 2.5 %collective-permute-done.5 = f32[64,256]{1,0:T(8,128)S(1)} collective-permute-done((f32[64,256]{1,0:T(8,128)S(1)}, f32[64,256]{1,0:T(8,128)S(1)}, u32[]{:S(2)}, u32[]{:S(2)}) %collective-permute-start.5) | collective-permute-done | bytes 65568 | tf_op jit(solution)/shard_map/ppermute | solution.py:25
  19.6 0.5 collective-permute-start.6
  20.1 0.4 constant_dynamic-update-slice_fusion.15
  20.5 0.1 collective-permute-start.10
  20.5 0.9 %collective-permute-start.11 = (f32[256,128]{1,0:T(8,128)S(1)}, f32[256,128]{1,0:T(8,128)S(1)}, u32[]{:S(2)}, u32[]{:S(2)}) collective-permute-start(f32[256,128]{1,0:T(8,128)S(1)} %get-tuple-element.15), channel_id=1, source_target_pairs={{0,8},{4,12},{8,0},{12,4},{16,24},{20,28},{24,16},{28,20},{1,9},{5... | collective-permute-start | bytes 393224 | tf_op jit(solution)/shard_map/ppermute | solution.py:25
  21.5 1.5 %collective-permute-start.13 = (f32[256,128]{1,0:T(8,128)S(1)}, f32[256,128]{1,0:T(8,128)S(1)}, u32[]{:S(2)}, u32[]{:S(2)}) collective-permute-start(f32[256,128]{1,0:T(8,128)S(1)} %get-tuple-element.15), channel_id=1, source_target_pairs={{0,16},{4,20},{8,24},{12,28},{16,0},{20,4},{24,8},{28,12},{1,17},{... | collective-permute-start | bytes 393224 | tf_op jit(solution)/shard_map/ppermute | solution.py:25
  23.0 1.2 %collective-permute-start.15 = (f32[256,128]{1,0:T(8,128)S(1)}, f32[256,128]{1,0:T(8,128)S(1)}, u32[]{:S(2)}, u32[]{:S(2)}) collective-permute-start(f32[256,128]{1,0:T(8,128)S(1)} %get-tuple-element.15), channel_id=1, source_target_pairs={{0,24},{4,28},{8,16},{12,20},{16,8},{20,12},{24,0},{28,4},{1,25},{... | collective-permute-start | bytes 393224 | tf_op jit(solution)/shard_map/ppermute | solution.py:25
  24.2 0.1 multiply_reduce_fusion
  24.3 0.0 copy-start
  24.3 0.0 copy-start.1
  24.3 3.0 %exponential_multiply_fusion = f32[256,2048]{1,0:T(8,128)S(1)} fusion(f32[64,2048]{1,0:T(8,128)S(1)} %constant_dynamic-update-slice_fusion, f32[2048]{0:T(1024)S(1)} %multiply_reduce_fusion, f32[256]{0:T(256)S(1)} %multiply_reduce_fusion.1, f32[256,64]{0,1:T(8,128)S(1)} %copy-done.2, f32[64]{0:T(128)S(1)} %copy-done.3), kind=kOutput, calls=%fused_computation.1 | convolution fusion | flops 406863872 | bytes 2696448 | tf_op jit(solution)/shard_map/dot_general | solution.py:17
  27.3 0.1 collective-permute-start.12
  27.4 2.5 %collective-permute-done.13 = f32[256,128]{1,0:T(8,128)S(1)} collective-permute-done((f32[256,128]{1,0:T(8,128)S(1)}, f32[256,128]{1,0:T(8,128)S(1)}, u32[]{:S(2)}, u32[]{:S(2)}) %collective-permute-start.13) | collective-permute-done | bytes 131104 | tf_op jit(solution)/shard_map/ppermute | solution.py:25
  29.9 0.5 collective-permute-start.16
  30.5 0.7 %collective-permute-done.14 = f32[256,128]{1,0:T(8,128)S(1)} collective-permute-done((f32[256,128]{1,0:T(8,128)S(1)}, f32[256,128]{1,0:T(8,128)S(1)}, u32[]{:S(2)}, u32[]{:S(2)}) %collective-permute-start.14) | collective-permute-done | bytes 131104 | tf_op jit(solution)/shard_map/ppermute | solution.py:26
  31.2 0.2 collective-permute-done.16
  31.4 1.0 %fusion.image_ref = f32[256,128]{1,0:T(8,128)S(1)} fusion(f32[256,2048]{1,0:T(8,128)S(1)} %exponential_multiply_fusion, f32[2048,128]{1,0:T(8,128)S(1)} %constant_dynamic-update-slice_fusion.8, f32[256]{0:T(256)S(1)} %copy-done, f32[256]{0:T(256)S(1)} %bitcast.14, f32[256,128]{1,0:T(8,128)S(1)} %copy-done.1), kind=kOutput, calls=%fused_computation.3 | convolution fusion | flops 402784256 | bytes 3409920 | tf_op jit(solution)/shard_map/dot_general | solution.py:17
  32.4 0.9 %collective-permute-start.17 = (f32[256,128]{1,0:T(8,128)S(1)}, f32[256,128]{1,0:T(8,128)S(1)}, u32[]{:S(2)}, u32[]{:S(2)}) collective-permute-start(f32[256,128]{1,0:T(8,128)S(1)} %fusion.image_ref), channel_id=1, source_target_pairs={{0,1},{1,0},{2,3},{3,2},{4,5},{5,4},{6,7},{7,6},{8,9},{9,8},{10,11... | collective-permute-start | bytes 393224 | tf_op jit(solution)/shard_map/ppermute | solution.py:31
  33.4 3.3 %collective-permute-start.18 = (f32[256,128]{1,0:T(8,128)S(1)}, f32[256,128]{1,0:T(8,128)S(1)}, u32[]{:S(2)}, u32[]{:S(2)}) collective-permute-start(f32[256,128]{1,0:T(8,128)S(1)} %fusion.image_ref), channel_id=1, source_target_pairs={{0,2},{1,3},{2,0},{3,1},{4,6},{5,7},{6,4},{7,5},{8,10},{9,11},{10,... | collective-permute-start | bytes 393224 | tf_op jit(solution)/shard_map/ppermute | solution.py:31
  36.7 0.2 collective-permute-start.19
  36.9 3.7 %collective-permute-done.17 = f32[256,128]{1,0:T(8,128)S(1)} collective-permute-done((f32[256,128]{1,0:T(8,128)S(1)}, f32[256,128]{1,0:T(8,128)S(1)}, u32[]{:S(2)}, u32[]{:S(2)}) %collective-permute-start.17) | collective-permute-done | bytes 131104 | tf_op jit(solution)/shard_map/ppermute | solution.py:31
  40.6 6.0 %collective-permute-done.18 = f32[256,128]{1,0:T(8,128)S(1)} collective-permute-done((f32[256,128]{1,0:T(8,128)S(1)}, f32[256,128]{1,0:T(8,128)S(1)}, u32[]{:S(2)}, u32[]{:S(2)}) %collective-permute-start.18) | collective-permute-done | bytes 131104 | tf_op jit(solution)/shard_map/ppermute | solution.py:31
  46.6 0.4 constant_dynamic-update-slice_fusion.23
  47.0 1.1 %collective-permute-start.21 = (f32[256,128]{1,0:T(8,128)S(1)}, f32[256,128]{1,0:T(8,128)S(1)}, u32[]{:S(2)}, u32[]{:S(2)}) collective-permute-start(f32[256,128]{1,0:T(8,128)S(1)} %get-tuple-element.17), channel_id=1, source_target_pairs={{0,8},{4,12},{8,0},{12,4},{16,24},{20,28},{24,16},{28,20},{1,9},{5... | collective-permute-start | bytes 393224 | tf_op jit(solution)/shard_map/ppermute | solution.py:25
  48.1 1.0 %collective-permute-start.23 = (f32[256,128]{1,0:T(8,128)S(1)}, f32[256,128]{1,0:T(8,128)S(1)}, u32[]{:S(2)}, u32[]{:S(2)}) collective-permute-start(f32[256,128]{1,0:T(8,128)S(1)} %get-tuple-element.17), channel_id=1, source_target_pairs={{0,16},{4,20},{8,24},{12,28},{16,0},{20,4},{24,8},{28,12},{1,17},{... | collective-permute-start | bytes 393224 | tf_op jit(solution)/shard_map/ppermute | solution.py:25
  49.1 1.4 %collective-permute-start.25 = (f32[256,128]{1,0:T(8,128)S(1)}, f32[256,128]{1,0:T(8,128)S(1)}, u32[]{:S(2)}, u32[]{:S(2)}) collective-permute-start(f32[256,128]{1,0:T(8,128)S(1)} %get-tuple-element.17), channel_id=1, source_target_pairs={{0,24},{4,28},{8,16},{12,20},{16,8},{20,12},{24,0},{28,4},{1,25},{... | collective-permute-start | bytes 393224 | tf_op jit(solution)/shard_map/ppermute | solution.py:25
  50.6 2.4 %collective-permute-done.21 = f32[256,128]{1,0:T(8,128)S(1)} collective-permute-done((f32[256,128]{1,0:T(8,128)S(1)}, f32[256,128]{1,0:T(8,128)S(1)}, u32[]{:S(2)}, u32[]{:S(2)}) %collective-permute-start.21) | collective-permute-done | bytes 131104 | tf_op jit(solution)/shard_map/ppermute | solution.py:25
  53.0 0.9 %collective-permute-done.23 = f32[256,128]{1,0:T(8,128)S(1)} collective-permute-done((f32[256,128]{1,0:T(8,128)S(1)}, f32[256,128]{1,0:T(8,128)S(1)}, u32[]{:S(2)}, u32[]{:S(2)}) %collective-permute-start.23) | collective-permute-done | bytes 131104 | tf_op jit(solution)/shard_map/ppermute | solution.py:25
  53.9 1.4 %collective-permute-done.25 = f32[256,128]{1,0:T(8,128)S(1)} collective-permute-done((f32[256,128]{1,0:T(8,128)S(1)}, f32[256,128]{1,0:T(8,128)S(1)}, u32[]{:S(2)}, u32[]{:S(2)}) %collective-permute-start.25) | collective-permute-done | bytes 131104 | tf_op jit(solution)/shard_map/ppermute | solution.py:25
  55.5 1.2 %collective-permute-done.26 = f32[256,128]{1,0:T(8,128)S(1)} collective-permute-done((f32[256,128]{1,0:T(8,128)S(1)}, f32[256,128]{1,0:T(8,128)S(1)}, u32[]{:S(2)}, u32[]{:S(2)}) %collective-permute-start.26) | collective-permute-done | bytes 131104 | tf_op jit(solution)/shard_map/ppermute | solution.py:26
  56.7 1.0 %fusion.21.mixed_ref = f32[256,128]{1,0:T(8,128)S(1)} fusion(f32[256,2048]{1,0:T(8,128)S(1)} %exponential_multiply_fusion, f32[2048,128]{1,0:T(8,128)S(1)} %constant_dynamic-update-slice_fusion.16), kind=kOutput, calls=%fused_computation.58 | convolution fusion | flops 402653184 | bytes 3276800 | tf_op jit(solution)/shard_map/dot_general | solution.py:17
  57.7 0.4 moments.1
  58.1 14.1 %all_to_all.5.parts_ref = f32[32,8,128]{2,1,0:T(8,128)S(1)} all-to-all(f32[32,8,128]{2,1,0:T(8,128)S(1)} %get-tuple-element.4), channel_id=1, replica_groups=mesh['cfg'=8,'tm'=4] {'cfg','tm'}, dimensions={0} | all-to-all | bytes 262144 | tf_op jit(solution)/shard_map/all_to_all | solution.py:117
  72.3 0.8 %finish.1 = (f32[256,128]{1,0:T(8,128)}, f32[256,128]{1,0:T(8,128)}) custom-call(f32[32,8,128]{2,1,0:T(8,128)S(1)} %all_to_all.5.parts_ref, f32[256,128]{1,0:T(8,128)S(1)} %broadcast_multiply_fusion.residual_ref, f32[256,128]{1,0:T(8,128)S(1)} %fusion.image_ref, f32[256,128]{1,0:T(8,128)S(1)} %get-tuple-element.5.second_ref), custom_call_target="tpu_custom_call" | custom-call | tf_op jit(solution)/shard_map/finish/pallas_call | solution.py:118
  (49 shorter events, 0.3 us)
Async XLA Ops:
  0.6 23.7 %copy-start.2 = (f32[256,64]{0,1:T(8,128)S(1)}, f32[256,64]{0,1:T(8,128)}, u32[]{:S(2)}) copy-start(f32[256,64]{0,1:T(8,128)} %param.7) | copy-start | bytes 196612
  0.6 23.7 %copy-start.3 = (f32[64]{0:T(128)S(1)}, f32[64]{0:T(128)}, u32[]{:S(2)}) copy-start(f32[64]{0:T(128)} %param.8) | copy-start | bytes 772
  2.4 17.2 %collective-permute-start.7 = (f32[256,128]{1,0:T(8,128)S(1)}, f32[256,128]{1,0:T(8,128)S(1)}, u32[]{:S(2)}, u32[]{:S(2)}) collective-permute-start(f32[256,128]{1,0:T(8,128)S(1)} %broadcast_multiply_fusion.residual_ref), channel_id=1, source_target_pairs={{0,1},{1,0},{2,3},{3,2},{4,5},{5,4},{6,7},{7,6},{8,9},{9,8},{10,11... | collective-permute-start | bytes 393224 | tf_op jit(solution)/shard_map/ppermute | solution.py:31
  5.5 14.6 %collective-permute-start.8 = (f32[256,128]{1,0:T(8,128)S(1)}, f32[256,128]{1,0:T(8,128)S(1)}, u32[]{:S(2)}, u32[]{:S(2)}) collective-permute-start(f32[256,128]{1,0:T(8,128)S(1)} %broadcast_multiply_fusion.residual_ref), channel_id=1, source_target_pairs={{0,2},{1,3},{2,0},{3,1},{4,6},{5,7},{6,4},{7,5},{8,10},{9,11},{10,... | collective-permute-start | bytes 393224 | tf_op jit(solution)/shard_map/ppermute | solution.py:31
  8.0 12.0 %collective-permute-start.9 = (f32[256,128]{1,0:T(8,128)S(1)}, f32[256,128]{1,0:T(8,128)S(1)}, u32[]{:S(2)}, u32[]{:S(2)}) collective-permute-start(f32[256,128]{1,0:T(8,128)S(1)} %broadcast_multiply_fusion.residual_ref), channel_id=1, source_target_pairs={{0,3},{1,2},{2,1},{3,0},{4,7},{5,6},{6,5},{7,4},{8,11},{9,10},{10,... | collective-permute-start | bytes 393224 | tf_op jit(solution)/shard_map/ppermute | solution.py:31
  9.0 3.7 %collective-permute-start = (f32[64,256]{1,0:T(8,128)S(1)}, f32[64,256]{1,0:T(8,128)S(1)}, u32[]{:S(2)}, u32[]{:S(2)}) collective-permute-start(f32[64,256]{1,0:T(8,128)S(1)} %get-tuple-element.7), channel_id=1, source_target_pairs={{0,4},{4,0},{8,12},{12,8},{16,20},{20,16},{24,28},{28,24},{1,5},{5... | collective-permute-start | bytes 196616 | tf_op jit(solution)/shard_map/ppermute | solution.py:26
  9.1 5.3 %collective-permute-start.1 = (f32[64,256]{1,0:T(8,128)S(1)}, f32[64,256]{1,0:T(8,128)S(1)}, u32[]{:S(2)}, u32[]{:S(2)}) collective-permute-start(f32[64,256]{1,0:T(8,128)S(1)} %get-tuple-element.7), channel_id=1, source_target_pairs={{0,8},{4,12},{8,0},{12,4},{16,24},{20,28},{24,16},{28,20},{1,9},{5... | collective-permute-start | bytes 196616 | tf_op jit(solution)/shard_map/ppermute | solution.py:25
  12.7 4.3 %collective-permute-start.3 = (f32[64,256]{1,0:T(8,128)S(1)}, f32[64,256]{1,0:T(8,128)S(1)}, u32[]{:S(2)}, u32[]{:S(2)}) collective-permute-start(f32[64,256]{1,0:T(8,128)S(1)} %get-tuple-element.7), channel_id=1, source_target_pairs={{0,16},{4,20},{8,24},{12,28},{16,0},{20,4},{24,8},{28,12},{1,17},{... | collective-permute-start | bytes 196616 | tf_op jit(solution)/shard_map/ppermute | solution.py:25
  14.3 5.2 %collective-permute-start.5 = (f32[64,256]{1,0:T(8,128)S(1)}, f32[64,256]{1,0:T(8,128)S(1)}, u32[]{:S(2)}, u32[]{:S(2)}) collective-permute-start(f32[64,256]{1,0:T(8,128)S(1)} %get-tuple-element.7), channel_id=1, source_target_pairs={{0,24},{4,28},{8,16},{12,20},{16,8},{20,12},{24,0},{28,4},{1,25},{... | collective-permute-start | bytes 196616 | tf_op jit(solution)/shard_map/ppermute | solution.py:25
  17.1 4.4 %collective-permute-start.2 = (f32[64,256]{1,0:T(8,128)S(1)}, f32[64,256]{1,0:T(8,128)S(1)}, u32[]{:S(2)}, u32[]{:S(2)}) collective-permute-start(f32[64,256]{1,0:T(8,128)S(1)} %collective-permute-done.1), channel_id=1, source_target_pairs={{0,4},{4,0},{8,12},{12,8},{16,20},{20,16},{24,28},{28,24},{1,5},{5... | collective-permute-start | bytes 196616 | tf_op jit(solution)/shard_map/ppermute | solution.py:26
  19.6 3.5 %collective-permute-start.4 = (f32[64,256]{1,0:T(8,128)S(1)}, f32[64,256]{1,0:T(8,128)S(1)}, u32[]{:S(2)}, u32[]{:S(2)}) collective-permute-start(f32[64,256]{1,0:T(8,128)S(1)} %collective-permute-done.3), channel_id=1, source_target_pairs={{0,4},{4,0},{8,12},{12,8},{16,20},{20,16},{24,28},{28,24},{1,5},{5... | collective-permute-start | bytes 196616 | tf_op jit(solution)/shard_map/ppermute | solution.py:26
  19.6 4.6 %collective-permute-start.6 = (f32[64,256]{1,0:T(8,128)S(1)}, f32[64,256]{1,0:T(8,128)S(1)}, u32[]{:S(2)}, u32[]{:S(2)}) collective-permute-start(f32[64,256]{1,0:T(8,128)S(1)} %collective-permute-done.5), channel_id=1, source_target_pairs={{0,4},{4,0},{8,12},{12,8},{16,20},{20,16},{24,28},{28,24},{1,5},{5... | collective-permute-start | bytes 196616 | tf_op jit(solution)/shard_map/ppermute | solution.py:26
  20.5 9.9 %collective-permute-start.10 = (f32[256,128]{1,0:T(8,128)S(1)}, f32[256,128]{1,0:T(8,128)S(1)}, u32[]{:S(2)}, u32[]{:S(2)}) collective-permute-start(f32[256,128]{1,0:T(8,128)S(1)} %get-tuple-element.15), channel_id=1, source_target_pairs={{0,4},{4,0},{8,12},{12,8},{16,20},{20,16},{24,28},{28,24},{1,5},{5... | collective-permute-start | bytes 393224 | tf_op jit(solution)/shard_map/ppermute | solution.py:26
  20.5 6.8 %collective-permute-start.11 = (f32[256,128]{1,0:T(8,128)S(1)}, f32[256,128]{1,0:T(8,128)S(1)}, u32[]{:S(2)}, u32[]{:S(2)}) collective-permute-start(f32[256,128]{1,0:T(8,128)S(1)} %get-tuple-element.15), channel_id=1, source_target_pairs={{0,8},{4,12},{8,0},{12,4},{16,24},{20,28},{24,16},{28,20},{1,9},{5... | collective-permute-start | bytes 393224 | tf_op jit(solution)/shard_map/ppermute | solution.py:25
  21.5 8.4 %collective-permute-start.13 = (f32[256,128]{1,0:T(8,128)S(1)}, f32[256,128]{1,0:T(8,128)S(1)}, u32[]{:S(2)}, u32[]{:S(2)}) collective-permute-start(f32[256,128]{1,0:T(8,128)S(1)} %get-tuple-element.15), channel_id=1, source_target_pairs={{0,16},{4,20},{8,24},{12,28},{16,0},{20,4},{24,8},{28,12},{1,17},{... | collective-permute-start | bytes 393224 | tf_op jit(solution)/shard_map/ppermute | solution.py:25
  23.0 6.8 %collective-permute-start.15 = (f32[256,128]{1,0:T(8,128)S(1)}, f32[256,128]{1,0:T(8,128)S(1)}, u32[]{:S(2)}, u32[]{:S(2)}) collective-permute-start(f32[256,128]{1,0:T(8,128)S(1)} %get-tuple-element.15), channel_id=1, source_target_pairs={{0,24},{4,28},{8,16},{12,20},{16,8},{20,12},{24,0},{28,4},{1,25},{... | collective-permute-start | bytes 393224 | tf_op jit(solution)/shard_map/ppermute | solution.py:25
  24.3 7.1 %copy-start = (f32[256]{0:T(256)S(1)}, f32[256]{0:T(256)}, u32[]{:S(2)}) copy-start(f32[256]{0:T(256)} %param.9) | copy-start | bytes 3076
  24.3 7.1 %copy-start.1 = (f32[256,128]{1,0:T(8,128)S(1)}, f32[256,128]{1,0:T(8,128)}, u32[]{:S(2)}) copy-start(f32[256,128]{1,0:T(8,128)} %param.6) | copy-start | bytes 393220
  27.3 3.1 %collective-permute-start.12 = (f32[256,128]{1,0:T(8,128)S(1)}, f32[256,128]{1,0:T(8,128)S(1)}, u32[]{:S(2)}, u32[]{:S(2)}) collective-permute-start(f32[256,128]{1,0:T(8,128)S(1)} %collective-permute-done.11), channel_id=1, source_target_pairs={{0,4},{4,0},{8,12},{12,8},{16,20},{20,16},{24,28},{28,24},{1,5},{5... | collective-permute-start | bytes 393224 | tf_op jit(solution)/shard_map/ppermute | solution.py:26
  29.9 1.3 %collective-permute-start.14 = (f32[256,128]{1,0:T(8,128)S(1)}, f32[256,128]{1,0:T(8,128)S(1)}, u32[]{:S(2)}, u32[]{:S(2)}) collective-permute-start(f32[256,128]{1,0:T(8,128)S(1)} %collective-permute-done.13), channel_id=1, source_target_pairs={{0,4},{4,0},{8,12},{12,8},{16,20},{20,16},{24,28},{28,24},{1,5},{5... | collective-permute-start | bytes 393224 | tf_op jit(solution)/shard_map/ppermute | solution.py:26
  29.9 1.5 %collective-permute-start.16 = (f32[256,128]{1,0:T(8,128)S(1)}, f32[256,128]{1,0:T(8,128)S(1)}, u32[]{:S(2)}, u32[]{:S(2)}) collective-permute-start(f32[256,128]{1,0:T(8,128)S(1)} %collective-permute-done.15), channel_id=1, source_target_pairs={{0,4},{4,0},{8,12},{12,8},{16,20},{20,16},{24,28},{28,24},{1,5},{5... | collective-permute-start | bytes 393224 | tf_op jit(solution)/shard_map/ppermute | solution.py:26
  32.4 8.2 %collective-permute-start.17 = (f32[256,128]{1,0:T(8,128)S(1)}, f32[256,128]{1,0:T(8,128)S(1)}, u32[]{:S(2)}, u32[]{:S(2)}) collective-permute-start(f32[256,128]{1,0:T(8,128)S(1)} %fusion.image_ref), channel_id=1, source_target_pairs={{0,1},{1,0},{2,3},{3,2},{4,5},{5,4},{6,7},{7,6},{8,9},{9,8},{10,11... | collective-permute-start | bytes 393224 | tf_op jit(solution)/shard_map/ppermute | solution.py:31
  33.4 13.2 %collective-permute-start.18 = (f32[256,128]{1,0:T(8,128)S(1)}, f32[256,128]{1,0:T(8,128)S(1)}, u32[]{:S(2)}, u32[]{:S(2)}) collective-permute-start(f32[256,128]{1,0:T(8,128)S(1)} %fusion.image_ref), channel_id=1, source_target_pairs={{0,2},{1,3},{2,0},{3,1},{4,6},{5,7},{6,4},{7,5},{8,10},{9,11},{10,... | collective-permute-start | bytes 393224 | tf_op jit(solution)/shard_map/ppermute | solution.py:31
  36.7 10.0 %collective-permute-start.19 = (f32[256,128]{1,0:T(8,128)S(1)}, f32[256,128]{1,0:T(8,128)S(1)}, u32[]{:S(2)}, u32[]{:S(2)}) collective-permute-start(f32[256,128]{1,0:T(8,128)S(1)} %fusion.image_ref), channel_id=1, source_target_pairs={{0,3},{1,2},{2,1},{3,0},{4,7},{5,6},{6,5},{7,4},{8,11},{9,10},{10,... | collective-permute-start | bytes 393224 | tf_op jit(solution)/shard_map/ppermute | solution.py:31
  47.0 6.0 %collective-permute-start.21 = (f32[256,128]{1,0:T(8,128)S(1)}, f32[256,128]{1,0:T(8,128)S(1)}, u32[]{:S(2)}, u32[]{:S(2)}) collective-permute-start(f32[256,128]{1,0:T(8,128)S(1)} %get-tuple-element.17), channel_id=1, source_target_pairs={{0,8},{4,12},{8,0},{12,4},{16,24},{20,28},{24,16},{28,20},{1,9},{5... | collective-permute-start | bytes 393224 | tf_op jit(solution)/shard_map/ppermute | solution.py:25
  48.1 5.8 %collective-permute-start.23 = (f32[256,128]{1,0:T(8,128)S(1)}, f32[256,128]{1,0:T(8,128)S(1)}, u32[]{:S(2)}, u32[]{:S(2)}) collective-permute-start(f32[256,128]{1,0:T(8,128)S(1)} %get-tuple-element.17), channel_id=1, source_target_pairs={{0,16},{4,20},{8,24},{12,28},{16,0},{20,4},{24,8},{28,12},{1,17},{... | collective-permute-start | bytes 393224 | tf_op jit(solution)/shard_map/ppermute | solution.py:25
  49.1 6.2 %collective-permute-start.25 = (f32[256,128]{1,0:T(8,128)S(1)}, f32[256,128]{1,0:T(8,128)S(1)}, u32[]{:S(2)}, u32[]{:S(2)}) collective-permute-start(f32[256,128]{1,0:T(8,128)S(1)} %get-tuple-element.17), channel_id=1, source_target_pairs={{0,24},{4,28},{8,16},{12,20},{16,8},{20,12},{24,0},{28,4},{1,25},{... | collective-permute-start | bytes 393224 | tf_op jit(solution)/shard_map/ppermute | solution.py:25
  50.6 4.8 %collective-permute-start.20 = (f32[256,128]{1,0:T(8,128)S(1)}, f32[256,128]{1,0:T(8,128)S(1)}, u32[]{:S(2)}, u32[]{:S(2)}) collective-permute-start(f32[256,128]{1,0:T(8,128)S(1)} %get-tuple-element.17), channel_id=1, source_target_pairs={{0,4},{4,0},{8,12},{12,8},{16,20},{20,16},{24,28},{28,24},{1,5},{5... | collective-permute-start | bytes 393224 | tf_op jit(solution)/shard_map/ppermute | solution.py:26
  53.0 2.4 %collective-permute-start.22 = (f32[256,128]{1,0:T(8,128)S(1)}, f32[256,128]{1,0:T(8,128)S(1)}, u32[]{:S(2)}, u32[]{:S(2)}) collective-permute-start(f32[256,128]{1,0:T(8,128)S(1)} %collective-permute-done.21), channel_id=1, source_target_pairs={{0,4},{4,0},{8,12},{12,8},{16,20},{20,16},{24,28},{28,24},{1,5},{5... | collective-permute-start | bytes 393224 | tf_op jit(solution)/shard_map/ppermute | solution.py:26
  53.9 1.5 %collective-permute-start.24 = (f32[256,128]{1,0:T(8,128)S(1)}, f32[256,128]{1,0:T(8,128)S(1)}, u32[]{:S(2)}, u32[]{:S(2)}) collective-permute-start(f32[256,128]{1,0:T(8,128)S(1)} %collective-permute-done.23), channel_id=1, source_target_pairs={{0,4},{4,0},{8,12},{12,8},{16,20},{20,16},{24,28},{28,24},{1,5},{5... | collective-permute-start | bytes 393224 | tf_op jit(solution)/shard_map/ppermute | solution.py:26
  55.3 1.3 %collective-permute-start.26 = (f32[256,128]{1,0:T(8,128)S(1)}, f32[256,128]{1,0:T(8,128)S(1)}, u32[]{:S(2)}, u32[]{:S(2)}) collective-permute-start(f32[256,128]{1,0:T(8,128)S(1)} %collective-permute-done.25), channel_id=1, source_target_pairs={{0,4},{4,0},{8,12},{12,8},{16,20},{20,16},{24,28},{28,24},{1,5},{5... | collective-permute-start | bytes 393224 | tf_op jit(solution)/shard_map/ppermute | solution.py:26

commit v3 on v2

v3 whole, which is shorter than its diff:
```python
import math

import jax
import jax.numpy as jnp
from jax import lax
from jax.experimental import pallas as pl
from jax.experimental.pallas import tpu as pltpu
from jax.sharding import PartitionSpec as P

HBM = pl.BlockSpec(memory_space=pltpu.HBM)
VMEM = pl.BlockSpec(memory_space=pltpu.VMEM)
SMEM = pl.BlockSpec(memory_space=pltpu.SMEM)
F32, BF16 = jnp.float32, jnp.bfloat16
LIMIT = 62
LOG2E, LN2 = math.log2(math.e), math.log(2.0)


def partners(axis, offset):
    return [(index, index ^ offset) for index in range(lax.axis_size(axis))]


def gather_cfg(block, count, meanwhile=None):
    own = [block] + [lax.ppermute(block, "cfg", partners("cfg", d)) for d in range(2, count, 2)]
    if meanwhile is not None:
        extra = meanwhile(block)
        *extra, own[-1] = lax.optimization_barrier((*extra, own[-1]))
    other = [lax.ppermute(piece, "cfg", partners("cfg", 1)) for piece in own]
    pieces = [piece for pair in zip(own, other) for piece in pair]
    return pieces if meanwhile is None else (pieces, extra)


def gather_tm(block, count):
    return [block] + [lax.ppermute(block, "tm", partners("tm", d)) for d in range(1, count)]


def call(kernel, name, outs, *args, scalars=0, scratch=(), limit=24, space=VMEM, cost=None):
    return pl.pallas_call(
        kernel,
        out_shape=outs,
        in_specs=[SMEM] * scalars + [space] * (len(args) - scalars),
        cost_estimate=cost,
        out_specs=jax.tree.map(lambda _: VMEM, outs),
        scratch_shapes=list(scratch),
        compiler_params=pltpu.CompilerParams(vmem_limit_bytes=limit * 1024 * 1024),
        name=name,
    )(*args)


def split(value):
    high = value.astype(BF16)
    return high, (value - high.astype(F32)).astype(BF16)


def mul(left, right):
    return jnp.dot(left, right, preferred_element_type=F32)


def mul3(left, right):
    return mul(left[0], right[0]) + (mul(left[0], right[1]) + mul(left[1], right[0]))


def column(row):
    size = min(128, row.shape[1])
    same = lax.broadcasted_iota(jnp.int32, (size, size), 0) == lax.broadcasted_iota(jnp.int32, (size, size), 1)
    return jnp.concatenate(
        [
            jnp.sum(jnp.where(same, row[:, at : at + size], 0.0), axis=1, keepdims=True)
            for at in range(0, row.shape[1], size)
        ],
        axis=0,
    )


def total_of(left, right):
    return jnp.sum(jnp.sum(left * right, axis=0, keepdims=True), axis=1, keepdims=True)


def fetch(pairs, sems):
    copies = [pltpu.make_async_copy(src, dst, sems.at[at]) for at, (src, dst) in enumerate(pairs)]
    for copy in copies:
        copy.start()
    for copy in copies:
        copy.wait()


def begin_kernel(targets_hbm, features_hbm, scales_hbm, mask_hbm, residual_ref, scaled_ref, flag_ref, *rest):
    targets_ref, features_ref, scales_ref, mask_ref, sems = rest
    fetch(
        [(mask_hbm, mask_ref), (targets_hbm, targets_ref), (scales_hbm, scales_ref), (features_hbm, features_ref)], sems
    )
    flag_ref[...] = mask_ref[...].astype(F32)
    residual_ref[...] = column(flag_ref[...]) * targets_ref[...]
    scaled_ref[...] = column(scales_ref[...] * (math.sqrt(3.0) * LOG2E)) * features_ref[...]


def split3(value):
    high, rest = value.astype(BF16), value
    rest = rest - high.astype(F32)
    middle = rest.astype(BF16)
    return high, middle, (rest - middle.astype(F32)).astype(BF16)


def mul_tile(high, low, field):
    width = field.shape[1]
    field_high, field_low = split(field)
    both = mul(high, jnp.concatenate([field_high, field_low], axis=1))
    return both[:, :width] + (both[:, width:] + mul(low, field_high))


def layers_kernel(place_ref, steps_ref, mask_ref, noise_ref, _, high_ref, low_ref, flag_ref, ridge_ref):
    width = steps_ref.shape[0]
    for offset in range(steps_ref.shape[1] // width):
        at = pl.ds(offset * width, width)
        high_ref[:, at], low_ref[:, at] = split(
            steps_ref[:, pl.ds(pl.multiple_of((place_ref[1] ^ offset) * width, width), width)]
        )
    flag_ref[...] = column(mask_ref[...])
    ridge_ref[...] = column(noise_ref[...])


def tile_kernel(place_ref, every_ref, _, high_ref, low_ref):
    rows = high_ref.shape[0]
    left = jnp.transpose(every_ref[place_ref[0]])
    left_sq = jnp.sum(left * left, axis=1, keepdims=True)
    high, middle, low = split3(-2.0 * left)
    left = jnp.concatenate([high, high, middle, middle, high, low], axis=1)
    for offset in range(every_ref.shape[0]):
        right = every_ref[place_ref[0] ^ offset]
        right_sq = jnp.sum(right * right, axis=0, keepdims=True)
        high, middle, low = split3(right)
        cross = mul(left, jnp.concatenate([high, middle, high, middle, low, high], axis=0))
        dist2 = jnp.maximum(left_sq + right_sq + cross, 1e-30)
        dist = dist2 * lax.rsqrt(dist2)
        high, low = split((1.0 + LN2 * dist) * jnp.exp2(-dist))
        high_ref[:, pl.ds(offset * rows, rows)] = high
        low_ref[:, pl.ds(offset * rows, rows)] = low


def mul_t(left, right):
    return lax.dot_general(left, right, (((1,), (1,)), ((), ())), preferred_element_type=F32)


def steps_kernel(*refs):
    pieces, (high_ref, low_ref, out_ref) = refs[:-3], refs[-3:]
    field = split(jnp.concatenate([piece[...] for piece in pieces], axis=1))
    out_ref[...] = mul_t(field[0], high_ref[...]) + (mul_t(field[0], low_ref[...]) + mul_t(field[1], high_ref[...]))


def image_of(refs):
    pieces, (high_ref, low_ref, flag_ref, ridge_ref, field_ref) = refs[:-5], refs[-5:]
    mixed = mul_tile(high_ref[...], low_ref[...], jnp.concatenate([piece[...] for piece in pieces], axis=0))
    return flag_ref[...] * mixed + ridge_ref[...] * field_ref[...]


def image_kernel(*refs):
    refs[-1][...] = image_of(refs[:-1])


def moments_kernel(*refs):
    image_ref, residual_ref, second_ref, parts_ref = refs[-4:]
    second = image_of(refs[:-3])
    image, residual = image_ref[...], residual_ref[...]
    second_ref[...] = second
    lane = lax.broadcasted_iota(jnp.int32, parts_ref.shape[1:], 1)
    parts = jnp.zeros(parts_ref.shape[1:], F32)
    for at, pair in enumerate([(residual, residual), (residual, image), (image, image), (image, second)]):
        parts = jnp.where(lane == at, total_of(*pair), parts)
    parts_ref[...] = jnp.broadcast_to(parts[None], parts_ref.shape)


def finish_kernel(parts_ref, residual_ref, image_ref, second_ref, field_ref, left_ref):
    sums = jnp.sum(parts_ref[...], axis=0)
    norm0, first, square, third = (sums[:, at : at + 1] for at in range(4))
    alpha = norm0 / first
    norm1 = norm0 - 2.0 * alpha * first + alpha * alpha * square
    keep = 1.0 + norm1 / norm0
    curv = keep * keep * first - 2.0 * keep * alpha * square + alpha * alpha * third
    beta = norm1 / curv
    residual, image = residual_ref[...], image_ref[...]
    field_ref[...] = (alpha + beta * keep) * residual - (beta * alpha) * image
    left_ref[...] = residual - (alpha + beta * keep) * image + (beta * alpha) * second_ref[...]


def solution(mesh):
    cfg, tm = mesh.shape["cfg"], mesh.shape["tm"]

    def body(targets, features, inv_scales, noise, time_kernel, block_mask):
        rows, width = targets.shape
        count = features.shape[1]
        place = jnp.stack([lax.axis_index("cfg"), lax.axis_index("tm")])
        mask = block_mask.reshape(1, rows)

        def shape(*size, kind=F32):
            return jax.ShapeDtypeStruct(size, kind)

        block = shape(rows, width)
        residual, scaled, flag = call(
            begin_kernel,
            "begin",
            (block, shape(count, rows), shape(1, rows)),
            targets, features.T, inv_scales.reshape(1, count), mask,
            space=HBM,
            scratch=[
                pltpu.VMEM((rows, width), F32),
                pltpu.VMEM((count, rows), F32),
                pltpu.VMEM((1, count), F32),
                pltpu.VMEM((1, rows), mask.dtype),
                pltpu.SemaphoreType.DMA((4,)),
            ],
            limit=LIMIT,
        )

        every = lax.all_gather(scaled, "cfg")
        half, steps, col = shape(rows, cfg * rows, kind=BF16), shape(width, tm * width, kind=BF16), shape(rows, 1)
        steps_high, steps_low, flag, ridge = call(
            layers_kernel,
            "layers",
            (steps, steps, col, col),
            place, time_kernel, flag, noise.reshape(1, rows), every,
            scalars=1,
        )

        def over_time(field):
            return call(steps_kernel, "steps", block, *gather_tm(field, tm), steps_high, steps_low)

        fields, (high, low) = gather_cfg(
            over_time(residual),
            cfg,
            lambda timed: call(tile_kernel, "tile", (half, half), place, every, timed, scalars=1),
        )
        image = call(image_kernel, "image", block, *fields, high, low, flag, ridge, residual)
        second, sums = call(
            moments_kernel,
            "moments",
            (block, shape(cfg * tm, 1, width)),
            *gather_cfg(over_time(image), cfg), high, low, flag, ridge, image, residual,
        )
        sums = lax.all_to_all(sums, ("cfg", "tm"), 0, 0, tiled=True)
        return call(finish_kernel, "finish", (block, block), sums, residual, image, second)

    return jax.shard_map(
        body,
        mesh=mesh,
        in_specs=(P("cfg", "tm"), P("cfg", None), P(), P("cfg"), P("tm", None), P("cfg", "tm")),
        out_specs=(P("cfg", "tm"), P("cfg", "tm")),
        check_vma=False,
    )
```

time: 73.4 us -> 71.1 us (0.969)
  blocking collectives: 14.1 us -> 22.8 us
  Pallas kernels: 1.2 us -> 7.75 us
  matrix products: 5.73 us -> 0 us
  starting transfers between devices: 23.8 us -> 18.1 us
  other arithmetic: 3.61 us -> 0.07 us
  waiting for transfers between devices: 22.4 us -> 20.5 us
    all_gather x0 -> x1, blocking collectives: none -> 10.5 us  [body(): every = lax.all_gather(scaled, 'cfg')]
    pallas_call x2 -> x8, Pallas kernels: 1.2 us -> 7.75 us  [call(): pl.pallas_call(kernel, out_shape=outs, in_specs=[SMEM] * scalars + [space...]
    dot_general x5 -> x0, matrix products: 5.73 us -> none  [the longest x3 4.98 us: dot(): jnp.dot(left, right, precision=precision, preferred_element_type=jnp.floa...]
    ppermute x27 -> x20, starting transfers between devices: 23.8 us -> 18.1 us  [the longest x6 10.1 us: gather_tm(): lax.ppermute(block, 'tm', partners('tm', d))]
    ppermute x27 -> x20, waiting for transfers between devices: 22.4 us -> 20.5 us  [the longest x6 9.76 us: gather_tm(): lax.ppermute(block, 'tm', partners('tm', d))]
    all_to_all x1, blocking collectives: 14.1 us -> 12.3 us  [body(): sums = lax.all_to_all(sums, ('cfg', 'tm'), 0, 0, tiled=True)]
    mul x1 -> x0, other arithmetic: 1 us -> none  [body(): residual = mask * targets]
    reduce_sum x2 -> x0, other arithmetic: 0.99 us -> none  [the longest x1 0.93 us: matern(): jnp.sum(left * left, axis=1)[:, None]]
  transfers between devices with their start and end apart: 27 -> 20, of which waited for: 11 -> 11; matrix products, arithmetic and copies ran while one was open for 9% -> 0% of each run, Pallas kernels for 0% -> 4%
where the time goes in v3:
time: 71.1 us; the launch traced here: 70.8 us
  blocking collectives  22.8 us (32%)
  waiting for transfers between devices  20.5 us (29%)
  starting transfers between devices  18.1 us (25%)
  Pallas kernels  7.75 us (11%)
  local copies, waits for them, and re-layouts  0.86 us (1%)
  between operations  0.73 us (1%)
    all_to_all x1, blocking collectives, body(): sums = lax.all_to_all(sums, ('cfg', 'tm'), 0, 0, tiled=True)  12.3 us
    all_gather x1, blocking collectives, body(): every = lax.all_gather(scaled, 'cfg')  10.5 us
    ppermute x6, starting transfers between devices, gather_tm(): lax.ppermute(block, 'tm', partners('tm', d))  10.1 us
    ppermute x6, waiting for transfers between devices, gather_tm(): lax.ppermute(block, 'tm', partners('tm', d))  9.76 us
    ppermute x6, waiting for transfers between devices, gather_cfg(): lax.ppermute(block, 'cfg', partners('cfg', d))  8.61 us
    pallas_call x8, Pallas kernels, call(): pl.pallas_call(kernel, out_shape=outs, in_specs=[SMEM] * scalars + [space...  7.75 us
    ppermute x6, starting transfers between devices, gather_cfg(): lax.ppermute(block, 'cfg', partners('cfg', d))  7.11 us
    ppermute x8, waiting for transfers between devices, gather_cfg(): other = [lax.ppermute(piece, 'cfg', partners('cfg', 1)) for piece in own]  2.09 us
  transfers between devices with their start and end apart: 20, of which 11 were waited for; matrix products, arithmetic and copies ran while one was open for 0% of the time, Pallas kernels for 4%

profile of v3, /device:TPU:0, one launch (start us, length us, event | category | flops | bytes accessed | tf_op | source)
XLA Modules:
  0.0 70.8 jit_solution(3161485222113361654)
XLA Ops:
  0.6 1.8 %begin.1 = (f32[256,128]{1,0:T(8,128)}, f32[64,256]{1,0:T(8,128)}, f32[1,256]{1,0:T(1,128)}) custom-call(f32[256,128]{1,0:T(8,128)} %targets_hbm.1, f32[64,256]{1,0:T(8,128)} %bitcast.10, f32[1,64]{1,0:T(1,128)} %bitcast.12, s32[1,256]{1,0:T(1,128)} %bitcast.11), custom_call_target="tpu_custom_call" | custom-call | tf_op jit(solution)/shard_map/begin/pallas_call | solution.py:37
  2.5 3.1 %collective-permute-start = (f32[256,128]{1,0:T(8,128)}, f32[256,128]{1,0:T(8,128)S(1)}, u32[]{:S(2)}, u32[]{:S(2)}) collective-permute-start(f32[256,128]{1,0:T(8,128)} %get-tuple-element.16.refs_0_.refs_12_.refs_13_.residual_ref), channel_id=1, source_target_pairs={{0,1},{1,0},{2,3},{3,2},{4,5},{5,4},{6,7},{7,6},{8,9},{9,8},{10,11... | collective-permute-start | bytes 393224 | tf_op jit(solution)/shard_map/ppermute | solution.py:33
  5.6 2.6 %collective-permute-start.1 = (f32[256,128]{1,0:T(8,128)}, f32[256,128]{1,0:T(8,128)S(1)}, u32[]{:S(2)}, u32[]{:S(2)}) collective-permute-start(f32[256,128]{1,0:T(8,128)} %get-tuple-element.16.refs_0_.refs_12_.refs_13_.residual_ref), channel_id=1, source_target_pairs={{0,2},{1,3},{2,0},{3,1},{4,6},{5,7},{6,4},{7,5},{8,10},{9,11},{10,... | collective-permute-start | bytes 393224 | tf_op jit(solution)/shard_map/ppermute | solution.py:33
  8.1 0.0 collective-permute-start.2
  8.2 0.1 pad_add_fusion.place_ref
  8.2 10.5 %all-gather = f32[512,256]{1,0:T(8,128)S(1)} all-gather(f32[64,256]{1,0:T(8,128)} %get-tuple-element.18), channel_id=2, replica_groups=mesh['cfg'=8,'tm'=4] {'cfg'}, dimensions={0}, use_global_device_ids=true | all-gather | bytes 589824 | tf_op jit(solution)/shard_map/all_gather | solution.py:213
  18.7 0.7 copy-done.2
  19.4 0.7 layers.1
  20.1 0.0 collective-permute-done.refs_1_
  20.1 0.0 collective-permute-done.1.refs_2_
  20.1 0.0 collective-permute-done.2.refs_3_
  20.1 0.2 copy-done
  20.3 0.4 steps.2._.refs_0_
  20.7 1.5 %collective-permute-start.8 = (f32[256,128]{1,0:T(8,128)S(1)}, f32[256,128]{1,0:T(8,128)S(1)}, u32[]{:S(2)}, u32[]{:S(2)}) collective-permute-start(f32[256,128]{1,0:T(8,128)S(1)} %steps.2._.refs_0_), channel_id=1, source_target_pairs={{0,24},{4,28},{8,16},{12,20},{16,8},{20,12},{24,0},{28,4},{1,25},{... | collective-permute-start | bytes 393224 | tf_op jit(solution)/shard_map/ppermute | solution.py:23
  22.2 1.2 %collective-permute-start.4 = (f32[256,128]{1,0:T(8,128)S(1)}, f32[256,128]{1,0:T(8,128)S(1)}, u32[]{:S(2)}, u32[]{:S(2)}) collective-permute-start(f32[256,128]{1,0:T(8,128)S(1)} %steps.2._.refs_0_), channel_id=1, source_target_pairs={{0,8},{4,12},{8,0},{12,4},{16,24},{20,28},{24,16},{28,20},{1,9},{5... | collective-permute-start | bytes 393224 | tf_op jit(solution)/shard_map/ppermute | solution.py:23
  23.4 0.8 %collective-permute-start.6 = (f32[256,128]{1,0:T(8,128)S(1)}, f32[256,128]{1,0:T(8,128)S(1)}, u32[]{:S(2)}, u32[]{:S(2)}) collective-permute-start(f32[256,128]{1,0:T(8,128)S(1)} %steps.2._.refs_0_), channel_id=1, source_target_pairs={{0,16},{4,20},{8,24},{12,28},{16,0},{20,4},{24,8},{28,12},{1,17},{... | collective-permute-start | bytes 393224 | tf_op jit(solution)/shard_map/ppermute | solution.py:23
  24.2 2.1 %tile.1 = (bf16[256,2048]{1,0:T(8,128)(2,1)S(1)}, bf16[256,2048]{1,0:T(8,128)(2,1)S(1)}) custom-call(s32[2]{0:T(128)S(1)} %pad_add_fusion.place_ref, f32[8,64,256]{2,1,0:T(8,128)S(1)} %bitcast.8, f32[256,128]{1,0:T(8,128)S(1)} %steps.2._.refs_0_), custom_call_target="tpu_custom_call" | custom-call | tf_op jit(solution)/shard_map/tile/pallas_call | solution.py:37
  26.3 0.1 collective-permute-start.3
  26.4 1.6 %collective-permute-done.8.refs_6_ = f32[256,128]{1,0:T(8,128)S(1)} collective-permute-done((f32[256,128]{1,0:T(8,128)S(1)}, f32[256,128]{1,0:T(8,128)S(1)}, u32[]{:S(2)}, u32[]{:S(2)}) %collective-permute-start.8) | collective-permute-done | bytes 131104 | tf_op jit(solution)/shard_map/ppermute | solution.py:23
  28.0 0.0 collective-permute-start.9
  28.0 2.0 %collective-permute-done.4.refs_2_ = f32[256,128]{1,0:T(8,128)S(1)} collective-permute-done((f32[256,128]{1,0:T(8,128)S(1)}, f32[256,128]{1,0:T(8,128)S(1)}, u32[]{:S(2)}, u32[]{:S(2)}) %collective-permute-start.4) | collective-permute-done | bytes 131104 | tf_op jit(solution)/shard_map/ppermute | solution.py:23
  30.0 0.0 collective-permute-start.5
  30.0 0.2 collective-permute-done.6.refs_4_
  30.2 0.3 collective-permute-start.7
  30.5 0.0 collective-permute-done.3.refs_1_
  30.5 0.0 collective-permute-done.9.refs_7_
  30.5 0.8 %collective-permute-done.5.refs_3_ = f32[256,128]{1,0:T(8,128)S(1)} collective-permute-done((f32[256,128]{1,0:T(8,128)S(1)}, f32[256,128]{1,0:T(8,128)S(1)}, u32[]{:S(2)}, u32[]{:S(2)}) %collective-permute-start.5) | collective-permute-done | bytes 131104 | tf_op jit(solution)/shard_map/ppermute | solution.py:27
  31.3 0.2 collective-permute-done.7.refs_5_
  31.6 0.7 %image.1.refs_0_.refs_12_.image_ref = f32[256,128]{1,0:T(8,128)S(1)} custom-call(f32[256,128]{1,0:T(8,128)S(1)} %steps.2._.refs_0_, f32[256,128]{1,0:T(8,128)S(1)} %collective-permute-done.3.refs_1_, f32[256,128]{1,0:T(8,128)S(1)} %collective-permute-done.4.refs_2_, f32[256,128]{1,0:T(8,128)S(1)} %collective-permute-done.5.refs_3_, ...), custom_call_target="tpu_custom_call" | custom-call | tf_op jit(solution)/shard_map/image/pallas_call | solution.py:37
  32.3 0.7 %collective-permute-start.10 = (f32[256,128]{1,0:T(8,128)S(1)}, f32[256,128]{1,0:T(8,128)S(1)}, u32[]{:S(2)}, u32[]{:S(2)}) collective-permute-start(f32[256,128]{1,0:T(8,128)S(1)} %image.1.refs_0_.refs_12_.image_ref), channel_id=1, source_target_pairs={{0,1},{1,0},{2,3},{3,2},{4,5},{5,4},{6,7},{7,6},{8,9},{9,8},{10,11... | collective-permute-start | bytes 393224 | tf_op jit(solution)/shard_map/ppermute | solution.py:33
  33.0 3.5 %collective-permute-start.11 = (f32[256,128]{1,0:T(8,128)S(1)}, f32[256,128]{1,0:T(8,128)S(1)}, u32[]{:S(2)}, u32[]{:S(2)}) collective-permute-start(f32[256,128]{1,0:T(8,128)S(1)} %image.1.refs_0_.refs_12_.image_ref), channel_id=1, source_target_pairs={{0,2},{1,3},{2,0},{3,1},{4,6},{5,7},{6,4},{7,5},{8,10},{9,11},{10,... | collective-permute-start | bytes 393224 | tf_op jit(solution)/shard_map/ppermute | solution.py:33
  36.5 0.2 collective-permute-start.12
  36.7 3.6 %collective-permute-done.10.refs_1_ = f32[256,128]{1,0:T(8,128)S(1)} collective-permute-done((f32[256,128]{1,0:T(8,128)S(1)}, f32[256,128]{1,0:T(8,128)S(1)}, u32[]{:S(2)}, u32[]{:S(2)}) %collective-permute-start.10) | collective-permute-done | bytes 131104 | tf_op jit(solution)/shard_map/ppermute | solution.py:33
  40.4 6.1 %collective-permute-done.11.refs_2_ = f32[256,128]{1,0:T(8,128)S(1)} collective-permute-done((f32[256,128]{1,0:T(8,128)S(1)}, f32[256,128]{1,0:T(8,128)S(1)}, u32[]{:S(2)}, u32[]{:S(2)}) %collective-permute-start.11) | collective-permute-done | bytes 131104 | tf_op jit(solution)/shard_map/ppermute | solution.py:33
  46.5 0.0 collective-permute-done.12.refs_3_
  46.5 0.4 steps.3.refs_0_
  46.9 1.3 %collective-permute-start.14 = (f32[256,128]{1,0:T(8,128)S(1)}, f32[256,128]{1,0:T(8,128)S(1)}, u32[]{:S(2)}, u32[]{:S(2)}) collective-permute-start(f32[256,128]{1,0:T(8,128)S(1)} %steps.3.refs_0_), channel_id=1, source_target_pairs={{0,8},{4,12},{8,0},{12,4},{16,24},{20,28},{24,16},{28,20},{1,9},{5... | collective-permute-start | bytes 393224 | tf_op jit(solution)/shard_map/ppermute | solution.py:23
  48.2 0.8 %collective-permute-start.16 = (f32[256,128]{1,0:T(8,128)S(1)}, f32[256,128]{1,0:T(8,128)S(1)}, u32[]{:S(2)}, u32[]{:S(2)}) collective-permute-start(f32[256,128]{1,0:T(8,128)S(1)} %steps.3.refs_0_), channel_id=1, source_target_pairs={{0,16},{4,20},{8,24},{12,28},{16,0},{20,4},{24,8},{28,12},{1,17},{... | collective-permute-start | bytes 393224 | tf_op jit(solution)/shard_map/ppermute | solution.py:23
  49.0 1.5 %collective-permute-start.18 = (f32[256,128]{1,0:T(8,128)S(1)}, f32[256,128]{1,0:T(8,128)S(1)}, u32[]{:S(2)}, u32[]{:S(2)}) collective-permute-start(f32[256,128]{1,0:T(8,128)S(1)} %steps.3.refs_0_), channel_id=1, source_target_pairs={{0,24},{4,28},{8,16},{12,20},{16,8},{20,12},{24,0},{28,4},{1,25},{... | collective-permute-start | bytes 393224 | tf_op jit(solution)/shard_map/ppermute | solution.py:23
  50.4 0.0 collective-permute-start.13
  50.4 2.6 %collective-permute-done.14.refs_2_ = f32[256,128]{1,0:T(8,128)S(1)} collective-permute-done((f32[256,128]{1,0:T(8,128)S(1)}, f32[256,128]{1,0:T(8,128)S(1)}, u32[]{:S(2)}, u32[]{:S(2)}) %collective-permute-start.14) | collective-permute-done | bytes 131104 | tf_op jit(solution)/shard_map/ppermute | solution.py:23
  53.0 2.2 %collective-permute-done.16.refs_4_ = f32[256,128]{1,0:T(8,128)S(1)} collective-permute-done((f32[256,128]{1,0:T(8,128)S(1)}, f32[256,128]{1,0:T(8,128)S(1)}, u32[]{:S(2)}, u32[]{:S(2)}) %collective-permute-start.16) | collective-permute-done | bytes 131104 | tf_op jit(solution)/shard_map/ppermute | solution.py:23
  55.3 0.5 collective-permute-start.19
  55.8 0.8 %collective-permute-done.17.refs_5_ = f32[256,128]{1,0:T(8,128)S(1)} collective-permute-done((f32[256,128]{1,0:T(8,128)S(1)}, f32[256,128]{1,0:T(8,128)S(1)}, u32[]{:S(2)}, u32[]{:S(2)}) %collective-permute-start.17) | collective-permute-done | bytes 131104 | tf_op jit(solution)/shard_map/ppermute | solution.py:27
  56.6 0.2 collective-permute-done.19.refs_7_
  56.8 0.8 %moments.1 = (f32[256,128]{1,0:T(8,128)S(1)}, f32[32,1,128]{2,1,0:T(1,128)S(1)}) custom-call(f32[256,128]{1,0:T(8,128)S(1)} %steps.3.refs_0_, f32[256,128]{1,0:T(8,128)S(1)} %collective-permute-done.13.refs_1_, f32[256,128]{1,0:T(8,128)S(1)} %collective-permute-done.14.refs_2_, f32[256,128]{1,0:T(8,128)S(1)} %collective-permute-done.15.refs_3_, ...), custom_call_target="tpu_custom_call" | custom-call | tf_op jit(solution)/shard_map/moments/pallas_call | solution.py:37
  57.6 12.3 %all_to_all.5.parts_ref = f32[32,1,128]{2,1,0:T(1,128)S(1)} all-to-all(f32[32,1,128]{2,1,0:T(1,128)S(1)} %get-tuple-element.28), channel_id=1, replica_groups=mesh['cfg'=8,'tm'=4] {'cfg','tm'}, dimensions={0} | all-to-all | bytes 32768 | tf_op jit(solution)/shard_map/all_to_all | solution.py:238
  69.9 0.9 %finish.1 = (f32[256,128]{1,0:T(8,128)}, f32[256,128]{1,0:T(8,128)}) custom-call(f32[32,1,128]{2,1,0:T(1,128)S(1)} %all_to_all.5.parts_ref, f32[256,128]{1,0:T(8,128)S(1)} %copy-done, f32[256,128]{1,0:T(8,128)S(1)} %image.1.refs_0_.refs_12_.image_ref, f32[256,128]{1,0:T(8,128)S(1)} %get-tuple-element.29.second_ref), custom_call_target="tpu_custom_call" | custom-call | tf_op jit(solution)/shard_map/finish/pallas_call | solution.py:37
  (11 shorter events, 0.0 us)
Async XLA Ops:
  2.5 17.6 %collective-permute-start = (f32[256,128]{1,0:T(8,128)}, f32[256,128]{1,0:T(8,128)S(1)}, u32[]{:S(2)}, u32[]{:S(2)}) collective-permute-start(f32[256,128]{1,0:T(8,128)} %get-tuple-element.16.refs_0_.refs_12_.refs_13_.residual_ref), channel_id=1, source_target_pairs={{0,1},{1,0},{2,3},{3,2},{4,5},{5,4},{6,7},{7,6},{8,9},{9,8},{10,11... | collective-permute-start | bytes 393224 | tf_op jit(solution)/shard_map/ppermute | solution.py:33
  5.6 14.5 %collective-permute-start.1 = (f32[256,128]{1,0:T(8,128)}, f32[256,128]{1,0:T(8,128)S(1)}, u32[]{:S(2)}, u32[]{:S(2)}) collective-permute-start(f32[256,128]{1,0:T(8,128)} %get-tuple-element.16.refs_0_.refs_12_.refs_13_.residual_ref), channel_id=1, source_target_pairs={{0,2},{1,3},{2,0},{3,1},{4,6},{5,7},{6,4},{7,5},{8,10},{9,11},{10,... | collective-permute-start | bytes 393224 | tf_op jit(solution)/shard_map/ppermute | solution.py:33
  8.1 12.0 %collective-permute-start.2 = (f32[256,128]{1,0:T(8,128)}, f32[256,128]{1,0:T(8,128)S(1)}, u32[]{:S(2)}, u32[]{:S(2)}) collective-permute-start(f32[256,128]{1,0:T(8,128)} %get-tuple-element.16.refs_0_.refs_12_.refs_13_.residual_ref), channel_id=1, source_target_pairs={{0,3},{1,2},{2,1},{3,0},{4,7},{5,6},{6,5},{7,4},{8,11},{9,10},{10,... | collective-permute-start | bytes 393224 | tf_op jit(solution)/shard_map/ppermute | solution.py:33
  8.2 10.5 %copy-start.1 = (f32[128,512]{1,0:T(8,128)S(1)}, f32[128,512]{1,0:T(8,128)}, u32[]{:S(2)}) copy-start(f32[128,512]{1,0:T(8,128)} %steps_ref.1) | copy-start | bytes 786436
  8.2 10.5 %copy-start.3 = (f32[1,256]{1,0:T(1,128)S(1)}, f32[1,256]{1,0:T(1,128)}, u32[]{:S(2)}) copy-start(f32[1,256]{1,0:T(1,128)} %get-tuple-element.17.mask_ref) | copy-start | bytes 3076
  18.7 0.7 copy-start.2
  19.4 0.9 %copy-start = (f32[256,128]{1,0:T(8,128)S(1)}, f32[256,128]{1,0:T(8,128)}, u32[]{:S(2)}) copy-start(f32[256,128]{1,0:T(8,128)} %get-tuple-element.16.refs_0_.refs_12_.refs_13_.residual_ref) | copy-start | bytes 393220
  20.7 7.3 %collective-permute-start.8 = (f32[256,128]{1,0:T(8,128)S(1)}, f32[256,128]{1,0:T(8,128)S(1)}, u32[]{:S(2)}, u32[]{:S(2)}) collective-permute-start(f32[256,128]{1,0:T(8,128)S(1)} %steps.2._.refs_0_), channel_id=1, source_target_pairs={{0,24},{4,28},{8,16},{12,20},{16,8},{20,12},{24,0},{28,4},{1,25},{... | collective-permute-start | bytes 393224 | tf_op jit(solution)/shard_map/ppermute | solution.py:23
  22.2 7.7 %collective-permute-start.4 = (f32[256,128]{1,0:T(8,128)S(1)}, f32[256,128]{1,0:T(8,128)S(1)}, u32[]{:S(2)}, u32[]{:S(2)}) collective-permute-start(f32[256,128]{1,0:T(8,128)S(1)} %steps.2._.refs_0_), channel_id=1, source_target_pairs={{0,8},{4,12},{8,0},{12,4},{16,24},{20,28},{24,16},{28,20},{1,9},{5... | collective-permute-start | bytes 393224 | tf_op jit(solution)/shard_map/ppermute | solution.py:23
  23.4 6.8 %collective-permute-start.6 = (f32[256,128]{1,0:T(8,128)S(1)}, f32[256,128]{1,0:T(8,128)S(1)}, u32[]{:S(2)}, u32[]{:S(2)}) collective-permute-start(f32[256,128]{1,0:T(8,128)S(1)} %steps.2._.refs_0_), channel_id=1, source_target_pairs={{0,16},{4,20},{8,24},{12,28},{16,0},{20,4},{24,8},{28,12},{1,17},{... | collective-permute-start | bytes 393224 | tf_op jit(solution)/shard_map/ppermute | solution.py:23
  26.3 4.2 %collective-permute-start.3 = (f32[256,128]{1,0:T(8,128)S(1)}, f32[256,128]{1,0:T(8,128)S(1)}, u32[]{:S(2)}, u32[]{:S(2)}) collective-permute-start(f32[256,128]{1,0:T(8,128)S(1)} %steps.2._.refs_0_), channel_id=1, source_target_pairs={{0,4},{4,0},{8,12},{12,8},{16,20},{20,16},{24,28},{28,24},{1,5},{5... | collective-permute-start | bytes 393224 | tf_op jit(solution)/shard_map/ppermute | solution.py:27
  28.0 2.5 %collective-permute-start.9 = (f32[256,128]{1,0:T(8,128)S(1)}, f32[256,128]{1,0:T(8,128)S(1)}, u32[]{:S(2)}, u32[]{:S(2)}) collective-permute-start(f32[256,128]{1,0:T(8,128)S(1)} %collective-permute-done.8.refs_6_), channel_id=1, source_target_pairs={{0,4},{4,0},{8,12},{12,8},{16,20},{20,16},{24,28},{28,24},{1,5},{5... | collective-permute-start | bytes 393224 | tf_op jit(solution)/shard_map/ppermute | solution.py:27
  30.0 1.3 %collective-permute-start.5 = (f32[256,128]{1,0:T(8,128)S(1)}, f32[256,128]{1,0:T(8,128)S(1)}, u32[]{:S(2)}, u32[]{:S(2)}) collective-permute-start(f32[256,128]{1,0:T(8,128)S(1)} %collective-permute-done.4.refs_2_), channel_id=1, source_target_pairs={{0,4},{4,0},{8,12},{12,8},{16,20},{20,16},{24,28},{28,24},{1,5},{5... | collective-permute-start | bytes 393224 | tf_op jit(solution)/shard_map/ppermute | solution.py:27
  30.2 1.3 %collective-permute-start.7 = (f32[256,128]{1,0:T(8,128)S(1)}, f32[256,128]{1,0:T(8,128)S(1)}, u32[]{:S(2)}, u32[]{:S(2)}) collective-permute-start(f32[256,128]{1,0:T(8,128)S(1)} %collective-permute-done.6.refs_4_), channel_id=1, source_target_pairs={{0,4},{4,0},{8,12},{12,8},{16,20},{20,16},{24,28},{28,24},{1,5},{5... | collective-permute-start | bytes 393224 | tf_op jit(solution)/shard_map/ppermute | solution.py:27
  32.3 8.1 %collective-permute-start.10 = (f32[256,128]{1,0:T(8,128)S(1)}, f32[256,128]{1,0:T(8,128)S(1)}, u32[]{:S(2)}, u32[]{:S(2)}) collective-permute-start(f32[256,128]{1,0:T(8,128)S(1)} %image.1.refs_0_.refs_12_.image_ref), channel_id=1, source_target_pairs={{0,1},{1,0},{2,3},{3,2},{4,5},{5,4},{6,7},{7,6},{8,9},{9,8},{10,11... | collective-permute-start | bytes 393224 | tf_op jit(solution)/shard_map/ppermute | solution.py:33
  33.0 13.5 %collective-permute-start.11 = (f32[256,128]{1,0:T(8,128)S(1)}, f32[256,128]{1,0:T(8,128)S(1)}, u32[]{:S(2)}, u32[]{:S(2)}) collective-permute-start(f32[256,128]{1,0:T(8,128)S(1)} %image.1.refs_0_.refs_12_.image_ref), channel_id=1, source_target_pairs={{0,2},{1,3},{2,0},{3,1},{4,6},{5,7},{6,4},{7,5},{8,10},{9,11},{10,... | collective-permute-start | bytes 393224 | tf_op jit(solution)/shard_map/ppermute | solution.py:33
  36.5 10.0 %collective-permute-start.12 = (f32[256,128]{1,0:T(8,128)S(1)}, f32[256,128]{1,0:T(8,128)S(1)}, u32[]{:S(2)}, u32[]{:S(2)}) collective-permute-start(f32[256,128]{1,0:T(8,128)S(1)} %image.1.refs_0_.refs_12_.image_ref), channel_id=1, source_target_pairs={{0,3},{1,2},{2,1},{3,0},{4,7},{5,6},{6,5},{7,4},{8,11},{9,10},{10,... | collective-permute-start | bytes 393224 | tf_op jit(solution)/shard_map/ppermute | solution.py:33
  46.9 6.1 %collective-permute-start.14 = (f32[256,128]{1,0:T(8,128)S(1)}, f32[256,128]{1,0:T(8,128)S(1)}, u32[]{:S(2)}, u32[]{:S(2)}) collective-permute-start(f32[256,128]{1,0:T(8,128)S(1)} %steps.3.refs_0_), channel_id=1, source_target_pairs={{0,8},{4,12},{8,0},{12,4},{16,24},{20,28},{24,16},{28,20},{1,9},{5... | collective-permute-start | bytes 393224 | tf_op jit(solution)/shard_map/ppermute | solution.py:23
  48.2 7.1 %collective-permute-start.16 = (f32[256,128]{1,0:T(8,128)S(1)}, f32[256,128]{1,0:T(8,128)S(1)}, u32[]{:S(2)}, u32[]{:S(2)}) collective-permute-start(f32[256,128]{1,0:T(8,128)S(1)} %steps.3.refs_0_), channel_id=1, source_target_pairs={{0,16},{4,20},{8,24},{12,28},{16,0},{20,4},{24,8},{28,12},{1,17},{... | collective-permute-start | bytes 393224 | tf_op jit(solution)/shard_map/ppermute | solution.py:23
  49.0 6.3 %collective-permute-start.18 = (f32[256,128]{1,0:T(8,128)S(1)}, f32[256,128]{1,0:T(8,128)S(1)}, u32[]{:S(2)}, u32[]{:S(2)}) collective-permute-start(f32[256,128]{1,0:T(8,128)S(1)} %steps.3.refs_0_), channel_id=1, source_target_pairs={{0,24},{4,28},{8,16},{12,20},{16,8},{20,12},{24,0},{28,4},{1,25},{... | collective-permute-start | bytes 393224 | tf_op jit(solution)/shard_map/ppermute | solution.py:23
  50.4 5.3 %collective-permute-start.13 = (f32[256,128]{1,0:T(8,128)S(1)}, f32[256,128]{1,0:T(8,128)S(1)}, u32[]{:S(2)}, u32[]{:S(2)}) collective-permute-start(f32[256,128]{1,0:T(8,128)S(1)} %steps.3.refs_0_), channel_id=1, source_target_pairs={{0,4},{4,0},{8,12},{12,8},{16,20},{20,16},{24,28},{28,24},{1,5},{5... | collective-permute-start | bytes 393224 | tf_op jit(solution)/shard_map/ppermute | solution.py:27
  53.0 2.7 %collective-permute-start.15 = (f32[256,128]{1,0:T(8,128)S(1)}, f32[256,128]{1,0:T(8,128)S(1)}, u32[]{:S(2)}, u32[]{:S(2)}) collective-permute-start(f32[256,128]{1,0:T(8,128)S(1)} %collective-permute-done.14.refs_2_), channel_id=1, source_target_pairs={{0,4},{4,0},{8,12},{12,8},{16,20},{20,16},{24,28},{28,24},{1,5},{5... | collective-permute-start | bytes 393224 | tf_op jit(solution)/shard_map/ppermute | solution.py:27
  55.2 1.3 %collective-permute-start.17 = (f32[256,128]{1,0:T(8,128)S(1)}, f32[256,128]{1,0:T(8,128)S(1)}, u32[]{:S(2)}, u32[]{:S(2)}) collective-permute-start(f32[256,128]{1,0:T(8,128)S(1)} %collective-permute-done.16.refs_4_), channel_id=1, source_target_pairs={{0,4},{4,0},{8,12},{12,8},{16,20},{20,16},{24,28},{28,24},{1,5},{5... | collective-permute-start | bytes 393224 | tf_op jit(solution)/shard_map/ppermute | solution.py:27
  55.3 1.5 %collective-permute-start.19 = (f32[256,128]{1,0:T(8,128)S(1)}, f32[256,128]{1,0:T(8,128)S(1)}, u32[]{:S(2)}, u32[]{:S(2)}) collective-permute-start(f32[256,128]{1,0:T(8,128)S(1)} %collective-permute-done.18.refs_6_), channel_id=1, source_target_pairs={{0,4},{4,0},{8,12},{12,8},{16,20},{20,16},{24,28},{28,24},{1,5},{5... | collective-permute-start | bytes 393224 | tf_op jit(solution)/shard_map/ppermute | solution.py:27

commit v4 on v3

--- a/solution.py
+++ b/solution.py
@@ -25,8 +25,7 @@
         extra = meanwhile(block)
         *extra, own[-1] = lax.optimization_barrier((*extra, own[-1]))
     other = [lax.ppermute(piece, "cfg", partners("cfg", 1)) for piece in own]
-    pieces = [piece for pair in zip(own, other) for piece in pair]
-    return pieces if meanwhile is None else (pieces, extra)
+    return own + other if meanwhile is None else (own + other, extra)
 
 
 def gather_tm(block, count):
@@ -107,33 +106,34 @@
     return both[:, :width] + (both[:, width:] + mul(low, field_high))
 
 
-def layers_kernel(place_ref, steps_ref, mask_ref, noise_ref, _, high_ref, low_ref, flag_ref, ridge_ref):
+def layers_kernel(place_ref, steps_ref, mask_ref, noise_ref, high_ref, low_ref, flag_ref, ridge_ref):
     width = steps_ref.shape[0]
     for offset in range(steps_ref.shape[1] // width):
         at = pl.ds(offset * width, width)
         high_ref[:, at], low_ref[:, at] = split(
-            steps_ref[:, pl.ds(pl.multiple_of((place_ref[1] ^ offset) * width, width), width)]
+            steps_ref[:, pl.ds(pl.multiple_of((place_ref[0] ^ offset) * width, width), width)]
         )
     flag_ref[...] = column(mask_ref[...])
     ridge_ref[...] = column(noise_ref[...])
 
 
-def tile_kernel(place_ref, every_ref, _, high_ref, low_ref):
+def tile_kernel(*refs):
+    pieces, (_, high_ref, low_ref) = refs[:-3], refs[-3:]
     rows = high_ref.shape[0]
-    left = jnp.transpose(every_ref[place_ref[0]])
+    left = jnp.transpose(pieces[0][...])
     left_sq = jnp.sum(left * left, axis=1, keepdims=True)
     high, middle, low = split3(-2.0 * left)
     left = jnp.concatenate([high, high, middle, middle, high, low], axis=1)
-    for offset in range(every_ref.shape[0]):
-        right = every_ref[place_ref[0] ^ offset]
+    for at, piece in enumerate(pieces):
+        right = piece[...]
         right_sq = jnp.sum(right * right, axis=0, keepdims=True)
         high, middle, low = split3(right)
         cross = mul(left, jnp.concatenate([high, middle, high, middle, low, high], axis=0))
         dist2 = jnp.maximum(left_sq + right_sq + cross, 1e-30)
         dist = dist2 * lax.rsqrt(dist2)
         high, low = split((1.0 + LN2 * dist) * jnp.exp2(-dist))
-        high_ref[:, pl.ds(offset * rows, rows)] = high
-        low_ref[:, pl.ds(offset * rows, rows)] = low
+        high_ref[:, pl.ds(at * rows, rows)] = high
+        low_ref[:, pl.ds(at * rows, rows)] = low
 
 
 def mul_t(left, right):
@@ -146,9 +146,18 @@
     out_ref[...] = mul_t(field[0], high_ref[...]) + (mul_t(field[0], low_ref[...]) + mul_t(field[1], high_ref[...]))
 
 
+def partial_kernel(*refs):
+    pieces, (high_ref, low_ref, out_ref) = refs[:-3], refs[-3:]
+    field = jnp.concatenate([piece[...] for piece in pieces], axis=0)
+    at = pl.ds(0, field.shape[0])
+    out_ref[...] = mul_tile(high_ref[:, at], low_ref[:, at], field)
+
+
 def image_of(refs):
-    pieces, (high_ref, low_ref, flag_ref, ridge_ref, field_ref) = refs[:-5], refs[-5:]
-    mixed = mul_tile(high_ref[...], low_ref[...], jnp.concatenate([piece[...] for piece in pieces], axis=0))
+    pieces, (partial_ref, high_ref, low_ref, flag_ref, ridge_ref, field_ref) = refs[:-6], refs[-6:]
+    field = jnp.concatenate([piece[...] for piece in pieces], axis=0)
+    at = pl.ds(high_ref.shape[1] - field.shape[0], field.shape[0])
+    mixed = partial_ref[...] + mul_tile(high_ref[:, at], low_ref[:, at], field)
     return flag_ref[...] * mixed + ridge_ref[...] * field_ref[...]
 
 
@@ -187,7 +196,7 @@
     def body(targets, features, inv_scales, noise, time_kernel, block_mask):
         rows, width = targets.shape
         count = features.shape[1]
-        place = jnp.stack([lax.axis_index("cfg"), lax.axis_index("tm")])
+        place = lax.axis_index("tm").reshape(1)
         mask = block_mask.reshape(1, rows)
 
         def shape(*size, kind=F32):
@@ -197,7 +206,7 @@
         residual, scaled, flag = call(
             begin_kernel,
             "begin",
-            (block, shape(count, rows), shape(1, rows)),
+            (pltpu.VMEM((rows, width), F32), pltpu.VMEM((count, rows), F32), pltpu.VMEM((1, rows), F32)),
             targets, features.T, inv_scales.reshape(1, count), mask,
             space=HBM,
             scratch=[
@@ -210,30 +219,34 @@
             limit=LIMIT,
         )
 
-        every = lax.all_gather(scaled, "cfg")
         half, steps, col = shape(rows, cfg * rows, kind=BF16), shape(width, tm * width, kind=BF16), shape(rows, 1)
         steps_high, steps_low, flag, ridge = call(
             layers_kernel,
             "layers",
             (steps, steps, col, col),
-            place, time_kernel, flag, noise.reshape(1, rows), every,
+            place, time_kernel, flag, noise.reshape(1, rows),
             scalars=1,
         )
-
-        def over_time(field):
-            return call(steps_kernel, "steps", block, *gather_tm(field, tm), steps_high, steps_low)
+        residuals, every = lax.optimization_barrier((gather_tm(residual, tm), gather_cfg(scaled, cfg)))
+
+        def over_time(pieces):
+            return call(steps_kernel, "steps", block, *pieces, steps_high, steps_low)
 
         fields, (high, low) = gather_cfg(
-            over_time(residual),
-            cfg,
-            lambda timed: call(tile_kernel, "tile", (half, half), place, every, timed, scalars=1),
-        )
-        image = call(image_kernel, "image", block, *fields, high, low, flag, ridge, residual)
+            over_time(residuals), cfg, lambda timed: call(tile_kernel, "tile", (half, half), *every, timed)
+        )
+
+        def over_cfg(pieces):
+            early = len(pieces) // 2 + 1
+            partial = call(partial_kernel, "partial", block, *pieces[:early], high, low)
+            return [*pieces[early:], partial, high, low, flag, ridge]
+
+        image = call(image_kernel, "image", block, *over_cfg(fields), residual)
         second, sums = call(
             moments_kernel,
             "moments",
             (block, shape(cfg * tm, 1, width)),
-            *gather_cfg(over_time(image), cfg), high, low, flag, ridge, image, residual,
+            *over_cfg(gather_cfg(over_time(gather_tm(image, tm)), cfg)), image, residual,
         )
         sums = lax.all_to_all(sums, ("cfg", "tm"), 0, 0, tiled=True)
         return call(finish_kernel, "finish", (block, block), sums, residual, image, second)

time: 71.1 us -> 68.4 us (0.962)
  blocking collectives: 22.8 us -> 12.8 us
  waiting for transfers between devices: 20.5 us -> 25.3 us
  starting transfers between devices: 18.1 us -> 21.4 us
  Pallas kernels: 7.75 us -> 6.32 us
  local copies, waits for them, and re-layouts: 0.86 us -> 1.63 us
    all_gather x1 -> x0, blocking collectives: 10.5 us -> none  [body(): every = lax.all_gather(scaled, 'cfg')]
    ppermute x6 -> x9, starting transfers between devices: 7.11 us -> 11.9 us  [gather_cfg(): lax.ppermute(block, 'cfg', partners('cfg', d))]
    ppermute x6 -> x9, waiting for transfers between devices: 8.61 us -> 11.3 us  [gather_cfg(): lax.ppermute(block, 'cfg', partners('cfg', d))]
    ppermute x6, waiting for transfers between devices: 9.76 us -> 12.4 us  [gather_tm(): lax.ppermute(block, 'tm', partners('tm', d))]
    pallas_call x8 -> x10, Pallas kernels: 7.75 us -> 6.32 us  [call(): pl.pallas_call(kernel, out_shape=outs, in_specs=[SMEM] * scalars + [space...]
    ppermute x6, starting transfers between devices: 10.1 us -> 8.84 us  [gather_tm(): lax.ppermute(block, 'tm', partners('tm', d))]
    unnamed x8 -> x4, local copies, waits for them, and re-layouts: 0.86 us -> 1.63 us
    ppermute x8 -> x12, waiting for transfers between devices: 2.09 us -> 1.65 us  [gather_cfg(): other = [lax.ppermute(piece, 'cfg', partners('cfg', 1)) for piece in own]]
  transfers between devices with their start and end apart: 20 -> 27, of which waited for: 11 -> 12; matrix products, arithmetic and copies ran while one was open for 0% -> 0% of each run, Pallas kernels for 4% -> 4%
where the time goes in v4:
time: 68.4 us; the launch traced here: 68.2 us
  waiting for transfers between devices  25.3 us (37%)
  starting transfers between devices  21.4 us (31%)
  blocking collectives  12.8 us (19%)
  Pallas kernels  6.32 us (9%)
  local copies, waits for them, and re-layouts  1.63 us (2%)
  between operations  0.75 us (1%)
    all_to_all x1, blocking collectives, body(): sums = lax.all_to_all(sums, ('cfg', 'tm'), 0, 0, tiled=True)  12.8 us
    ppermute x6, waiting for transfers between devices, gather_tm(): lax.ppermute(block, 'tm', partners('tm', d))  12.4 us
    ppermute x9, starting transfers between devices, gather_cfg(): lax.ppermute(block, 'cfg', partners('cfg', d))  11.9 us
    ppermute x9, waiting for transfers between devices, gather_cfg(): lax.ppermute(block, 'cfg', partners('cfg', d))  11.3 us
    ppermute x6, starting transfers between devices, gather_tm(): lax.ppermute(block, 'tm', partners('tm', d))  8.84 us
    pallas_call x10, Pallas kernels, call(): pl.pallas_call(kernel, out_shape=outs, in_specs=[SMEM] * scalars + [space...  6.32 us
    ppermute x12, waiting for transfers between devices, gather_cfg(): other = [lax.ppermute(piece, 'cfg', partners('cfg', 1)) for piece in own]  1.65 us
    unnamed x4, local copies, waits for them, and re-layouts  1.63 us
  transfers between devices with their start and end apart: 27, of which 12 were waited for; matrix products, arithmetic and copies ran while one was open for 0% of the time, Pallas kernels for 4%

profile of v4, /device:TPU:0, one launch (start us, length us, event | category | flops | bytes accessed | tf_op | source)
XLA Modules:
  0.0 68.2 jit_solution(8805451426131976815)
XLA Ops:
  0.6 1.2 %begin.1 = (f32[256,128]{1,0:T(8,128)S(1)}, f32[64,256]{1,0:T(8,128)S(1)}, f32[1,256]{1,0:T(1,128)S(1)}) custom-call(f32[256,128]{1,0:T(8,128)} %targets_hbm.1, f32[64,256]{1,0:T(8,128)} %bitcast.6, f32[1,64]{1,0:T(1,128)} %bitcast.8, s32[1,256]{1,0:T(1,128)} %bitcast.7), custom_call_target="tpu_custom_call" | custom-call | tf_op jit(solution)/shard_map/begin/pallas_call | solution.py:36
  1.8 3.0 %collective-permute-start.3 = (f32[64,256]{1,0:T(8,128)S(1)}, f32[64,256]{1,0:T(8,128)S(1)}, u32[]{:S(2)}, u32[]{:S(2)}) collective-permute-start(f32[64,256]{1,0:T(8,128)S(1)} %get-tuple-element.37.refs_0_), channel_id=1, source_target_pairs={{0,8},{4,12},{8,0},{12,4},{16,24},{20,28},{24,16},{28,20},{1,9},{5... | collective-permute-start | bytes 196616 | tf_op jit(solution)/shard_map/ppermute | solution.py:23
  4.8 1.5 %collective-permute-start.4 = (f32[64,256]{1,0:T(8,128)S(1)}, f32[64,256]{1,0:T(8,128)S(1)}, u32[]{:S(2)}, u32[]{:S(2)}) collective-permute-start(f32[64,256]{1,0:T(8,128)S(1)} %get-tuple-element.37.refs_0_), channel_id=1, source_target_pairs={{0,16},{4,20},{8,24},{12,28},{16,0},{20,4},{24,8},{28,12},{1,17},{... | collective-permute-start | bytes 196616 | tf_op jit(solution)/shard_map/ppermute | solution.py:23
  6.3 1.6 %collective-permute-start = (f32[256,128]{1,0:T(8,128)S(1)}, f32[256,128]{1,0:T(8,128)S(1)}, u32[]{:S(2)}, u32[]{:S(2)}) collective-permute-start(f32[256,128]{1,0:T(8,128)S(1)} %get-tuple-element.30.refs_0_.refs_8_.refs_9_.residual_ref), channel_id=1, source_target_pairs={{0,1},{1,0},{2,3},{3,2},{4,5},{5,4},{6,7},{7,6},{8,9},{9,8},{10,11... | collective-permute-start | bytes 393224 | tf_op jit(solution)/shard_map/ppermute | solution.py:32
  7.9 2.6 %collective-permute-start.1 = (f32[256,128]{1,0:T(8,128)S(1)}, f32[256,128]{1,0:T(8,128)S(1)}, u32[]{:S(2)}, u32[]{:S(2)}) collective-permute-start(f32[256,128]{1,0:T(8,128)S(1)} %get-tuple-element.30.refs_0_.refs_8_.refs_9_.residual_ref), channel_id=1, source_target_pairs={{0,2},{1,3},{2,0},{3,1},{4,6},{5,7},{6,4},{7,5},{8,10},{9,11},{10,... | collective-permute-start | bytes 393224 | tf_op jit(solution)/shard_map/ppermute | solution.py:32
  10.5 0.2 collective-permute-start.2
  10.7 0.3 collective-permute-start.5
  11.0 0.0 collective-permute-start.6
  11.0 4.9 %collective-permute-done.5.refs_3_ = f32[64,256]{1,0:T(8,128)S(1)} collective-permute-done((f32[64,256]{1,0:T(8,128)S(1)}, f32[64,256]{1,0:T(8,128)S(1)}, u32[]{:S(2)}, u32[]{:S(2)}) %collective-permute-start.5) | collective-permute-done | bytes 65568 | tf_op jit(solution)/shard_map/ppermute | solution.py:23
  15.9 0.0 collective-permute-start.7
  15.9 0.0 collective-permute-done.6.refs_4_
  15.9 0.5 collective-permute-start.8
  16.4 0.1 collective-permute-start.9
  16.5 0.7 copy-done.1
  17.2 0.9 %copy-done = f32[128,512]{1,0:T(8,128)S(1)} copy-done((f32[128,512]{1,0:T(8,128)S(1)}, f32[128,512]{1,0:T(8,128)}, u32[]{:S(2)}) %copy-start) | copy-done | bytes 262168
  18.1 0.1 layers.1
  18.3 2.0 %collective-permute-done.1.refs_2_ = f32[256,128]{1,0:T(8,128)S(1)} collective-permute-done((f32[256,128]{1,0:T(8,128)S(1)}, f32[256,128]{1,0:T(8,128)S(1)}, u32[]{:S(2)}, u32[]{:S(2)}) %collective-permute-start.1) | collective-permute-done | bytes 131104 | tf_op jit(solution)/shard_map/ppermute | solution.py:32
  20.3 0.0 collective-permute-done.2.refs_3_
  20.3 0.0 collective-permute-done.7.refs_5_
  20.3 0.4 steps.2.refs_8_.refs_0_
  20.7 0.5 collective-permute-start.14
  21.2 1.5 %collective-permute-start.10 = (f32[256,128]{1,0:T(8,128)S(1)}, f32[256,128]{1,0:T(8,128)S(1)}, u32[]{:S(2)}, u32[]{:S(2)}) collective-permute-start(f32[256,128]{1,0:T(8,128)S(1)} %steps.2.refs_8_.refs_0_), channel_id=1, source_target_pairs={{0,8},{4,12},{8,0},{12,4},{16,24},{20,28},{24,16},{28,20},{1,9},{5... | collective-permute-start | bytes 393224 | tf_op jit(solution)/shard_map/ppermute | solution.py:23
  22.7 1.5 %collective-permute-start.12 = (f32[256,128]{1,0:T(8,128)S(1)}, f32[256,128]{1,0:T(8,128)S(1)}, u32[]{:S(2)}, u32[]{:S(2)}) collective-permute-start(f32[256,128]{1,0:T(8,128)S(1)} %steps.2.refs_8_.refs_0_), channel_id=1, source_target_pairs={{0,16},{4,20},{8,24},{12,28},{16,0},{20,4},{24,8},{28,12},{1,17},{... | collective-permute-start | bytes 393224 | tf_op jit(solution)/shard_map/ppermute | solution.py:23
  24.2 1.5 %tile.1 = (bf16[256,2048]{1,0:T(8,128)(2,1)S(1)}, bf16[256,2048]{1,0:T(8,128)(2,1)S(1)}) custom-call(f32[64,256]{1,0:T(8,128)S(1)} %get-tuple-element.37.refs_0_, f32[64,256]{1,0:T(8,128)S(1)} %collective-permute-done.3.refs_1_, f32[64,256]{1,0:T(8,128)S(1)} %collective-permute-done.4.refs_2_, f32[64,256]{1,0:T(8,128)S(1)} %collective-permute-done.5.refs_3_, ...), custom_call_target="tpu_custom_call" | custom-call | tf_op jit(solution)/shard_map/tile/pallas_call | solution.py:36
  25.8 1.2 %collective-permute-done.14.refs_3_ = f32[256,128]{1,0:T(8,128)S(1)} collective-permute-done((f32[256,128]{1,0:T(8,128)S(1)}, f32[256,128]{1,0:T(8,128)S(1)}, u32[]{:S(2)}, u32[]{:S(2)}) %collective-permute-start.14) | collective-permute-done | bytes 131104 | tf_op jit(solution)/shard_map/ppermute | solution.py:23
  27.0 0.4 collective-permute-done.10.refs_1_
  27.4 0.1 collective-permute-start.11
  27.5 0.8 %collective-permute-done.12.refs_2_ = f32[256,128]{1,0:T(8,128)S(1)} collective-permute-done((f32[256,128]{1,0:T(8,128)S(1)}, f32[256,128]{1,0:T(8,128)S(1)}, u32[]{:S(2)}, u32[]{:S(2)}) %collective-permute-start.12) | collective-permute-done | bytes 131104 | tf_op jit(solution)/shard_map/ppermute | solution.py:23
  28.3 0.5 partial.2.refs_3_
  28.9 0.8 %collective-permute-done.13.refs_1_ = f32[256,128]{1,0:T(8,128)S(1)} collective-permute-done((f32[256,128]{1,0:T(8,128)S(1)}, f32[256,128]{1,0:T(8,128)S(1)}, u32[]{:S(2)}, u32[]{:S(2)}) %collective-permute-start.13) | collective-permute-done | bytes 131104 | tf_op jit(solution)/shard_map/ppermute | solution.py:27
  29.7 0.4 image.1.refs_0_.refs_8_.image_ref
  30.1 1.9 %collective-permute-start.17 = (f32[256,128]{1,0:T(8,128)S(1)}, f32[256,128]{1,0:T(8,128)S(1)}, u32[]{:S(2)}, u32[]{:S(2)}) collective-permute-start(f32[256,128]{1,0:T(8,128)S(1)} %image.1.refs_0_.refs_8_.image_ref), channel_id=1, source_target_pairs={{0,1},{1,0},{2,3},{3,2},{4,5},{5,4},{6,7},{7,6},{8,9},{9,8},{10,11... | collective-permute-start | bytes 393224 | tf_op jit(solution)/shard_map/ppermute | solution.py:32
  32.0 2.3 %collective-permute-start.18 = (f32[256,128]{1,0:T(8,128)S(1)}, f32[256,128]{1,0:T(8,128)S(1)}, u32[]{:S(2)}, u32[]{:S(2)}) collective-permute-start(f32[256,128]{1,0:T(8,128)S(1)} %image.1.refs_0_.refs_8_.image_ref), channel_id=1, source_target_pairs={{0,2},{1,3},{2,0},{3,1},{4,6},{5,7},{6,4},{7,5},{8,10},{9,11},{10,... | collective-permute-start | bytes 393224 | tf_op jit(solution)/shard_map/ppermute | solution.py:32
  34.3 0.2 collective-permute-start.19
  34.5 3.2 %collective-permute-done.17.refs_1_ = f32[256,128]{1,0:T(8,128)S(1)} collective-permute-done((f32[256,128]{1,0:T(8,128)S(1)}, f32[256,128]{1,0:T(8,128)S(1)}, u32[]{:S(2)}, u32[]{:S(2)}) %collective-permute-start.17) | collective-permute-done | bytes 131104 | tf_op jit(solution)/shard_map/ppermute | solution.py:32
  37.7 7.2 %collective-permute-done.18.refs_2_ = f32[256,128]{1,0:T(8,128)S(1)} collective-permute-done((f32[256,128]{1,0:T(8,128)S(1)}, f32[256,128]{1,0:T(8,128)S(1)}, u32[]{:S(2)}, u32[]{:S(2)}) %collective-permute-start.18) | collective-permute-done | bytes 131104 | tf_op jit(solution)/shard_map/ppermute | solution.py:32
  44.9 0.4 steps.3.refs_0_
  45.3 0.6 collective-permute-start.20
  45.9 1.0 %collective-permute-start.22 = (f32[256,128]{1,0:T(8,128)S(1)}, f32[256,128]{1,0:T(8,128)S(1)}, u32[]{:S(2)}, u32[]{:S(2)}) collective-permute-start(f32[256,128]{1,0:T(8,128)S(1)} %steps.3.refs_0_), channel_id=1, source_target_pairs={{0,16},{4,20},{8,24},{12,28},{16,0},{20,4},{24,8},{28,12},{1,17},{... | collective-permute-start | bytes 393224 | tf_op jit(solution)/shard_map/ppermute | solution.py:23
  46.9 2.0 %collective-permute-start.24 = (f32[256,128]{1,0:T(8,128)S(1)}, f32[256,128]{1,0:T(8,128)S(1)}, u32[]{:S(2)}, u32[]{:S(2)}) collective-permute-start(f32[256,128]{1,0:T(8,128)S(1)} %steps.3.refs_0_), channel_id=1, source_target_pairs={{0,24},{4,28},{8,16},{12,20},{16,8},{20,12},{24,0},{28,4},{1,25},{... | collective-permute-start | bytes 393224 | tf_op jit(solution)/shard_map/ppermute | solution.py:23
  48.8 1.5 %collective-permute-done.20.refs_1_ = f32[256,128]{1,0:T(8,128)S(1)} collective-permute-done((f32[256,128]{1,0:T(8,128)S(1)}, f32[256,128]{1,0:T(8,128)S(1)}, u32[]{:S(2)}, u32[]{:S(2)}) %collective-permute-start.20) | collective-permute-done | bytes 131104 | tf_op jit(solution)/shard_map/ppermute | solution.py:23
  50.3 0.5 collective-permute-done.22.refs_2_
  50.8 1.9 %collective-permute-done.24.refs_3_ = f32[256,128]{1,0:T(8,128)S(1)} collective-permute-done((f32[256,128]{1,0:T(8,128)S(1)}, f32[256,128]{1,0:T(8,128)S(1)}, u32[]{:S(2)}, u32[]{:S(2)}) %collective-permute-start.24) | collective-permute-done | bytes 131104 | tf_op jit(solution)/shard_map/ppermute | solution.py:23
  52.7 0.5 partial.3.refs_3_
  53.3 0.8 %collective-permute-done.25.refs_2_ = f32[256,128]{1,0:T(8,128)S(1)} collective-permute-done((f32[256,128]{1,0:T(8,128)S(1)}, f32[256,128]{1,0:T(8,128)S(1)}, u32[]{:S(2)}, u32[]{:S(2)}) %collective-permute-start.25) | collective-permute-done | bytes 131104 | tf_op jit(solution)/shard_map/ppermute | solution.py:27
  54.1 0.5 moments.1
  54.5 12.8 %all_to_all.5.parts_ref = f32[32,1,128]{2,1,0:T(1,128)S(1)} all-to-all(f32[32,1,128]{2,1,0:T(1,128)S(1)} %get-tuple-element.52), channel_id=1, replica_groups=mesh['cfg'=8,'tm'=4] {'cfg','tm'}, dimensions={0} | all-to-all | bytes 32768 | tf_op jit(solution)/shard_map/all_to_all | solution.py:251
  67.3 0.9 %finish.1 = (f32[256,128]{1,0:T(8,128)}, f32[256,128]{1,0:T(8,128)}) custom-call(f32[32,1,128]{2,1,0:T(1,128)S(1)} %all_to_all.5.parts_ref, f32[256,128]{1,0:T(8,128)S(1)} %get-tuple-element.30.refs_0_.refs_8_.refs_9_.residual_ref, f32[256,128]{1,0:T(8,128)S(1)} %image.1.refs_0_.refs_8_.image_ref, f32[256,128]{1,0:T(8,128)S(1)} %get-tuple-element.53.second_ref), custom_call_target="tpu_custom_call" | custom-call | tf_op jit(solution)/shard_map/finish/pallas_call | solution.py:36
  (21 shorter events, 0.1 us)
Async XLA Ops:
  1.8 8.9 %collective-permute-start.3 = (f32[64,256]{1,0:T(8,128)S(1)}, f32[64,256]{1,0:T(8,128)S(1)}, u32[]{:S(2)}, u32[]{:S(2)}) collective-permute-start(f32[64,256]{1,0:T(8,128)S(1)} %get-tuple-element.37.refs_0_), channel_id=1, source_target_pairs={{0,8},{4,12},{8,0},{12,4},{16,24},{20,28},{24,16},{28,20},{1,9},{5... | collective-permute-start | bytes 196616 | tf_op jit(solution)/shard_map/ppermute | solution.py:23
  4.8 6.2 %collective-permute-start.4 = (f32[64,256]{1,0:T(8,128)S(1)}, f32[64,256]{1,0:T(8,128)S(1)}, u32[]{:S(2)}, u32[]{:S(2)}) collective-permute-start(f32[64,256]{1,0:T(8,128)S(1)} %get-tuple-element.37.refs_0_), channel_id=1, source_target_pairs={{0,16},{4,20},{8,24},{12,28},{16,0},{20,4},{24,8},{28,12},{1,17},{... | collective-permute-start | bytes 196616 | tf_op jit(solution)/shard_map/ppermute | solution.py:23
  6.3 10.1 %collective-permute-start = (f32[256,128]{1,0:T(8,128)S(1)}, f32[256,128]{1,0:T(8,128)S(1)}, u32[]{:S(2)}, u32[]{:S(2)}) collective-permute-start(f32[256,128]{1,0:T(8,128)S(1)} %get-tuple-element.30.refs_0_.refs_8_.refs_9_.residual_ref), channel_id=1, source_target_pairs={{0,1},{1,0},{2,3},{3,2},{4,5},{5,4},{6,7},{7,6},{8,9},{9,8},{10,11... | collective-permute-start | bytes 393224 | tf_op jit(solution)/shard_map/ppermute | solution.py:32
  7.9 12.4 %collective-permute-start.1 = (f32[256,128]{1,0:T(8,128)S(1)}, f32[256,128]{1,0:T(8,128)S(1)}, u32[]{:S(2)}, u32[]{:S(2)}) collective-permute-start(f32[256,128]{1,0:T(8,128)S(1)} %get-tuple-element.30.refs_0_.refs_8_.refs_9_.residual_ref), channel_id=1, source_target_pairs={{0,2},{1,3},{2,0},{3,1},{4,6},{5,7},{6,4},{7,5},{8,10},{9,11},{10,... | collective-permute-start | bytes 393224 | tf_op jit(solution)/shard_map/ppermute | solution.py:32
  10.5 9.8 %collective-permute-start.2 = (f32[256,128]{1,0:T(8,128)S(1)}, f32[256,128]{1,0:T(8,128)S(1)}, u32[]{:S(2)}, u32[]{:S(2)}) collective-permute-start(f32[256,128]{1,0:T(8,128)S(1)} %get-tuple-element.30.refs_0_.refs_8_.refs_9_.residual_ref), channel_id=1, source_target_pairs={{0,3},{1,2},{2,1},{3,0},{4,7},{5,6},{6,5},{7,4},{8,11},{9,10},{10,... | collective-permute-start | bytes 393224 | tf_op jit(solution)/shard_map/ppermute | solution.py:32
  10.7 5.2 %collective-permute-start.5 = (f32[64,256]{1,0:T(8,128)S(1)}, f32[64,256]{1,0:T(8,128)S(1)}, u32[]{:S(2)}, u32[]{:S(2)}) collective-permute-start(f32[64,256]{1,0:T(8,128)S(1)} %get-tuple-element.37.refs_0_), channel_id=1, source_target_pairs={{0,24},{4,28},{8,16},{12,20},{16,8},{20,12},{24,0},{28,4},{1,25},{... | collective-permute-start | bytes 196616 | tf_op jit(solution)/shard_map/ppermute | solution.py:23
  11.0 4.9 %collective-permute-start.6 = (f32[64,256]{1,0:T(8,128)S(1)}, f32[64,256]{1,0:T(8,128)S(1)}, u32[]{:S(2)}, u32[]{:S(2)}) collective-permute-start(f32[64,256]{1,0:T(8,128)S(1)} %get-tuple-element.37.refs_0_), channel_id=1, source_target_pairs={{0,4},{4,0},{8,12},{12,8},{16,20},{20,16},{24,28},{28,24},{1,5},{5... | collective-permute-start | bytes 196616 | tf_op jit(solution)/shard_map/ppermute | solution.py:27
  15.9 4.4 %collective-permute-start.7 = (f32[64,256]{1,0:T(8,128)S(1)}, f32[64,256]{1,0:T(8,128)S(1)}, u32[]{:S(2)}, u32[]{:S(2)}) collective-permute-start(f32[64,256]{1,0:T(8,128)S(1)} %collective-permute-done.3.refs_1_), channel_id=1, source_target_pairs={{0,4},{4,0},{8,12},{12,8},{16,20},{20,16},{24,28},{28,24},{1,5},{5... | collective-permute-start | bytes 196616 | tf_op jit(solution)/shard_map/ppermute | solution.py:27
  15.9 4.4 %collective-permute-start.8 = (f32[64,256]{1,0:T(8,128)S(1)}, f32[64,256]{1,0:T(8,128)S(1)}, u32[]{:S(2)}, u32[]{:S(2)}) collective-permute-start(f32[64,256]{1,0:T(8,128)S(1)} %collective-permute-done.4.refs_2_), channel_id=1, source_target_pairs={{0,4},{4,0},{8,12},{12,8},{16,20},{20,16},{24,28},{28,24},{1,5},{5... | collective-permute-start | bytes 196616 | tf_op jit(solution)/shard_map/ppermute | solution.py:27
  16.4 3.9 %collective-permute-start.9 = (f32[64,256]{1,0:T(8,128)S(1)}, f32[64,256]{1,0:T(8,128)S(1)}, u32[]{:S(2)}, u32[]{:S(2)}) collective-permute-start(f32[64,256]{1,0:T(8,128)S(1)} %collective-permute-done.5.refs_3_), channel_id=1, source_target_pairs={{0,4},{4,0},{8,12},{12,8},{16,20},{20,16},{24,28},{28,24},{1,5},{5... | collective-permute-start | bytes 196616 | tf_op jit(solution)/shard_map/ppermute | solution.py:27
  16.5 0.7 copy-start.1
  17.2 0.9 %copy-start = (f32[128,512]{1,0:T(8,128)S(1)}, f32[128,512]{1,0:T(8,128)}, u32[]{:S(2)}) copy-start(f32[128,512]{1,0:T(8,128)} %steps_ref.1) | copy-start | bytes 786436
  20.7 6.3 %collective-permute-start.14 = (f32[256,128]{1,0:T(8,128)S(1)}, f32[256,128]{1,0:T(8,128)S(1)}, u32[]{:S(2)}, u32[]{:S(2)}) collective-permute-start(f32[256,128]{1,0:T(8,128)S(1)} %steps.2.refs_8_.refs_0_), channel_id=1, source_target_pairs={{0,24},{4,28},{8,16},{12,20},{16,8},{20,12},{24,0},{28,4},{1,25},{... | collective-permute-start | bytes 393224 | tf_op jit(solution)/shard_map/ppermute | solution.py:23
  21.2 6.2 %collective-permute-start.10 = (f32[256,128]{1,0:T(8,128)S(1)}, f32[256,128]{1,0:T(8,128)S(1)}, u32[]{:S(2)}, u32[]{:S(2)}) collective-permute-start(f32[256,128]{1,0:T(8,128)S(1)} %steps.2.refs_8_.refs_0_), channel_id=1, source_target_pairs={{0,8},{4,12},{8,0},{12,4},{16,24},{20,28},{24,16},{28,20},{1,9},{5... | collective-permute-start | bytes 393224 | tf_op jit(solution)/shard_map/ppermute | solution.py:23
  22.7 5.6 %collective-permute-start.12 = (f32[256,128]{1,0:T(8,128)S(1)}, f32[256,128]{1,0:T(8,128)S(1)}, u32[]{:S(2)}, u32[]{:S(2)}) collective-permute-start(f32[256,128]{1,0:T(8,128)S(1)} %steps.2.refs_8_.refs_0_), channel_id=1, source_target_pairs={{0,16},{4,20},{8,24},{12,28},{16,0},{20,4},{24,8},{28,12},{1,17},{... | collective-permute-start | bytes 393224 | tf_op jit(solution)/shard_map/ppermute | solution.py:23
  24.2 4.1 %collective-permute-start.16 = (f32[256,128]{1,0:T(8,128)S(1)}, f32[256,128]{1,0:T(8,128)S(1)}, u32[]{:S(2)}, u32[]{:S(2)}) collective-permute-start(f32[256,128]{1,0:T(8,128)S(1)} %steps.2.refs_8_.refs_0_), channel_id=1, source_target_pairs={{0,4},{4,0},{8,12},{12,8},{16,20},{20,16},{24,28},{28,24},{1,5},{5... | collective-permute-start | bytes 393224 | tf_op jit(solution)/shard_map/ppermute | solution.py:27
  27.0 1.9 %collective-permute-start.15 = (f32[256,128]{1,0:T(8,128)S(1)}, f32[256,128]{1,0:T(8,128)S(1)}, u32[]{:S(2)}, u32[]{:S(2)}) collective-permute-start(f32[256,128]{1,0:T(8,128)S(1)} %collective-permute-done.14.refs_3_), channel_id=1, source_target_pairs={{0,4},{4,0},{8,12},{12,8},{16,20},{20,16},{24,28},{28,24},{1,5},{5... | collective-permute-start | bytes 393224 | tf_op jit(solution)/shard_map/ppermute | solution.py:27
  27.4 1.4 %collective-permute-start.11 = (f32[256,128]{1,0:T(8,128)S(1)}, f32[256,128]{1,0:T(8,128)S(1)}, u32[]{:S(2)}, u32[]{:S(2)}) collective-permute-start(f32[256,128]{1,0:T(8,128)S(1)} %collective-permute-done.10.refs_1_), channel_id=1, source_target_pairs={{0,4},{4,0},{8,12},{12,8},{16,20},{20,16},{24,28},{28,24},{1,5},{5... | collective-permute-start | bytes 393224 | tf_op jit(solution)/shard_map/ppermute | solution.py:27
  28.3 1.3 %collective-permute-start.13 = (f32[256,128]{1,0:T(8,128)S(1)}, f32[256,128]{1,0:T(8,128)S(1)}, u32[]{:S(2)}, u32[]{:S(2)}) collective-permute-start(f32[256,128]{1,0:T(8,128)S(1)} %collective-permute-done.12.refs_2_), channel_id=1, source_target_pairs={{0,4},{4,0},{8,12},{12,8},{16,20},{20,16},{24,28},{28,24},{1,5},{5... | collective-permute-start | bytes 393224 | tf_op jit(solution)/shard_map/ppermute | solution.py:27
  30.1 7.6 %collective-permute-start.17 = (f32[256,128]{1,0:T(8,128)S(1)}, f32[256,128]{1,0:T(8,128)S(1)}, u32[]{:S(2)}, u32[]{:S(2)}) collective-permute-start(f32[256,128]{1,0:T(8,128)S(1)} %image.1.refs_0_.refs_8_.image_ref), channel_id=1, source_target_pairs={{0,1},{1,0},{2,3},{3,2},{4,5},{5,4},{6,7},{7,6},{8,9},{9,8},{10,11... | collective-permute-start | bytes 393224 | tf_op jit(solution)/shard_map/ppermute | solution.py:32
  32.0 12.9 %collective-permute-start.18 = (f32[256,128]{1,0:T(8,128)S(1)}, f32[256,128]{1,0:T(8,128)S(1)}, u32[]{:S(2)}, u32[]{:S(2)}) collective-permute-start(f32[256,128]{1,0:T(8,128)S(1)} %image.1.refs_0_.refs_8_.image_ref), channel_id=1, source_target_pairs={{0,2},{1,3},{2,0},{3,1},{4,6},{5,7},{6,4},{7,5},{8,10},{9,11},{10,... | collective-permute-start | bytes 393224 | tf_op jit(solution)/shard_map/ppermute | solution.py:32
  34.3 10.6 %collective-permute-start.19 = (f32[256,128]{1,0:T(8,128)S(1)}, f32[256,128]{1,0:T(8,128)S(1)}, u32[]{:S(2)}, u32[]{:S(2)}) collective-permute-start(f32[256,128]{1,0:T(8,128)S(1)} %image.1.refs_0_.refs_8_.image_ref), channel_id=1, source_target_pairs={{0,3},{1,2},{2,1},{3,0},{4,7},{5,6},{6,5},{7,4},{8,11},{9,10},{10,... | collective-permute-start | bytes 393224 | tf_op jit(solution)/shard_map/ppermute | solution.py:32
  45.3 5.0 %collective-permute-start.20 = (f32[256,128]{1,0:T(8,128)S(1)}, f32[256,128]{1,0:T(8,128)S(1)}, u32[]{:S(2)}, u32[]{:S(2)}) collective-permute-start(f32[256,128]{1,0:T(8,128)S(1)} %steps.3.refs_0_), channel_id=1, source_target_pairs={{0,8},{4,12},{8,0},{12,4},{16,24},{20,28},{24,16},{28,20},{1,9},{5... | collective-permute-start | bytes 393224 | tf_op jit(solution)/shard_map/ppermute | solution.py:23
  45.9 5.0 %collective-permute-start.22 = (f32[256,128]{1,0:T(8,128)S(1)}, f32[256,128]{1,0:T(8,128)S(1)}, u32[]{:S(2)}, u32[]{:S(2)}) collective-permute-start(f32[256,128]{1,0:T(8,128)S(1)} %steps.3.refs_0_), channel_id=1, source_target_pairs={{0,16},{4,20},{8,24},{12,28},{16,0},{20,4},{24,8},{28,12},{1,17},{... | collective-permute-start | bytes 393224 | tf_op jit(solution)/shard_map/ppermute | solution.py:23
  46.9 5.9 %collective-permute-start.24 = (f32[256,128]{1,0:T(8,128)S(1)}, f32[256,128]{1,0:T(8,128)S(1)}, u32[]{:S(2)}, u32[]{:S(2)}) collective-permute-start(f32[256,128]{1,0:T(8,128)S(1)} %steps.3.refs_0_), channel_id=1, source_target_pairs={{0,24},{4,28},{8,16},{12,20},{16,8},{20,12},{24,0},{28,4},{1,25},{... | collective-permute-start | bytes 393224 | tf_op jit(solution)/shard_map/ppermute | solution.py:23
  48.8 3.9 %collective-permute-start.26 = (f32[256,128]{1,0:T(8,128)S(1)}, f32[256,128]{1,0:T(8,128)S(1)}, u32[]{:S(2)}, u32[]{:S(2)}) collective-permute-start(f32[256,128]{1,0:T(8,128)S(1)} %steps.3.refs_0_), channel_id=1, source_target_pairs={{0,4},{4,0},{8,12},{12,8},{16,20},{20,16},{24,28},{28,24},{1,5},{5... | collective-permute-start | bytes 393224 | tf_op jit(solution)/shard_map/ppermute | solution.py:27
  50.3 2.9 %collective-permute-start.21 = (f32[256,128]{1,0:T(8,128)S(1)}, f32[256,128]{1,0:T(8,128)S(1)}, u32[]{:S(2)}, u32[]{:S(2)}) collective-permute-start(f32[256,128]{1,0:T(8,128)S(1)} %collective-permute-done.20.refs_1_), channel_id=1, source_target_pairs={{0,4},{4,0},{8,12},{12,8},{16,20},{20,16},{24,28},{28,24},{1,5},{5... | collective-permute-start | bytes 393224 | tf_op jit(solution)/shard_map/ppermute | solution.py:27
  50.8 2.4 %collective-permute-start.23 = (f32[256,128]{1,0:T(8,128)S(1)}, f32[256,128]{1,0:T(8,128)S(1)}, u32[]{:S(2)}, u32[]{:S(2)}) collective-permute-start(f32[256,128]{1,0:T(8,128)S(1)} %collective-permute-done.22.refs_2_), channel_id=1, source_target_pairs={{0,4},{4,0},{8,12},{12,8},{16,20},{20,16},{24,28},{28,24},{1,5},{5... | collective-permute-start | bytes 393224 | tf_op jit(solution)/shard_map/ppermute | solution.py:27
  52.7 1.3 %collective-permute-start.25 = (f32[256,128]{1,0:T(8,128)S(1)}, f32[256,128]{1,0:T(8,128)S(1)}, u32[]{:S(2)}, u32[]{:S(2)}) collective-permute-start(f32[256,128]{1,0:T(8,128)S(1)} %collective-permute-done.24.refs_3_), channel_id=1, source_target_pairs={{0,4},{4,0},{8,12},{12,8},{16,20},{20,16},{24,28},{28,24},{1,5},{5... | collective-permute-start | bytes 393224 | tf_op jit(solution)/shard_map/ppermute | solution.py:27

commit v5 on v3

v5 whole, which is shorter than its diff:
```python
import functools
import math

import jax
import jax.numpy as jnp
from jax import lax
from jax.experimental import pallas as pl
from jax.experimental.pallas import tpu as pltpu
from jax.sharding import PartitionSpec as P

HBM = pl.BlockSpec(memory_space=pltpu.HBM)
ANY = pl.BlockSpec(memory_space=pl.ANY)
VMEM = pl.BlockSpec(memory_space=pltpu.VMEM)
SMEM = pl.BlockSpec(memory_space=pltpu.SMEM)
F32, BF16 = jnp.float32, jnp.bfloat16
LIMIT = 62
LOG2E, LN2 = math.log2(math.e), math.log(2.0)


def partners(axis, offset):
    return [(index, index ^ offset) for index in range(lax.axis_size(axis))]


def far_cfg(block):
    return [block] + [lax.ppermute(block, "cfg", partners("cfg", d)) for d in range(2, lax.axis_size("cfg"), 2)]


def near_cfg(block):
    return lax.ppermute(block, "cfg", partners("cfg", 1))


def offsets_tm(layers):
    return [0] + [d for d in (layers - 1, *range(1, layers - 1)) if d]


def gather_tm(block):
    return [block] + [lax.ppermute(block, "tm", partners("tm", d)) for d in offsets_tm(lax.axis_size("tm"))[1:]]


def call(kernel, name, outs, *args, scalars=0, unread=0, scratch=(), limit=24, space=VMEM, cost=None):
    return pl.pallas_call(
        kernel,
        out_shape=outs,
        in_specs=[SMEM] * scalars + [space] * (len(args) - scalars - unread) + [ANY] * unread,
        cost_estimate=cost,
        out_specs=jax.tree.map(lambda _: VMEM, outs),
        scratch_shapes=list(scratch),
        compiler_params=pltpu.CompilerParams(vmem_limit_bytes=limit * 1024 * 1024),
        name=name,
    )(*args)


def split(value):
    high = value.astype(BF16)
    return high, (value - high.astype(F32)).astype(BF16)


def mul(left, right):
    return jnp.dot(left, right, preferred_element_type=F32)


def mul3(left, right):
    return mul(left[0], right[0]) + (mul(left[0], right[1]) + mul(left[1], right[0]))


def column(row):
    size = min(128, row.shape[1])
    same = lax.broadcasted_iota(jnp.int32, (size, size), 0) == lax.broadcasted_iota(jnp.int32, (size, size), 1)
    return jnp.concatenate(
        [
            jnp.sum(jnp.where(same, row[:, at : at + size], 0.0), axis=1, keepdims=True)
            for at in range(0, row.shape[1], size)
        ],
        axis=0,
    )


def total_of(left, right):
    return jnp.sum(jnp.sum(left * right, axis=0, keepdims=True), axis=1, keepdims=True)


def fetch(pairs, sems):
    copies = [pltpu.make_async_copy(src, dst, sems.at[at]) for at, (src, dst) in enumerate(pairs)]
    for copy in copies:
        copy.start()
    for copy in copies:
        copy.wait()


def begin_kernel(targets_hbm, features_hbm, scales_hbm, mask_hbm, noise_hbm, residual_ref, scaled_ref, *rest):
    flag_ref, ridge_ref, targets_ref, features_ref, scales_ref, mask_ref, sems = rest
    fetch(
        [
            (mask_hbm, mask_ref),
            (targets_hbm, targets_ref),
            (scales_hbm, scales_ref),
            (features_hbm, features_ref),
            (noise_hbm, ridge_ref),
        ],
        sems,
    )
    flag_ref[...] = mask_ref[...].astype(F32)
    residual_ref[...] = column(flag_ref[...]) * targets_ref[...]
    scaled_ref[...] = column(scales_ref[...] * (math.sqrt(3.0) * LOG2E)) * features_ref[...]


def split3(value):
    high, rest = value.astype(BF16), value
    rest = rest - high.astype(F32)
    middle = rest.astype(BF16)
    return high, middle, (rest - middle.astype(F32)).astype(BF16)


def mul_tile(high, low, field):
    width = field.shape[1]
    field_high, field_low = split(field)
    both = mul(high, jnp.concatenate([field_high, field_low], axis=1))
    return both[:, :width] + (both[:, width:] + mul(low, field_high))


def layers_kernel(layer_ref, steps_ref, _, __, high_ref, low_ref):
    width = steps_ref.shape[0]
    for place, offset in enumerate(offsets_tm(steps_ref.shape[1] // width)):
        at = pl.ds(place * width, width)
        high_ref[:, at], low_ref[:, at] = split(
            steps_ref[:, pl.ds(pl.multiple_of((layer_ref[0] ^ offset) * width, width), width)]
        )


def tile_kernel(pair_ref, near_ref, every_ref, mask_ref, noise_ref, _, high_ref, low_ref, flag_ref, ridge_ref):
    flag_ref[...] = column(mask_ref[...])
    ridge_ref[...] = column(noise_ref[...])
    rows, pair = every_ref.shape[2], pair_ref[0]
    pieces = [every_ref.at[pair ^ offset] for offset in range(every_ref.shape[0])]
    left = jnp.transpose(jnp.concatenate([pieces[0][...], near_ref[...]], axis=1))
    left_sq = jnp.sum(left * left, axis=1, keepdims=True)
    high, middle, low = split3(-2.0 * left)
    left = jnp.concatenate([high, high, middle, middle, high, low], axis=1)
    for at, piece in enumerate(pieces):
        right = piece[...]
        right_sq = jnp.sum(right * right, axis=0, keepdims=True)
        high, middle, low = split3(right)
        cross = mul(left, jnp.concatenate([high, middle, high, middle, low, high], axis=0))
        dist2 = jnp.maximum(left_sq + right_sq + cross, 1e-30)
        dist = dist2 * lax.rsqrt(dist2)
        high, low = split((1.0 + LN2 * dist) * jnp.exp2(-dist))
        high_ref[:, pl.ds(at * rows, rows)] = high
        low_ref[:, pl.ds(at * rows, rows)] = low


def mul_t(left, right):
    return lax.dot_general(left, right, (((1,), (1,)), ((), ())), preferred_element_type=F32)


def steps_kernel(*refs):
    pieces, (high_ref, low_ref, out_ref) = refs[:-3], refs[-3:]
    field = split(jnp.concatenate([piece[...] for piece in pieces], axis=1))
    out_ref[...] = mul_t(field[0], high_ref[...]) + (mul_t(field[0], low_ref[...]) + mul_t(field[1], high_ref[...]))


def share(at, pieces, high_ref, low_ref):
    rows = pieces[0].shape[0]
    high, low = (jnp.concatenate([ref[:, pl.ds(place * rows, rows)] for place in at], axis=1) for ref in (high_ref, low_ref))
    return mul_tile(high, low, jnp.concatenate([piece[...] for piece in pieces], axis=0))


def early_kernel(at, *refs):
    pieces, (high_ref, low_ref, out_ref) = refs[:-3], refs[-3:]
    out_ref[...] = share(at, pieces, high_ref, low_ref)


def late_kernel(at, *refs):
    pieces, (early_ref, high_ref, low_ref, own_ref, near_ref) = refs[:-5], refs[-5:]
    mixed = early_ref[...] + share(at, pieces, high_ref, low_ref)
    own_ref[...] = mixed[: own_ref.shape[0]]
    near_ref[...] = mixed[own_ref.shape[0] :]


def image_of(own_ref, near_ref, flag_ref, ridge_ref, field_ref):
    return flag_ref[...] * (own_ref[...] + near_ref[...]) + ridge_ref[...] * field_ref[...]


def image_kernel(*refs):
    refs[-1][...] = image_of(*refs[:-1])


def moments_kernel(*refs):
    image_ref, residual_ref, second_ref, parts_ref = refs[-4:]
    second = image_of(*refs[:-3])
    image, residual = image_ref[...], residual_ref[...]
    second_ref[...] = second
    lane = lax.broadcasted_iota(jnp.int32, parts_ref.shape[1:], 1)
    parts = jnp.zeros(parts_ref.shape[1:], F32)
    for at, pair in enumerate([(residual, residual), (residual, image), (image, image), (image, second)]):
        parts = jnp.where(lane == at, total_of(*pair), parts)
    parts_ref[...] = jnp.broadcast_to(parts[None], parts_ref.shape)


def finish_kernel(parts_ref, residual_ref, image_ref, second_ref, field_ref, left_ref):
    sums = jnp.sum(parts_ref[...], axis=0)
    norm0, first, square, third = (sums[:, at : at + 1] for at in range(4))
    alpha = norm0 / first
    norm1 = norm0 - 2.0 * alpha * first + alpha * alpha * square
    keep = 1.0 + norm1 / norm0
    curv = keep * keep * first - 2.0 * keep * alpha * square + alpha * alpha * third
    beta = norm1 / curv
    residual, image = residual_ref[...], image_ref[...]
    field_ref[...] = (alpha + beta * keep) * residual - (beta * alpha) * image
    left_ref[...] = residual - (alpha + beta * keep) * image + (beta * alpha) * second_ref[...]


def solution(mesh):
    cfg, tm = mesh.shape["cfg"], mesh.shape["tm"]

    def body(targets, features, inv_scales, noise, time_kernel, block_mask):
        rows, width = targets.shape
        count = features.shape[1]
        last = cfg // 2 - 1
        layer, pair = lax.axis_index("tm").reshape(1), (lax.axis_index("cfg") // 2).reshape(1)
        mask = block_mask.reshape(1, rows)

        def shape(*size, kind=F32):
            return jax.ShapeDtypeStruct(size, kind)

        block, row, col = shape(rows, width), pltpu.VMEM((1, rows), F32), shape(rows, 1)
        residual, scaled, flag, ridge = call(
            begin_kernel,
            "begin",
            (pltpu.VMEM((rows, width), F32), pltpu.VMEM((count, rows), F32), row, row),
            targets, features.T, inv_scales.reshape(1, count), mask, noise.reshape(1, rows),
            space=HBM,
            scratch=[
                pltpu.VMEM((rows, width), F32),
                pltpu.VMEM((count, rows), F32),
                pltpu.VMEM((1, count), F32),
                pltpu.VMEM((1, rows), mask.dtype),
                pltpu.SemaphoreType.DMA((5,)),
            ],
            limit=LIMIT,
        )

        half, steps = shape(2 * rows, cfg // 2 * rows, kind=BF16), shape(width, tm * width, kind=BF16)
        groups = [[first + core for first in range(0, cfg, 2)] for core in range(2)]
        every, near = lax.all_gather(scaled, "cfg", axis_index_groups=groups), near_cfg(scaled)
        steps_high, steps_low = call(
            layers_kernel, "layers", (steps, steps), layer, time_kernel, every, near, scalars=1, unread=2
        )
        def over_time(field):
            pieces = gather_tm(field)
            return call(
                steps_kernel, "steps", block, *pieces, steps_high, steps_low
            )

        def over_cfg(pieces, high, low, early):
            partial = call(
                functools.partial(early_kernel, early),
                "early",
                shape(2 * rows, width),
                *[pieces[at] for at in early], high, low,
            )
            own, theirs = call(
                functools.partial(late_kernel, (last,)), "late", (block, block), pieces[last], partial, high, low
            )
            return own, near_cfg(theirs), flag, ridge

        timed = over_time(residual)
        pieces = far_cfg(timed)
        high, low, flag, ridge = call(
            tile_kernel,
            "tile",
            (half, half, col, col),
            pair, near, every, flag, ridge, timed,
            scalars=1,
            unread=1,
        )

        high, pieces[last] = lax.optimization_barrier((high, pieces[last]))
        image = call(image_kernel, "image", block, *over_cfg(pieces, high, low, (0, *range(last - 1, 0, -1))), residual)
        second, sums = call(
            moments_kernel,
            "moments",
            (block, shape(cfg * tm, 1, width)),
            *over_cfg(far_cfg(over_time(image)), high, low, tuple(range(last))), image, residual,
        )
        sums = lax.all_to_all(sums, ("cfg", "tm"), 0, 0, tiled=True)
        return call(finish_kernel, "finish", (block, block), sums, residual, image, second)

    return jax.shard_map(
        body,
        mesh=mesh,
        in_specs=(P("cfg", "tm"), P("cfg", None), P(), P("cfg"), P("tm", None), P("cfg", "tm")),
        out_specs=(P("cfg", "tm"), P("cfg", "tm")),
        check_vma=False,
    )
```

time: 71.1 us -> 66.6 us (0.937)
  blocking collectives: 22.8 us -> 19.8 us
  waiting for transfers between devices: 20.5 us -> 21.8 us
  Pallas kernels: 7.75 us -> 6.63 us
  local copies, waits for them, and re-layouts: 0.86 us -> 0.01 us
    all_to_all x1, blocking collectives: 12.3 us -> 10.6 us  [body(): sums = lax.all_to_all(sums, ('cfg', 'tm'), 0, 0, tiled=True)]
    all_gather x1, blocking collectives: 10.5 us -> 9.13 us  [body(): lax.all_gather(scaled, 'cfg', axis_index_groups=groups)]
    pallas_call x8 -> x12, Pallas kernels: 7.75 us -> 6.63 us  [call(): pl.pallas_call(kernel, out_shape=outs, in_specs=[SMEM] * scalars + [space...]
    ppermute x14 -> x9, waiting for transfers between devices: 10.7 us -> 11.8 us  [the longest x6 9.1 us: far_cfg(): lax.ppermute(block, 'cfg', partners('cfg', d))]
    unnamed x8 -> x2, local copies, waits for them, and re-layouts: 0.86 us -> 0.01 us
    ppermute x14 -> x9, starting transfers between devices: 7.97 us -> 7.25 us  [the longest x6 7.11 us: far_cfg(): lax.ppermute(block, 'cfg', partners('cfg', d))]
  transfers between devices with their start and end apart: 20 -> 15, of which waited for: 11 -> 11; matrix products, arithmetic and copies ran while one was open for 0% -> 0% of each run, Pallas kernels for 4% -> 3%
where the time goes in v5:
time: 66.6 us; the launch traced here: 66.4 us
  waiting for transfers between devices  21.8 us (33%)
  blocking collectives  19.8 us (30%)
  starting transfers between devices  17.5 us (26%)
  Pallas kernels  6.63 us (10%)
  between operations  0.77 us (1%)
    all_to_all x1, blocking collectives, body(): sums = lax.all_to_all(sums, ('cfg', 'tm'), 0, 0, tiled=True)  10.6 us
    ppermute x6, starting transfers between devices, gather_tm(): lax.ppermute(block, 'tm', partners('tm', d))  10.2 us
    ppermute x6, waiting for transfers between devices, gather_tm(): lax.ppermute(block, 'tm', partners('tm', d))  10 us
    all_gather x1, blocking collectives, body(): lax.all_gather(scaled, 'cfg', axis_index_groups=groups)  9.13 us
    ppermute x6, waiting for transfers between devices, far_cfg(): lax.ppermute(block, 'cfg', partners('cfg', d))  9.1 us
    ppermute x6, starting transfers between devices, far_cfg(): lax.ppermute(block, 'cfg', partners('cfg', d))  7.11 us
    pallas_call x12, Pallas kernels, call(): pl.pallas_call(kernel, out_shape=outs, in_specs=[SMEM] * scalars + [space...  6.63 us
    ppermute x3, waiting for transfers between devices, near_cfg(): return lax.ppermute(block, 'cfg', partners('cfg', 1))  2.67 us
  transfers between devices with their start and end apart: 15, of which 11 were waited for; matrix products, arithmetic and copies ran while one was open for 0% of the time, Pallas kernels for 3%

profile of v5, /device:TPU:0, one launch (start us, length us, event | category | flops | bytes accessed | tf_op | source)
XLA Modules:
  0.0 66.4 jit_solution(17459885111115743168)
XLA Ops:
  0.6 0.0 copy-start
  0.6 1.2 %begin.1 = (f32[256,128]{1,0:T(8,128)S(1)}, f32[64,256]{1,0:T(8,128)S(1)}, f32[1,256]{1,0:T(1,128)S(1)}, f32[1,256]{1,0:T(1,128)S(1)}) custom-call(f32[256,128]{1,0:T(8,128)} %targets_hbm.1, f32[64,256]{1,0:T(8,128)} %bitcast.9, f32[1,64]{1,0:T(1,128)} %bitcast.12, s32[1,256]{1,0:T(1,128)} %bitcast.10, f32[1,256]{1,0:T(1,128)} %bitcast.11), custom_call_target="tpu_custom_call" | custom-call | tf_op jit(solution)/shard_map/begin/pallas_call | solution.py:41
  1.9 5.1 %collective-permute-start.1 = (f32[256,128]{1,0:T(8,128)S(1)}, f32[256,128]{1,0:T(8,128)S(1)}, u32[]{:S(2)}, u32[]{:S(2)}) collective-permute-start(f32[256,128]{1,0:T(8,128)S(1)} %get-tuple-element.23.refs_0_.refs_4_.refs_5_.residual_ref), channel_id=1, source_target_pairs={{0,3},{1,2},{2,1},{3,0},{4,7},{5,6},{6,5},{7,4},{8,11},{9,10},{10,... | collective-permute-start | bytes 393224 | tf_op jit(solution)/shard_map/ppermute | solution.py:37
  7.0 0.0 collective-permute-start.2
  7.0 0.6 collective-permute-start.3
  7.6 0.0 collective-permute-start
  7.6 9.1 %all-gather = f32[256,256]{1,0:T(8,128)S(1)} all-gather(f32[64,256]{1,0:T(8,128)S(1)} %get-tuple-element.20), channel_id=2, replica_groups={{0,8,16,24},{4,12,20,28},{1,9,17,25},{5,13,21,29},{2,10,18,26},{6,14,22..., dimensions={0}, use_global_device_ids=true | all-gather | bytes 327680 | tf_op jit(solution)/shard_map/all_gather | solution.py:244
  16.8 0.0 collective-permute-done.__.near_ref
  16.8 0.0 copy-done
  16.8 0.1 layers.1
  16.8 0.0 collective-permute-done.1.refs_1_
  16.9 0.0 collective-permute-done.2.refs_2_
  16.9 1.2 %collective-permute-done.3.refs_3_ = f32[256,128]{1,0:T(8,128)S(1)} collective-permute-done((f32[256,128]{1,0:T(8,128)S(1)}, f32[256,128]{1,0:T(8,128)S(1)}, u32[]{:S(2)}, u32[]{:S(2)}) %collective-permute-start.3) | collective-permute-done | bytes 131104 | tf_op jit(solution)/shard_map/ppermute | solution.py:37
  18.1 0.4 steps.2._.refs_0_
  18.5 2.5 %collective-permute-start.4 = (f32[256,128]{1,0:T(8,128)S(1)}, f32[256,128]{1,0:T(8,128)S(1)}, u32[]{:S(2)}, u32[]{:S(2)}) collective-permute-start(f32[256,128]{1,0:T(8,128)S(1)} %steps.2._.refs_0_), channel_id=1, source_target_pairs={{0,24},{4,28},{8,16},{12,20},{16,8},{20,12},{24,0},{28,4},{1,25},{... | collective-permute-start | bytes 393224 | tf_op jit(solution)/shard_map/ppermute | solution.py:25
  21.0 0.5 collective-permute-start.5
  21.5 0.5 collective-permute-start.6
  22.0 1.6 %tile.1 = (bf16[512,1024]{1,0:T(8,128)(2,1)S(1)}, bf16[512,1024]{1,0:T(8,128)(2,1)S(1)}, f32[256,1]{1,0:T(8,128)S(1)}, f32[256,1]{1,0:T(8,128)S(1)}) custom-call(s32[1]{0:T(128)} %bitcast.pair_ref, f32[64,256]{1,0:T(8,128)S(1)} %collective-permute-done.__.near_ref, f32[4,64,256]{2,1,0:T(8,128)S(1)} %bitcast.8, f32[1,256]{1,0:T(1,128)S(1)} %get-tuple-element.21.mask_ref, ...), custom_call_target="tpu_custom_call" | custom-call | tf_op jit(solution)/shard_map/tile/pallas_call | solution.py:41
  23.6 1.6 %collective-permute-done.4.refs_0_ = f32[256,128]{1,0:T(8,128)S(1)} collective-permute-done((f32[256,128]{1,0:T(8,128)S(1)}, f32[256,128]{1,0:T(8,128)S(1)}, u32[]{:S(2)}, u32[]{:S(2)}) %collective-permute-start.4) | collective-permute-done | bytes 131104 | tf_op jit(solution)/shard_map/ppermute | solution.py:25
  25.2 1.6 %collective-permute-done.5.refs_1_ = f32[256,128]{1,0:T(8,128)S(1)} collective-permute-done((f32[256,128]{1,0:T(8,128)S(1)}, f32[256,128]{1,0:T(8,128)S(1)}, u32[]{:S(2)}, u32[]{:S(2)}) %collective-permute-start.5) | collective-permute-done | bytes 131104 | tf_op jit(solution)/shard_map/ppermute | solution.py:25
  26.8 0.1 collective-permute-done.6.refs_2_
  26.9 0.6 early.2.refs_1_
  27.4 0.3 late.2
  27.8 0.1 collective-permute-start.7
  27.8 1.3 %collective-permute-done.7.refs_1_ = f32[256,128]{1,0:T(8,128)S(1)} collective-permute-done((f32[256,128]{1,0:T(8,128)S(1)}, f32[256,128]{1,0:T(8,128)S(1)}, u32[]{:S(2)}, u32[]{:S(2)}) %collective-permute-start.7) | collective-permute-done | bytes 131104 | tf_op jit(solution)/shard_map/ppermute | solution.py:29
  29.2 0.1 image.1.refs_0_.refs_4_.image_ref
  29.3 2.4 %collective-permute-start.8 = (f32[256,128]{1,0:T(8,128)S(1)}, f32[256,128]{1,0:T(8,128)S(1)}, u32[]{:S(2)}, u32[]{:S(2)}) collective-permute-start(f32[256,128]{1,0:T(8,128)S(1)} %image.1.refs_0_.refs_4_.image_ref), channel_id=1, source_target_pairs={{0,3},{1,2},{2,1},{3,0},{4,7},{5,6},{6,5},{7,4},{8,11},{9,10},{10,... | collective-permute-start | bytes 393224 | tf_op jit(solution)/shard_map/ppermute | solution.py:37
  31.7 0.0 collective-permute-start.9
  31.7 2.0 %collective-permute-start.10 = (f32[256,128]{1,0:T(8,128)S(1)}, f32[256,128]{1,0:T(8,128)S(1)}, u32[]{:S(2)}, u32[]{:S(2)}) collective-permute-start(f32[256,128]{1,0:T(8,128)S(1)} %image.1.refs_0_.refs_4_.image_ref), channel_id=1, source_target_pairs={{0,2},{1,3},{2,0},{3,1},{4,6},{5,7},{6,4},{7,5},{8,10},{9,11},{10,... | collective-permute-start | bytes 393224 | tf_op jit(solution)/shard_map/ppermute | solution.py:37
  33.8 3.9 %collective-permute-done.8.refs_1_ = f32[256,128]{1,0:T(8,128)S(1)} collective-permute-done((f32[256,128]{1,0:T(8,128)S(1)}, f32[256,128]{1,0:T(8,128)S(1)}, u32[]{:S(2)}, u32[]{:S(2)}) %collective-permute-start.8) | collective-permute-done | bytes 131104 | tf_op jit(solution)/shard_map/ppermute | solution.py:37
  37.6 4.7 %collective-permute-done.9.refs_2_ = f32[256,128]{1,0:T(8,128)S(1)} collective-permute-done((f32[256,128]{1,0:T(8,128)S(1)}, f32[256,128]{1,0:T(8,128)S(1)}, u32[]{:S(2)}, u32[]{:S(2)}) %collective-permute-start.9) | collective-permute-done | bytes 131104 | tf_op jit(solution)/shard_map/ppermute | solution.py:37
  42.4 0.2 collective-permute-done.10.refs_3_
  42.6 0.4 steps.3.refs_0_
  43.0 1.5 %collective-permute-start.12 = (f32[256,128]{1,0:T(8,128)S(1)}, f32[256,128]{1,0:T(8,128)S(1)}, u32[]{:S(2)}, u32[]{:S(2)}) collective-permute-start(f32[256,128]{1,0:T(8,128)S(1)} %steps.3.refs_0_), channel_id=1, source_target_pairs={{0,8},{4,12},{8,0},{12,4},{16,24},{20,28},{24,16},{28,20},{1,9},{5... | collective-permute-start | bytes 393224 | tf_op jit(solution)/shard_map/ppermute | solution.py:25
  44.4 0.7 collective-permute-start.13
  45.1 1.4 %collective-permute-start.11 = (f32[256,128]{1,0:T(8,128)S(1)}, f32[256,128]{1,0:T(8,128)S(1)}, u32[]{:S(2)}, u32[]{:S(2)}) collective-permute-start(f32[256,128]{1,0:T(8,128)S(1)} %steps.3.refs_0_), channel_id=1, source_target_pairs={{0,24},{4,28},{8,16},{12,20},{16,8},{20,12},{24,0},{28,4},{1,25},{... | collective-permute-start | bytes 393224 | tf_op jit(solution)/shard_map/ppermute | solution.py:25
  46.5 2.5 %collective-permute-done.12.refs_1_ = f32[256,128]{1,0:T(8,128)S(1)} collective-permute-done((f32[256,128]{1,0:T(8,128)S(1)}, f32[256,128]{1,0:T(8,128)S(1)}, u32[]{:S(2)}, u32[]{:S(2)}) %collective-permute-start.12) | collective-permute-done | bytes 131104 | tf_op jit(solution)/shard_map/ppermute | solution.py:25
  49.0 3.4 %collective-permute-done.13.refs_2_ = f32[256,128]{1,0:T(8,128)S(1)} collective-permute-done((f32[256,128]{1,0:T(8,128)S(1)}, f32[256,128]{1,0:T(8,128)S(1)}, u32[]{:S(2)}, u32[]{:S(2)}) %collective-permute-start.13) | collective-permute-done | bytes 131104 | tf_op jit(solution)/shard_map/ppermute | solution.py:25
  52.4 0.6 early.3.refs_1_
  52.9 0.0 collective-permute-done.11.refs_0_
  52.9 0.3 late.3
  53.3 0.1 collective-permute-start.14
  53.3 1.3 %collective-permute-done.14.refs_1_ = f32[256,128]{1,0:T(8,128)S(1)} collective-permute-done((f32[256,128]{1,0:T(8,128)S(1)}, f32[256,128]{1,0:T(8,128)S(1)}, u32[]{:S(2)}, u32[]{:S(2)}) %collective-permute-start.14) | collective-permute-done | bytes 131104 | tf_op jit(solution)/shard_map/ppermute | solution.py:29
  54.7 0.2 moments.1
  54.9 10.6 %all_to_all.5.parts_ref = f32[32,1,128]{2,1,0:T(1,128)S(1)} all-to-all(f32[32,1,128]{2,1,0:T(1,128)S(1)} %get-tuple-element.36), channel_id=1, replica_groups=mesh['cfg'=8,'tm'=4] {'cfg','tm'}, dimensions={0} | all-to-all | bytes 32768 | tf_op jit(solution)/shard_map/all_to_all | solution.py:285
  65.5 0.9 %finish.1 = (f32[256,128]{1,0:T(8,128)}, f32[256,128]{1,0:T(8,128)}) custom-call(f32[32,1,128]{2,1,0:T(1,128)S(1)} %all_to_all.5.parts_ref, f32[256,128]{1,0:T(8,128)S(1)} %get-tuple-element.23.refs_0_.refs_4_.refs_5_.residual_ref, f32[256,128]{1,0:T(8,128)S(1)} %image.1.refs_0_.refs_4_.image_ref, f32[256,128]{1,0:T(8,128)S(1)} %get-tuple-element.37.second_ref), custom_call_target="tpu_custom_call" | custom-call | tf_op jit(solution)/shard_map/finish/pallas_call | solution.py:41
Async XLA Ops:
  0.6 16.1 %copy-start = (f32[128,512]{1,0:T(8,128)S(1)}, f32[128,512]{1,0:T(8,128)}, u32[]{:S(2)}) copy-start(f32[128,512]{1,0:T(8,128)} %steps_ref.1) | copy-start | bytes 786436
  1.9 15.0 %collective-permute-start.1 = (f32[256,128]{1,0:T(8,128)S(1)}, f32[256,128]{1,0:T(8,128)S(1)}, u32[]{:S(2)}, u32[]{:S(2)}) collective-permute-start(f32[256,128]{1,0:T(8,128)S(1)} %get-tuple-element.23.refs_0_.refs_4_.refs_5_.residual_ref), channel_id=1, source_target_pairs={{0,3},{1,2},{2,1},{3,0},{4,7},{5,6},{6,5},{7,4},{8,11},{9,10},{10,... | collective-permute-start | bytes 393224 | tf_op jit(solution)/shard_map/ppermute | solution.py:37
  7.0 9.9 %collective-permute-start.2 = (f32[256,128]{1,0:T(8,128)S(1)}, f32[256,128]{1,0:T(8,128)S(1)}, u32[]{:S(2)}, u32[]{:S(2)}) collective-permute-start(f32[256,128]{1,0:T(8,128)S(1)} %get-tuple-element.23.refs_0_.refs_4_.refs_5_.residual_ref), channel_id=1, source_target_pairs={{0,1},{1,0},{2,3},{3,2},{4,5},{5,4},{6,7},{7,6},{8,9},{9,8},{10,11... | collective-permute-start | bytes 393224 | tf_op jit(solution)/shard_map/ppermute | solution.py:37
  7.0 11.1 %collective-permute-start.3 = (f32[256,128]{1,0:T(8,128)S(1)}, f32[256,128]{1,0:T(8,128)S(1)}, u32[]{:S(2)}, u32[]{:S(2)}) collective-permute-start(f32[256,128]{1,0:T(8,128)S(1)} %get-tuple-element.23.refs_0_.refs_4_.refs_5_.residual_ref), channel_id=1, source_target_pairs={{0,2},{1,3},{2,0},{3,1},{4,6},{5,7},{6,4},{7,5},{8,10},{9,11},{10,... | collective-permute-start | bytes 393224 | tf_op jit(solution)/shard_map/ppermute | solution.py:37
  7.6 9.1 %collective-permute-start = (f32[64,256]{1,0:T(8,128)S(1)}, f32[64,256]{1,0:T(8,128)S(1)}, u32[]{:S(2)}, u32[]{:S(2)}) collective-permute-start(f32[64,256]{1,0:T(8,128)S(1)} %get-tuple-element.20), channel_id=1, source_target_pairs={{0,4},{4,0},{8,12},{12,8},{16,20},{20,16},{24,28},{28,24},{1,5},{5... | collective-permute-start | bytes 196616 | tf_op jit(solution)/shard_map/ppermute | solution.py:29
  18.5 6.7 %collective-permute-start.4 = (f32[256,128]{1,0:T(8,128)S(1)}, f32[256,128]{1,0:T(8,128)S(1)}, u32[]{:S(2)}, u32[]{:S(2)}) collective-permute-start(f32[256,128]{1,0:T(8,128)S(1)} %steps.2._.refs_0_), channel_id=1, source_target_pairs={{0,24},{4,28},{8,16},{12,20},{16,8},{20,12},{24,0},{28,4},{1,25},{... | collective-permute-start | bytes 393224 | tf_op jit(solution)/shard_map/ppermute | solution.py:25
  21.0 5.8 %collective-permute-start.5 = (f32[256,128]{1,0:T(8,128)S(1)}, f32[256,128]{1,0:T(8,128)S(1)}, u32[]{:S(2)}, u32[]{:S(2)}) collective-permute-start(f32[256,128]{1,0:T(8,128)S(1)} %steps.2._.refs_0_), channel_id=1, source_target_pairs={{0,16},{4,20},{8,24},{12,28},{16,0},{20,4},{24,8},{28,12},{1,17},{... | collective-permute-start | bytes 393224 | tf_op jit(solution)/shard_map/ppermute | solution.py:25
  21.5 5.4 %collective-permute-start.6 = (f32[256,128]{1,0:T(8,128)S(1)}, f32[256,128]{1,0:T(8,128)S(1)}, u32[]{:S(2)}, u32[]{:S(2)}) collective-permute-start(f32[256,128]{1,0:T(8,128)S(1)} %steps.2._.refs_0_), channel_id=1, source_target_pairs={{0,8},{4,12},{8,0},{12,4},{16,24},{20,28},{24,16},{28,20},{1,9},{5... | collective-permute-start | bytes 393224 | tf_op jit(solution)/shard_map/ppermute | solution.py:25
  27.8 1.4 %collective-permute-start.7 = (f32[256,128]{1,0:T(8,128)S(1)}, f32[256,128]{1,0:T(8,128)S(1)}, u32[]{:S(2)}, u32[]{:S(2)}) collective-permute-start(f32[256,128]{1,0:T(8,128)S(1)} %get-tuple-element.31), channel_id=1, source_target_pairs={{0,4},{4,0},{8,12},{12,8},{16,20},{20,16},{24,28},{28,24},{1,5},{5... | collective-permute-start | bytes 393224 | tf_op jit(solution)/shard_map/ppermute | solution.py:29
  29.3 8.3 %collective-permute-start.8 = (f32[256,128]{1,0:T(8,128)S(1)}, f32[256,128]{1,0:T(8,128)S(1)}, u32[]{:S(2)}, u32[]{:S(2)}) collective-permute-start(f32[256,128]{1,0:T(8,128)S(1)} %image.1.refs_0_.refs_4_.image_ref), channel_id=1, source_target_pairs={{0,3},{1,2},{2,1},{3,0},{4,7},{5,6},{6,5},{7,4},{8,11},{9,10},{10,... | collective-permute-start | bytes 393224 | tf_op jit(solution)/shard_map/ppermute | solution.py:37
  31.7 10.6 %collective-permute-start.9 = (f32[256,128]{1,0:T(8,128)S(1)}, f32[256,128]{1,0:T(8,128)S(1)}, u32[]{:S(2)}, u32[]{:S(2)}) collective-permute-start(f32[256,128]{1,0:T(8,128)S(1)} %image.1.refs_0_.refs_4_.image_ref), channel_id=1, source_target_pairs={{0,1},{1,0},{2,3},{3,2},{4,5},{5,4},{6,7},{7,6},{8,9},{9,8},{10,11... | collective-permute-start | bytes 393224 | tf_op jit(solution)/shard_map/ppermute | solution.py:37
  31.7 10.9 %collective-permute-start.10 = (f32[256,128]{1,0:T(8,128)S(1)}, f32[256,128]{1,0:T(8,128)S(1)}, u32[]{:S(2)}, u32[]{:S(2)}) collective-permute-start(f32[256,128]{1,0:T(8,128)S(1)} %image.1.refs_0_.refs_4_.image_ref), channel_id=1, source_target_pairs={{0,2},{1,3},{2,0},{3,1},{4,6},{5,7},{6,4},{7,5},{8,10},{9,11},{10,... | collective-permute-start | bytes 393224 | tf_op jit(solution)/shard_map/ppermute | solution.py:37
  43.0 6.0 %collective-permute-start.12 = (f32[256,128]{1,0:T(8,128)S(1)}, f32[256,128]{1,0:T(8,128)S(1)}, u32[]{:S(2)}, u32[]{:S(2)}) collective-permute-start(f32[256,128]{1,0:T(8,128)S(1)} %steps.3.refs_0_), channel_id=1, source_target_pairs={{0,8},{4,12},{8,0},{12,4},{16,24},{20,28},{24,16},{28,20},{1,9},{5... | collective-permute-start | bytes 393224 | tf_op jit(solution)/shard_map/ppermute | solution.py:25
  44.4 7.9 %collective-permute-start.13 = (f32[256,128]{1,0:T(8,128)S(1)}, f32[256,128]{1,0:T(8,128)S(1)}, u32[]{:S(2)}, u32[]{:S(2)}) collective-permute-start(f32[256,128]{1,0:T(8,128)S(1)} %steps.3.refs_0_), channel_id=1, source_target_pairs={{0,16},{4,20},{8,24},{12,28},{16,0},{20,4},{24,8},{28,12},{1,17},{... | collective-permute-start | bytes 393224 | tf_op jit(solution)/shard_map/ppermute | solution.py:25
  45.1 7.9 %collective-permute-start.11 = (f32[256,128]{1,0:T(8,128)S(1)}, f32[256,128]{1,0:T(8,128)S(1)}, u32[]{:S(2)}, u32[]{:S(2)}) collective-permute-start(f32[256,128]{1,0:T(8,128)S(1)} %steps.3.refs_0_), channel_id=1, source_target_pairs={{0,24},{4,28},{8,16},{12,20},{16,8},{20,12},{24,0},{28,4},{1,25},{... | collective-permute-start | bytes 393224 | tf_op jit(solution)/shard_map/ppermute | solution.py:25
  53.3 1.4 %collective-permute-start.14 = (f32[256,128]{1,0:T(8,128)S(1)}, f32[256,128]{1,0:T(8,128)S(1)}, u32[]{:S(2)}, u32[]{:S(2)}) collective-permute-start(f32[256,128]{1,0:T(8,128)S(1)} %get-tuple-element.35), channel_id=1, source_target_pairs={{0,4},{4,0},{8,12},{12,8},{16,20},{20,16},{24,28},{28,24},{1,5},{5... | collective-permute-start | bytes 393224 | tf_op jit(solution)/shard_map/ppermute | solution.py:29

commit v6 on v5

--- a/solution.py
+++ b/solution.py
@@ -176,12 +176,36 @@
     near_ref[...] = mixed[own_ref.shape[0] :]
 
 
+def rows_share(at, size, pieces, high_ref, low_ref):
+    step = high_ref.shape[1] // len(pieces)
+    high, low = (
+        jnp.concatenate([ref[:, pl.ds(place * step + at, size)] for place in range(len(pieces))], axis=1)
+        for ref in (high_ref, low_ref)
+    )
+    return mul_tile(high, low, jnp.concatenate([piece[...] for piece in pieces], axis=0))
+
+
+def early_rows_kernel(*refs):
+    pieces, (high_ref, low_ref, out_ref) = refs[:-3], refs[-3:]
+    out_ref[...] = rows_share(0, pieces[0].shape[0], pieces, high_ref, low_ref)
+
+
+def late_rows_kernel(*refs):
+    pieces, (early_ref, high_ref, low_ref, own_ref, near_ref) = refs[:-5], refs[-5:]
+    size = pieces[0].shape[0]
+    mixed = early_ref[...] + rows_share(own_ref.shape[0] - size, size, pieces, high_ref, low_ref)
+    own_ref[...] = mixed[: own_ref.shape[0]]
+    near_ref[...] = mixed[own_ref.shape[0] :]
+
+
 def image_of(own_ref, near_ref, flag_ref, ridge_ref, field_ref):
     return flag_ref[...] * (own_ref[...] + near_ref[...]) + ridge_ref[...] * field_ref[...]
 
 
 def image_kernel(*refs):
-    refs[-1][...] = image_of(*refs[:-1])
+    image, size = image_of(*refs[:-3]), refs[-2].shape[0]
+    refs[-3][...] = image
+    refs[-2][...], refs[-1][...] = image[:size], image[size:]
 
 
 def moments_kernel(*refs):
@@ -247,9 +271,7 @@
         )
         def over_time(field):
             pieces = gather_tm(field)
-            return call(
-                steps_kernel, "steps", block, *pieces, steps_high, steps_low
-            )
+            return call(steps_kernel, "steps", shape(*field.shape), *pieces, steps_high, steps_low)
 
         def over_cfg(pieces, high, low, early):
             partial = call(
@@ -275,12 +297,22 @@
         )
 
         high, pieces[last] = lax.optimization_barrier((high, pieces[last]))
-        image = call(image_kernel, "image", block, *over_cfg(pieces, high, low, (0, *range(last - 1, 0, -1))), residual)
+        first = rows * 1 // 2
+        image, one, two = call(
+            image_kernel,
+            "image",
+            (block, shape(first, width), shape(rows - first, width)),
+            *over_cfg(pieces, high, low, (0, *range(last - 1, 0, -1))), residual,
+        )
+
+        ones, twos = far_cfg(over_time(one)), far_cfg(over_time(two))
+        partial = call(early_rows_kernel, "early_rows", shape(2 * rows, width), *ones, high, low)
+        own, theirs = call(late_rows_kernel, "late_rows", (block, block), *twos, partial, high, low)
         second, sums = call(
             moments_kernel,
             "moments",
             (block, shape(cfg * tm, 1, width)),
-            *over_cfg(far_cfg(over_time(image)), high, low, tuple(range(last))), image, residual,
+            own, near_cfg(theirs), flag, ridge, image, residual,
         )
         sums = lax.all_to_all(sums, ("cfg", "tm"), 0, 0, tiled=True)
         return call(finish_kernel, "finish", (block, block), sums, residual, image, second)

time: 66.6 us -> 65.1 us (0.977)
  waiting for transfers between devices: 21.8 us -> 13.1 us
  starting transfers between devices: 17.5 us -> 25.3 us
  blocking collectives: 19.8 us -> 18.8 us
    ppermute x6 -> x9, waiting for transfers between devices: 10 us -> 3.97 us  [gather_tm(): lax.ppermute(block, 'tm', partners('tm', d))]
    ppermute x6 -> x9, starting transfers between devices: 10.2 us -> 14.5 us  [gather_tm(): lax.ppermute(block, 'tm', partners('tm', d))]
    ppermute x6 -> x9, starting transfers between devices: 7.11 us -> 10.7 us  [far_cfg(): lax.ppermute(block, 'cfg', partners('cfg', d))]
    ppermute x6 -> x9, waiting for transfers between devices: 9.1 us -> 6.51 us  [far_cfg(): lax.ppermute(block, 'cfg', partners('cfg', d))]
    all_to_all x1, blocking collectives: 10.6 us -> 9.69 us  [body(): sums = lax.all_to_all(sums, ('cfg', 'tm'), 0, 0, tiled=True)]
    pallas_call x12 -> x13, Pallas kernels: 6.63 us -> 6.78 us  [call(): pl.pallas_call(kernel, out_shape=outs, in_specs=[SMEM] * scalars + [space...]
  transfers between devices with their start and end apart: 15 -> 21, of which waited for: 11 -> 13; matrix products, arithmetic and copies ran while one was open for 0% -> 0% of each run, Pallas kernels for 3% -> 4%
where the time goes in v6:
time: 65.1 us; the launch traced here: 64.9 us
  starting transfers between devices  25.3 us (39%)
  blocking collectives  18.8 us (29%)
  waiting for transfers between devices  13.1 us (20%)
  Pallas kernels  6.78 us (10%)
  between operations  0.78 us (1%)
    ppermute x9, starting transfers between devices, gather_tm(): lax.ppermute(block, 'tm', partners('tm', d))  14.5 us
    ppermute x9, starting transfers between devices, far_cfg(): lax.ppermute(block, 'cfg', partners('cfg', d))  10.7 us
    all_to_all x1, blocking collectives, body(): sums = lax.all_to_all(sums, ('cfg', 'tm'), 0, 0, tiled=True)  9.69 us
    all_gather x1, blocking collectives, body(): lax.all_gather(scaled, 'cfg', axis_index_groups=groups)  9.13 us
    pallas_call x13, Pallas kernels, call(): pl.pallas_call(kernel, out_shape=outs, in_specs=[SMEM] * scalars + [space...  6.78 us
    ppermute x9, waiting for transfers between devices, far_cfg(): lax.ppermute(block, 'cfg', partners('cfg', d))  6.51 us
    ppermute x9, waiting for transfers between devices, gather_tm(): lax.ppermute(block, 'tm', partners('tm', d))  3.97 us
    ppermute x3, waiting for transfers between devices, near_cfg(): return lax.ppermute(block, 'cfg', partners('cfg', 1))  2.67 us
  transfers between devices with their start and end apart: 21, of which 13 were waited for; matrix products, arithmetic and copies ran while one was open for 0% of the time, Pallas kernels for 4%

profile of v6, /device:TPU:0, one launch (start us, length us, event | category | flops | bytes accessed | tf_op | source)
XLA Modules:
  0.0 64.9 jit_solution(4301133775214823349)
XLA Ops:
  0.6 1.2 %begin.1 = (f32[256,128]{1,0:T(8,128)S(1)}, f32[64,256]{1,0:T(8,128)S(1)}, f32[1,256]{1,0:T(1,128)S(1)}, f32[1,256]{1,0:T(1,128)S(1)}) custom-call(f32[256,128]{1,0:T(8,128)} %targets_hbm.1, f32[64,256]{1,0:T(8,128)} %bitcast.9, f32[1,64]{1,0:T(1,128)} %bitcast.12, s32[1,256]{1,0:T(1,128)} %bitcast.10, f32[1,256]{1,0:T(1,128)} %bitcast.11), custom_call_target="tpu_custom_call" | custom-call | tf_op jit(solution)/shard_map/begin/pallas_call | solution.py:41
  1.9 5.1 %collective-permute-start.1 = (f32[256,128]{1,0:T(8,128)S(1)}, f32[256,128]{1,0:T(8,128)S(1)}, u32[]{:S(2)}, u32[]{:S(2)}) collective-permute-start(f32[256,128]{1,0:T(8,128)S(1)} %get-tuple-element.26.refs_0_.refs_4_.refs_5_.residual_ref), channel_id=1, source_target_pairs={{0,3},{1,2},{2,1},{3,0},{4,7},{5,6},{6,5},{7,4},{8,11},{9,10},{10,... | collective-permute-start | bytes 393224 | tf_op jit(solution)/shard_map/ppermute | solution.py:37
  7.0 0.6 collective-permute-start.3
  7.6 9.1 %all-gather = f32[256,256]{1,0:T(8,128)S(1)} all-gather(f32[64,256]{1,0:T(8,128)S(1)} %get-tuple-element.23), channel_id=2, replica_groups={{0,8,16,24},{4,12,20,28},{1,9,17,25},{5,13,21,29},{2,10,18,26},{6,14,22..., dimensions={0}, use_global_device_ids=true | all-gather | bytes 327680 | tf_op jit(solution)/shard_map/all_gather | solution.py:268
  16.8 0.0 collective-permute-done.__.near_ref
  16.8 0.1 layers.1
  16.9 0.0 collective-permute-done.2.refs_2_
  16.9 1.2 %collective-permute-done.3.refs_3_ = f32[256,128]{1,0:T(8,128)S(1)} collective-permute-done((f32[256,128]{1,0:T(8,128)S(1)}, f32[256,128]{1,0:T(8,128)S(1)}, u32[]{:S(2)}, u32[]{:S(2)}) %collective-permute-start.3) | collective-permute-done | bytes 131104 | tf_op jit(solution)/shard_map/ppermute | solution.py:37
  18.1 0.4 steps.3._.refs_0_
  18.5 2.5 %collective-permute-start.4 = (f32[256,128]{1,0:T(8,128)S(1)}, f32[256,128]{1,0:T(8,128)S(1)}, u32[]{:S(2)}, u32[]{:S(2)}) collective-permute-start(f32[256,128]{1,0:T(8,128)S(1)} %steps.3._.refs_0_), channel_id=1, source_target_pairs={{0,24},{4,28},{8,16},{12,20},{16,8},{20,12},{24,0},{28,4},{1,25},{... | collective-permute-start | bytes 393224 | tf_op jit(solution)/shard_map/ppermute | solution.py:25
  21.0 0.5 collective-permute-start.5
  21.5 0.5 collective-permute-start.6
  22.0 1.6 %tile.1 = (bf16[512,1024]{1,0:T(8,128)(2,1)S(1)}, bf16[512,1024]{1,0:T(8,128)(2,1)S(1)}, f32[256,1]{1,0:T(8,128)S(1)}, f32[256,1]{1,0:T(8,128)S(1)}) custom-call(s32[1]{0:T(128)} %bitcast.pair_ref, f32[64,256]{1,0:T(8,128)S(1)} %collective-permute-done.__.near_ref, f32[4,64,256]{2,1,0:T(8,128)S(1)} %bitcast.8, f32[1,256]{1,0:T(1,128)S(1)} %get-tuple-element.24.mask_ref, ...), custom_call_target="tpu_custom_call" | custom-call | tf_op jit(solution)/shard_map/tile/pallas_call | solution.py:41
  23.6 1.6 %collective-permute-done.4.refs_0_ = f32[256,128]{1,0:T(8,128)S(1)} collective-permute-done((f32[256,128]{1,0:T(8,128)S(1)}, f32[256,128]{1,0:T(8,128)S(1)}, u32[]{:S(2)}, u32[]{:S(2)}) %collective-permute-start.4) | collective-permute-done | bytes 131104 | tf_op jit(solution)/shard_map/ppermute | solution.py:25
  25.2 1.6 %collective-permute-done.5.refs_1_ = f32[256,128]{1,0:T(8,128)S(1)} collective-permute-done((f32[256,128]{1,0:T(8,128)S(1)}, f32[256,128]{1,0:T(8,128)S(1)}, u32[]{:S(2)}, u32[]{:S(2)}) %collective-permute-start.5) | collective-permute-done | bytes 131104 | tf_op jit(solution)/shard_map/ppermute | solution.py:25
  26.8 0.1 collective-permute-done.6.refs_2_
  26.9 0.6 early.1.refs_1_
  27.4 0.3 late.1
  27.8 0.1 collective-permute-start.7
  27.8 1.3 %collective-permute-done.7.refs_1_ = f32[256,128]{1,0:T(8,128)S(1)} collective-permute-done((f32[256,128]{1,0:T(8,128)S(1)}, f32[256,128]{1,0:T(8,128)S(1)}, u32[]{:S(2)}, u32[]{:S(2)}) %collective-permute-start.7) | collective-permute-done | bytes 131104 | tf_op jit(solution)/shard_map/ppermute | solution.py:29
  29.2 0.1 image.1
  29.3 2.4 %collective-permute-start.14 = (f32[128,128]{1,0:T(8,128)S(1)}, f32[128,128]{1,0:T(8,128)S(1)}, u32[]{:S(2)}, u32[]{:S(2)}) collective-permute-start(f32[128,128]{1,0:T(8,128)S(1)} %get-tuple-element.38.refs_0_), channel_id=1, source_target_pairs={{0,3},{1,2},{2,1},{3,0},{4,7},{5,6},{6,5},{7,4},{8,11},{9,10},{10,... | collective-permute-start | bytes 196616 | tf_op jit(solution)/shard_map/ppermute | solution.py:37
  31.7 2.0 %collective-permute-start.16 = (f32[128,128]{1,0:T(8,128)S(1)}, f32[128,128]{1,0:T(8,128)S(1)}, u32[]{:S(2)}, u32[]{:S(2)}) collective-permute-start(f32[128,128]{1,0:T(8,128)S(1)} %get-tuple-element.38.refs_0_), channel_id=1, source_target_pairs={{0,2},{1,3},{2,0},{3,1},{4,6},{5,7},{6,4},{7,5},{8,10},{9,11},{10,... | collective-permute-start | bytes 196616 | tf_op jit(solution)/shard_map/ppermute | solution.py:37
  33.8 2.3 %collective-permute-start.8 = (f32[128,128]{1,0:T(8,128)S(1)}, f32[128,128]{1,0:T(8,128)S(1)}, u32[]{:S(2)}, u32[]{:S(2)}) collective-permute-start(f32[128,128]{1,0:T(8,128)S(1)} %get-tuple-element.37.refs_0_), channel_id=1, source_target_pairs={{0,3},{1,2},{2,1},{3,0},{4,7},{5,6},{6,5},{7,4},{8,11},{9,10},{10,... | collective-permute-start | bytes 196616 | tf_op jit(solution)/shard_map/ppermute | solution.py:37
  36.1 0.1 collective-permute-done.14.refs_1_
  36.2 2.0 %collective-permute-start.10 = (f32[128,128]{1,0:T(8,128)S(1)}, f32[128,128]{1,0:T(8,128)S(1)}, u32[]{:S(2)}, u32[]{:S(2)}) collective-permute-start(f32[128,128]{1,0:T(8,128)S(1)} %get-tuple-element.37.refs_0_), channel_id=1, source_target_pairs={{0,2},{1,3},{2,0},{3,1},{4,6},{5,7},{6,4},{7,5},{8,10},{9,11},{10,... | collective-permute-start | bytes 196616 | tf_op jit(solution)/shard_map/ppermute | solution.py:37
  38.2 0.2 collective-permute-done.15.refs_2_
  38.4 2.4 %collective-permute-done.16.refs_3_ = f32[128,128]{1,0:T(8,128)S(1)} collective-permute-done((f32[128,128]{1,0:T(8,128)S(1)}, f32[128,128]{1,0:T(8,128)S(1)}, u32[]{:S(2)}, u32[]{:S(2)}) %collective-permute-start.16) | collective-permute-done | bytes 65568 | tf_op jit(solution)/shard_map/ppermute | solution.py:37
  40.8 0.3 steps.5.refs_0_
  41.1 1.5 %collective-permute-start.17 = (f32[128,128]{1,0:T(8,128)S(1)}, f32[128,128]{1,0:T(8,128)S(1)}, u32[]{:S(2)}, u32[]{:S(2)}) collective-permute-start(f32[128,128]{1,0:T(8,128)S(1)} %steps.5.refs_0_), channel_id=1, source_target_pairs={{0,8},{4,12},{8,0},{12,4},{16,24},{20,28},{24,16},{28,20},{1,9},{5... | collective-permute-start | bytes 196616 | tf_op jit(solution)/shard_map/ppermute | solution.py:25
  42.6 0.6 collective-permute-start.18
  43.2 1.5 %collective-permute-start.19 = (f32[128,128]{1,0:T(8,128)S(1)}, f32[128,128]{1,0:T(8,128)S(1)}, u32[]{:S(2)}, u32[]{:S(2)}) collective-permute-start(f32[128,128]{1,0:T(8,128)S(1)} %steps.5.refs_0_), channel_id=1, source_target_pairs={{0,24},{4,28},{8,16},{12,20},{16,8},{20,12},{24,0},{28,4},{1,25},{... | collective-permute-start | bytes 196616 | tf_op jit(solution)/shard_map/ppermute | solution.py:25
  44.7 0.0 collective-permute-done.9.refs_2_
  44.7 0.3 steps.4.refs_0_
  44.9 1.5 %collective-permute-start.11 = (f32[128,128]{1,0:T(8,128)S(1)}, f32[128,128]{1,0:T(8,128)S(1)}, u32[]{:S(2)}, u32[]{:S(2)}) collective-permute-start(f32[128,128]{1,0:T(8,128)S(1)} %steps.4.refs_0_), channel_id=1, source_target_pairs={{0,8},{4,12},{8,0},{12,4},{16,24},{20,28},{24,16},{28,20},{1,9},{5... | collective-permute-start | bytes 196616 | tf_op jit(solution)/shard_map/ppermute | solution.py:25
  46.4 0.6 collective-permute-start.12
  47.0 1.5 %collective-permute-start.13 = (f32[128,128]{1,0:T(8,128)S(1)}, f32[128,128]{1,0:T(8,128)S(1)}, u32[]{:S(2)}, u32[]{:S(2)}) collective-permute-start(f32[128,128]{1,0:T(8,128)S(1)} %steps.4.refs_0_), channel_id=1, source_target_pairs={{0,24},{4,28},{8,16},{12,20},{16,8},{20,12},{24,0},{28,4},{1,25},{... | collective-permute-start | bytes 196616 | tf_op jit(solution)/shard_map/ppermute | solution.py:25
  48.5 0.3 collective-permute-done.19.refs_3_
  48.8 0.4 early_rows.1.refs_4_
  49.2 0.5 collective-permute-done.11.refs_1_
  49.7 1.0 %collective-permute-done.12.refs_2_ = f32[128,128]{1,0:T(8,128)S(1)} collective-permute-done((f32[128,128]{1,0:T(8,128)S(1)}, f32[128,128]{1,0:T(8,128)S(1)}, u32[]{:S(2)}, u32[]{:S(2)}) %collective-permute-start.12) | collective-permute-done | bytes 65568 | tf_op jit(solution)/shard_map/ppermute | solution.py:25
  50.7 1.5 %collective-permute-done.13.refs_3_ = f32[128,128]{1,0:T(8,128)S(1)} collective-permute-done((f32[128,128]{1,0:T(8,128)S(1)}, f32[128,128]{1,0:T(8,128)S(1)}, u32[]{:S(2)}, u32[]{:S(2)}) %collective-permute-start.13) | collective-permute-done | bytes 65568 | tf_op jit(solution)/shard_map/ppermute | solution.py:25
  52.2 0.4 late_rows.1
  52.7 0.1 collective-permute-start.20
  52.7 1.3 %collective-permute-done.20.refs_1_ = f32[256,128]{1,0:T(8,128)S(1)} collective-permute-done((f32[256,128]{1,0:T(8,128)S(1)}, f32[256,128]{1,0:T(8,128)S(1)}, u32[]{:S(2)}, u32[]{:S(2)}) %collective-permute-start.20) | collective-permute-done | bytes 131104 | tf_op jit(solution)/shard_map/ppermute | solution.py:29
  54.1 0.2 moments.1
  54.3 9.7 %all_to_all.5.parts_ref = f32[32,1,128]{2,1,0:T(1,128)S(1)} all-to-all(f32[32,1,128]{2,1,0:T(1,128)S(1)} %get-tuple-element.42), channel_id=1, replica_groups=mesh['cfg'=8,'tm'=4] {'cfg','tm'}, dimensions={0} | all-to-all | bytes 32768 | tf_op jit(solution)/shard_map/all_to_all | solution.py:317
  64.0 0.9 %finish.1 = (f32[256,128]{1,0:T(8,128)}, f32[256,128]{1,0:T(8,128)}) custom-call(f32[32,1,128]{2,1,0:T(1,128)S(1)} %all_to_all.5.parts_ref, f32[256,128]{1,0:T(8,128)S(1)} %get-tuple-element.26.refs_0_.refs_4_.refs_5_.residual_ref, f32[256,128]{1,0:T(8,128)S(1)} %get-tuple-element.41.refs_4_.image_ref, f32[256,128]{1,0:T(8,128)S(1)} %get-tuple-element.43.second_ref), custom_call_target="tpu_custom_call" | custom-call | tf_op jit(solution)/shard_map/finish/pallas_call | solution.py:41
  (11 shorter events, 0.0 us)
Async XLA Ops:
  0.6 16.1 %copy-start = (f32[128,512]{1,0:T(8,128)S(1)}, f32[128,512]{1,0:T(8,128)}, u32[]{:S(2)}) copy-start(f32[128,512]{1,0:T(8,128)} %steps_ref.1) | copy-start | bytes 786436
  1.9 15.0 %collective-permute-start.1 = (f32[256,128]{1,0:T(8,128)S(1)}, f32[256,128]{1,0:T(8,128)S(1)}, u32[]{:S(2)}, u32[]{:S(2)}) collective-permute-start(f32[256,128]{1,0:T(8,128)S(1)} %get-tuple-element.26.refs_0_.refs_4_.refs_5_.residual_ref), channel_id=1, source_target_pairs={{0,3},{1,2},{2,1},{3,0},{4,7},{5,6},{6,5},{7,4},{8,11},{9,10},{10,... | collective-permute-start | bytes 393224 | tf_op jit(solution)/shard_map/ppermute | solution.py:37
  7.0 9.9 %collective-permute-start.2 = (f32[256,128]{1,0:T(8,128)S(1)}, f32[256,128]{1,0:T(8,128)S(1)}, u32[]{:S(2)}, u32[]{:S(2)}) collective-permute-start(f32[256,128]{1,0:T(8,128)S(1)} %get-tuple-element.26.refs_0_.refs_4_.refs_5_.residual_ref), channel_id=1, source_target_pairs={{0,1},{1,0},{2,3},{3,2},{4,5},{5,4},{6,7},{7,6},{8,9},{9,8},{10,11... | collective-permute-start | bytes 393224 | tf_op jit(solution)/shard_map/ppermute | solution.py:37
  7.0 11.1 %collective-permute-start.3 = (f32[256,128]{1,0:T(8,128)S(1)}, f32[256,128]{1,0:T(8,128)S(1)}, u32[]{:S(2)}, u32[]{:S(2)}) collective-permute-start(f32[256,128]{1,0:T(8,128)S(1)} %get-tuple-element.26.refs_0_.refs_4_.refs_5_.residual_ref), channel_id=1, source_target_pairs={{0,2},{1,3},{2,0},{3,1},{4,6},{5,7},{6,4},{7,5},{8,10},{9,11},{10,... | collective-permute-start | bytes 393224 | tf_op jit(solution)/shard_map/ppermute | solution.py:37
  7.6 9.1 %collective-permute-start = (f32[64,256]{1,0:T(8,128)S(1)}, f32[64,256]{1,0:T(8,128)S(1)}, u32[]{:S(2)}, u32[]{:S(2)}) collective-permute-start(f32[64,256]{1,0:T(8,128)S(1)} %get-tuple-element.23), channel_id=1, source_target_pairs={{0,4},{4,0},{8,12},{12,8},{16,20},{20,16},{24,28},{28,24},{1,5},{5... | collective-permute-start | bytes 196616 | tf_op jit(solution)/shard_map/ppermute | solution.py:29
  18.5 6.7 %collective-permute-start.4 = (f32[256,128]{1,0:T(8,128)S(1)}, f32[256,128]{1,0:T(8,128)S(1)}, u32[]{:S(2)}, u32[]{:S(2)}) collective-permute-start(f32[256,128]{1,0:T(8,128)S(1)} %steps.3._.refs_0_), channel_id=1, source_target_pairs={{0,24},{4,28},{8,16},{12,20},{16,8},{20,12},{24,0},{28,4},{1,25},{... | collective-permute-start | bytes 393224 | tf_op jit(solution)/shard_map/ppermute | solution.py:25
  21.0 5.8 %collective-permute-start.5 = (f32[256,128]{1,0:T(8,128)S(1)}, f32[256,128]{1,0:T(8,128)S(1)}, u32[]{:S(2)}, u32[]{:S(2)}) collective-permute-start(f32[256,128]{1,0:T(8,128)S(1)} %steps.3._.refs_0_), channel_id=1, source_target_pairs={{0,16},{4,20},{8,24},{12,28},{16,0},{20,4},{24,8},{28,12},{1,17},{... | collective-permute-start | bytes 393224 | tf_op jit(solution)/shard_map/ppermute | solution.py:25
  21.5 5.4 %collective-permute-start.6 = (f32[256,128]{1,0:T(8,128)S(1)}, f32[256,128]{1,0:T(8,128)S(1)}, u32[]{:S(2)}, u32[]{:S(2)}) collective-permute-start(f32[256,128]{1,0:T(8,128)S(1)} %steps.3._.refs_0_), channel_id=1, source_target_pairs={{0,8},{4,12},{8,0},{12,4},{16,24},{20,28},{24,16},{28,20},{1,9},{5... | collective-permute-start | bytes 393224 | tf_op jit(solution)/shard_map/ppermute | solution.py:25
  27.8 1.4 %collective-permute-start.7 = (f32[256,128]{1,0:T(8,128)S(1)}, f32[256,128]{1,0:T(8,128)S(1)}, u32[]{:S(2)}, u32[]{:S(2)}) collective-permute-start(f32[256,128]{1,0:T(8,128)S(1)} %get-tuple-element.34), channel_id=1, source_target_pairs={{0,4},{4,0},{8,12},{12,8},{16,20},{20,16},{24,28},{28,24},{1,5},{5... | collective-permute-start | bytes 393224 | tf_op jit(solution)/shard_map/ppermute | solution.py:29
  29.3 6.9 %collective-permute-start.14 = (f32[128,128]{1,0:T(8,128)S(1)}, f32[128,128]{1,0:T(8,128)S(1)}, u32[]{:S(2)}, u32[]{:S(2)}) collective-permute-start(f32[128,128]{1,0:T(8,128)S(1)} %get-tuple-element.38.refs_0_), channel_id=1, source_target_pairs={{0,3},{1,2},{2,1},{3,0},{4,7},{5,6},{6,5},{7,4},{8,11},{9,10},{10,... | collective-permute-start | bytes 196616 | tf_op jit(solution)/shard_map/ppermute | solution.py:37
  31.7 6.7 %collective-permute-start.15 = (f32[128,128]{1,0:T(8,128)S(1)}, f32[128,128]{1,0:T(8,128)S(1)}, u32[]{:S(2)}, u32[]{:S(2)}) collective-permute-start(f32[128,128]{1,0:T(8,128)S(1)} %get-tuple-element.38.refs_0_), channel_id=1, source_target_pairs={{0,1},{1,0},{2,3},{3,2},{4,5},{5,4},{6,7},{7,6},{8,9},{9,8},{10,11... | collective-permute-start | bytes 196616 | tf_op jit(solution)/shard_map/ppermute | solution.py:37
  31.7 9.1 %collective-permute-start.16 = (f32[128,128]{1,0:T(8,128)S(1)}, f32[128,128]{1,0:T(8,128)S(1)}, u32[]{:S(2)}, u32[]{:S(2)}) collective-permute-start(f32[128,128]{1,0:T(8,128)S(1)} %get-tuple-element.38.refs_0_), channel_id=1, source_target_pairs={{0,2},{1,3},{2,0},{3,1},{4,6},{5,7},{6,4},{7,5},{8,10},{9,11},{10,... | collective-permute-start | bytes 196616 | tf_op jit(solution)/shard_map/ppermute | solution.py:37
  33.8 9.4 %collective-permute-start.8 = (f32[128,128]{1,0:T(8,128)S(1)}, f32[128,128]{1,0:T(8,128)S(1)}, u32[]{:S(2)}, u32[]{:S(2)}) collective-permute-start(f32[128,128]{1,0:T(8,128)S(1)} %get-tuple-element.37.refs_0_), channel_id=1, source_target_pairs={{0,3},{1,2},{2,1},{3,0},{4,7},{5,6},{6,5},{7,4},{8,11},{9,10},{10,... | collective-permute-start | bytes 196616 | tf_op jit(solution)/shard_map/ppermute | solution.py:37
  36.1 8.6 %collective-permute-start.9 = (f32[128,128]{1,0:T(8,128)S(1)}, f32[128,128]{1,0:T(8,128)S(1)}, u32[]{:S(2)}, u32[]{:S(2)}) collective-permute-start(f32[128,128]{1,0:T(8,128)S(1)} %get-tuple-element.37.refs_0_), channel_id=1, source_target_pairs={{0,1},{1,0},{2,3},{3,2},{4,5},{5,4},{6,7},{7,6},{8,9},{9,8},{10,11... | collective-permute-start | bytes 196616 | tf_op jit(solution)/shard_map/ppermute | solution.py:37
  36.2 8.5 %collective-permute-start.10 = (f32[128,128]{1,0:T(8,128)S(1)}, f32[128,128]{1,0:T(8,128)S(1)}, u32[]{:S(2)}, u32[]{:S(2)}) collective-permute-start(f32[128,128]{1,0:T(8,128)S(1)} %get-tuple-element.37.refs_0_), channel_id=1, source_target_pairs={{0,2},{1,3},{2,0},{3,1},{4,6},{5,7},{6,4},{7,5},{8,10},{9,11},{10,... | collective-permute-start | bytes 196616 | tf_op jit(solution)/shard_map/ppermute | solution.py:37
  41.1 5.9 %collective-permute-start.17 = (f32[128,128]{1,0:T(8,128)S(1)}, f32[128,128]{1,0:T(8,128)S(1)}, u32[]{:S(2)}, u32[]{:S(2)}) collective-permute-start(f32[128,128]{1,0:T(8,128)S(1)} %steps.5.refs_0_), channel_id=1, source_target_pairs={{0,8},{4,12},{8,0},{12,4},{16,24},{20,28},{24,16},{28,20},{1,9},{5... | collective-permute-start | bytes 196616 | tf_op jit(solution)/shard_map/ppermute | solution.py:25
  42.6 5.9 %collective-permute-start.18 = (f32[128,128]{1,0:T(8,128)S(1)}, f32[128,128]{1,0:T(8,128)S(1)}, u32[]{:S(2)}, u32[]{:S(2)}) collective-permute-start(f32[128,128]{1,0:T(8,128)S(1)} %steps.5.refs_0_), channel_id=1, source_target_pairs={{0,16},{4,20},{8,24},{12,28},{16,0},{20,4},{24,8},{28,12},{1,17},{... | collective-permute-start | bytes 196616 | tf_op jit(solution)/shard_map/ppermute | solution.py:25
  43.2 5.5 %collective-permute-start.19 = (f32[128,128]{1,0:T(8,128)S(1)}, f32[128,128]{1,0:T(8,128)S(1)}, u32[]{:S(2)}, u32[]{:S(2)}) collective-permute-start(f32[128,128]{1,0:T(8,128)S(1)} %steps.5.refs_0_), channel_id=1, source_target_pairs={{0,24},{4,28},{8,16},{12,20},{16,8},{20,12},{24,0},{28,4},{1,25},{... | collective-permute-start | bytes 196616 | tf_op jit(solution)/shard_map/ppermute | solution.py:25
  44.9 4.8 %collective-permute-start.11 = (f32[128,128]{1,0:T(8,128)S(1)}, f32[128,128]{1,0:T(8,128)S(1)}, u32[]{:S(2)}, u32[]{:S(2)}) collective-permute-start(f32[128,128]{1,0:T(8,128)S(1)} %steps.4.refs_0_), channel_id=1, source_target_pairs={{0,8},{4,12},{8,0},{12,4},{16,24},{20,28},{24,16},{28,20},{1,9},{5... | collective-permute-start | bytes 196616 | tf_op jit(solution)/shard_map/ppermute | solution.py:25
  46.4 4.3 %collective-permute-start.12 = (f32[128,128]{1,0:T(8,128)S(1)}, f32[128,128]{1,0:T(8,128)S(1)}, u32[]{:S(2)}, u32[]{:S(2)}) collective-permute-start(f32[128,128]{1,0:T(8,128)S(1)} %steps.4.refs_0_), channel_id=1, source_target_pairs={{0,16},{4,20},{8,24},{12,28},{16,0},{20,4},{24,8},{28,12},{1,17},{... | collective-permute-start | bytes 196616 | tf_op jit(solution)/shard_map/ppermute | solution.py:25
  47.0 5.2 %collective-permute-start.13 = (f32[128,128]{1,0:T(8,128)S(1)}, f32[128,128]{1,0:T(8,128)S(1)}, u32[]{:S(2)}, u32[]{:S(2)}) collective-permute-start(f32[128,128]{1,0:T(8,128)S(1)} %steps.4.refs_0_), channel_id=1, source_target_pairs={{0,24},{4,28},{8,16},{12,20},{16,8},{20,12},{24,0},{28,4},{1,25},{... | collective-permute-start | bytes 196616 | tf_op jit(solution)/shard_map/ppermute | solution.py:25
  52.7 1.4 %collective-permute-start.20 = (f32[256,128]{1,0:T(8,128)S(1)}, f32[256,128]{1,0:T(8,128)S(1)}, u32[]{:S(2)}, u32[]{:S(2)}) collective-permute-start(f32[256,128]{1,0:T(8,128)S(1)} %get-tuple-element.40), channel_id=1, source_target_pairs={{0,4},{4,0},{8,12},{12,8},{16,20},{20,16},{24,28},{28,24},{1,5},{5... | collective-permute-start | bytes 393224 | tf_op jit(solution)/shard_map/ppermute | solution.py:29

commit v7 on v6

--- a/solution.py
+++ b/solution.py
@@ -152,8 +152,9 @@
     return lax.dot_general(left, right, (((1,), (1,)), ((), ())), preferred_element_type=F32)
 
 
-def steps_kernel(*refs):
+def steps_kernel(places, *refs):
     pieces, (high_ref, low_ref, out_ref) = refs[:-3], refs[-3:]
+    pieces = [pieces[places.index(at)] for at in range(len(pieces))]
     field = split(jnp.concatenate([piece[...] for piece in pieces], axis=1))
     out_ref[...] = mul_t(field[0], high_ref[...]) + (mul_t(field[0], low_ref[...]) + mul_t(field[1], high_ref[...]))
 
@@ -191,11 +192,19 @@
 
 
 def late_rows_kernel(*refs):
-    pieces, (early_ref, high_ref, low_ref, own_ref, near_ref) = refs[:-5], refs[-5:]
+    pieces, (early_ref, high_ref, low_ref, ridge_ref, image_ref, image_near_ref, residual_ref) = refs[:-10], refs[-10:-3]
+    own_ref, near_ref, parts_ref = refs[-3:]
     size = pieces[0].shape[0]
     mixed = early_ref[...] + rows_share(own_ref.shape[0] - size, size, pieces, high_ref, low_ref)
-    own_ref[...] = mixed[: own_ref.shape[0]]
-    near_ref[...] = mixed[own_ref.shape[0] :]
+    own, near = mixed[: own_ref.shape[0]], mixed[own_ref.shape[0] :]
+    own_ref[...], near_ref[...] = own, near
+    image, residual = image_ref[...], residual_ref[...]
+    third = total_of(image, own + ridge_ref[...] * image) + total_of(image_near_ref[...], near)
+    lane = lax.broadcasted_iota(jnp.int32, parts_ref.shape[1:], 1)
+    parts = jnp.where(lane == 3, third, jnp.zeros(parts_ref.shape[1:], F32))
+    for at, pair in enumerate([(residual, residual), (residual, image), (image, image)]):
+        parts = jnp.where(lane == at, total_of(*pair), parts)
+    parts_ref[...] = jnp.broadcast_to(parts[None], parts_ref.shape)
 
 
 def image_of(own_ref, near_ref, flag_ref, ridge_ref, field_ref):
@@ -208,19 +217,7 @@
     refs[-2][...], refs[-1][...] = image[:size], image[size:]
 
 
-def moments_kernel(*refs):
-    image_ref, residual_ref, second_ref, parts_ref = refs[-4:]
-    second = image_of(*refs[:-3])
-    image, residual = image_ref[...], residual_ref[...]
-    second_ref[...] = second
-    lane = lax.broadcasted_iota(jnp.int32, parts_ref.shape[1:], 1)
-    parts = jnp.zeros(parts_ref.shape[1:], F32)
-    for at, pair in enumerate([(residual, residual), (residual, image), (image, image), (image, second)]):
-        parts = jnp.where(lane == at, total_of(*pair), parts)
-    parts_ref[...] = jnp.broadcast_to(parts[None], parts_ref.shape)
-
-
-def finish_kernel(parts_ref, residual_ref, image_ref, second_ref, field_ref, left_ref):
+def finish_kernel(parts_ref, residual_ref, own_ref, near_ref, flag_ref, ridge_ref, image_ref, field_ref, left_ref):
     sums = jnp.sum(parts_ref[...], axis=0)
     norm0, first, square, third = (sums[:, at : at + 1] for at in range(4))
     alpha = norm0 / first
@@ -229,8 +226,9 @@
     curv = keep * keep * first - 2.0 * keep * alpha * square + alpha * alpha * third
     beta = norm1 / curv
     residual, image = residual_ref[...], image_ref[...]
+    second = image_of(own_ref, near_ref, flag_ref, ridge_ref, image_ref)
     field_ref[...] = (alpha + beta * keep) * residual - (beta * alpha) * image
-    left_ref[...] = residual - (alpha + beta * keep) * image + (beta * alpha) * second_ref[...]
+    left_ref[...] = residual - (alpha + beta * keep) * image + (beta * alpha) * second
 
 
 def solution(mesh):
@@ -269,9 +267,14 @@
         steps_high, steps_low = call(
             layers_kernel, "layers", (steps, steps), layer, time_kernel, every, near, scalars=1, unread=2
         )
-        def over_time(field):
-            pieces = gather_tm(field)
-            return call(steps_kernel, "steps", shape(*field.shape), *pieces, steps_high, steps_low)
+        def over_time(field, *places):
+            pieces, places = gather_tm(field), places or tuple(range(tm))
+            return call(
+                functools.partial(steps_kernel, places),
+                "steps",
+                shape(*field.shape),
+                *[pieces[at] for at in places], steps_high, steps_low,
+            )
 
         def over_cfg(pieces, high, low, early):
             partial = call(
@@ -305,17 +308,18 @@
             *over_cfg(pieces, high, low, (0, *range(last - 1, 0, -1))), residual,
         )
 
-        ones, twos = far_cfg(over_time(one)), far_cfg(over_time(two))
+        ones, twos = far_cfg(over_time(one)), far_cfg(over_time(two, 0, *range(2, tm), 1))
         partial = call(early_rows_kernel, "early_rows", shape(2 * rows, width), *ones, high, low)
-        own, theirs = call(late_rows_kernel, "late_rows", (block, block), *twos, partial, high, low)
-        second, sums = call(
-            moments_kernel,
-            "moments",
-            (block, shape(cfg * tm, 1, width)),
-            own, near_cfg(theirs), flag, ridge, image, residual,
+        own, theirs, sums = call(
+            late_rows_kernel,
+            "late_rows",
+            (block, block, shape(cfg * tm, 1, width)),
+            *twos, partial, high, low, ridge, image, near_cfg(image), residual,
         )
         sums = lax.all_to_all(sums, ("cfg", "tm"), 0, 0, tiled=True)
-        return call(finish_kernel, "finish", (block, block), sums, residual, image, second)
+        return call(
+            finish_kernel, "finish", (block, block), sums, residual, own, near_cfg(theirs), flag, ridge, image
+        )
 
     return jax.shard_map(
         body,

time: 65.1 us -> 63.7 us (0.978)
  waiting for transfers between devices: 13.1 us -> 11.8 us
    ppermute x3 -> x4, waiting for transfers between devices: 2.67 us -> 1.34 us  [near_cfg(): return lax.ppermute(block, 'cfg', partners('cfg', 1))]
    pallas_call x13 -> x12, Pallas kernels: 6.78 us -> 6.69 us  [call(): pl.pallas_call(kernel, out_shape=outs, in_specs=[SMEM] * scalars + [space...]
  transfers between devices with their start and end apart: 21 -> 22, of which waited for: 13 -> 11; matrix products, arithmetic and copies ran while one was open for 0% -> 0% of each run, Pallas kernels for 4% -> 4%
where the time goes in v7:
time: 63.7 us; the launch traced here: 63.6 us
  starting transfers between devices  25.4 us (40%)
  blocking collectives  18.8 us (30%)
  waiting for transfers between devices  11.8 us (19%)
  Pallas kernels  6.69 us (11%)
  between operations  0.78 us (1%)
    ppermute x9, starting transfers between devices, gather_tm(): lax.ppermute(block, 'tm', partners('tm', d))  14.5 us
    ppermute x9, starting transfers between devices, far_cfg(): lax.ppermute(block, 'cfg', partners('cfg', d))  10.7 us
    all_to_all x1, blocking collectives, body(): sums = lax.all_to_all(sums, ('cfg', 'tm'), 0, 0, tiled=True)  9.71 us
    all_gather x1, blocking collectives, body(): lax.all_gather(scaled, 'cfg', axis_index_groups=groups)  9.13 us
    pallas_call x12, Pallas kernels, call(): pl.pallas_call(kernel, out_shape=outs, in_specs=[SMEM] * scalars + [space...  6.69 us
    ppermute x9, waiting for transfers between devices, far_cfg(): lax.ppermute(block, 'cfg', partners('cfg', d))  6.52 us
    ppermute x9, waiting for transfers between devices, gather_tm(): lax.ppermute(block, 'tm', partners('tm', d))  3.97 us
    ppermute x4, waiting for transfers between devices, near_cfg(): return lax.ppermute(block, 'cfg', partners('cfg', 1))  1.34 us
  transfers between devices with their start and end apart: 22, of which 11 were waited for; matrix products, arithmetic and copies ran while one was open for 0% of the time, Pallas kernels for 4%

profile of v7, /device:TPU:0, one launch (start us, length us, event | category | flops | bytes accessed | tf_op | source)
XLA Modules:
  0.0 63.6 jit_solution(12432228098058902443)
XLA Ops:
  0.6 1.2 %begin.1 = (f32[256,128]{1,0:T(8,128)S(1)}, f32[64,256]{1,0:T(8,128)S(1)}, f32[1,256]{1,0:T(1,128)S(1)}, f32[1,256]{1,0:T(1,128)S(1)}) custom-call(f32[256,128]{1,0:T(8,128)} %targets_hbm.1, f32[64,256]{1,0:T(8,128)} %bitcast.9, f32[1,64]{1,0:T(1,128)} %bitcast.12, s32[1,256]{1,0:T(1,128)} %bitcast.10, f32[1,256]{1,0:T(1,128)} %bitcast.11), custom_call_target="tpu_custom_call" | custom-call | tf_op jit(solution)/shard_map/begin/pallas_call | solution.py:41
  1.9 5.1 %collective-permute-start.1 = (f32[256,128]{1,0:T(8,128)S(1)}, f32[256,128]{1,0:T(8,128)S(1)}, u32[]{:S(2)}, u32[]{:S(2)}) collective-permute-start(f32[256,128]{1,0:T(8,128)S(1)} %get-tuple-element.25.refs_0_.refs_4_.refs_10_.residual_ref), channel_id=1, source_target_pairs={{0,3},{1,2},{2,1},{3,0},{4,7},{5,6},{6,5},{7,4},{8,11},{9,10},{10,... | collective-permute-start | bytes 393224 | tf_op jit(solution)/shard_map/ppermute | solution.py:37
  7.0 0.6 %collective-permute-start.3 = (f32[256,128]{1,0:T(8,128)S(1)}, f32[256,128]{1,0:T(8,128)S(1)}, u32[]{:S(2)}, u32[]{:S(2)}) collective-permute-start(f32[256,128]{1,0:T(8,128)S(1)} %get-tuple-element.25.refs_0_.refs_4_.refs_10_.residual_ref), channel_id=1, source_target_pairs={{0,2},{1,3},{2,0},{3,1},{4,6},{5,7},{6,4},{7,5},{8,10},{9,11},{10,... | collective-permute-start | bytes 393224 | tf_op jit(solution)/shard_map/ppermute | solution.py:37
  7.6 9.1 %all-gather = f32[256,256]{1,0:T(8,128)S(1)} all-gather(f32[64,256]{1,0:T(8,128)S(1)} %get-tuple-element.22), channel_id=2, replica_groups={{0,8,16,24},{4,12,20,28},{1,9,17,25},{5,13,21,29},{2,10,18,26},{6,14,22..., dimensions={0}, use_global_device_ids=true | all-gather | bytes 327680 | tf_op jit(solution)/shard_map/all_gather | solution.py:266
  16.8 0.0 collective-permute-done.__.near_ref
  16.8 0.1 layers.1
  16.9 0.0 collective-permute-done.2.refs_2_
  16.9 1.2 %collective-permute-done.3.refs_3_ = f32[256,128]{1,0:T(8,128)S(1)} collective-permute-done((f32[256,128]{1,0:T(8,128)S(1)}, f32[256,128]{1,0:T(8,128)S(1)}, u32[]{:S(2)}, u32[]{:S(2)}) %collective-permute-start.3) | collective-permute-done | bytes 131104 | tf_op jit(solution)/shard_map/ppermute | solution.py:37
  18.1 0.4 steps.3._.refs_0_
  18.5 2.5 %collective-permute-start.4 = (f32[256,128]{1,0:T(8,128)S(1)}, f32[256,128]{1,0:T(8,128)S(1)}, u32[]{:S(2)}, u32[]{:S(2)}) collective-permute-start(f32[256,128]{1,0:T(8,128)S(1)} %steps.3._.refs_0_), channel_id=1, source_target_pairs={{0,24},{4,28},{8,16},{12,20},{16,8},{20,12},{24,0},{28,4},{1,25},{... | collective-permute-start | bytes 393224 | tf_op jit(solution)/shard_map/ppermute | solution.py:25
  21.0 0.5 collective-permute-start.5
  21.5 0.5 collective-permute-start.6
  22.0 1.6 %tile.1 = (bf16[512,1024]{1,0:T(8,128)(2,1)S(1)}, bf16[512,1024]{1,0:T(8,128)(2,1)S(1)}, f32[256,1]{1,0:T(8,128)S(1)}, f32[256,1]{1,0:T(8,128)S(1)}) custom-call(s32[1]{0:T(128)} %bitcast.pair_ref, f32[64,256]{1,0:T(8,128)S(1)} %collective-permute-done.__.near_ref, f32[4,64,256]{2,1,0:T(8,128)S(1)} %bitcast.8, f32[1,256]{1,0:T(1,128)S(1)} %get-tuple-element.23.mask_ref, ...), custom_call_target="tpu_custom_call" | custom-call | tf_op jit(solution)/shard_map/tile/pallas_call | solution.py:41
  23.6 1.6 %collective-permute-done.4.refs_0_ = f32[256,128]{1,0:T(8,128)S(1)} collective-permute-done((f32[256,128]{1,0:T(8,128)S(1)}, f32[256,128]{1,0:T(8,128)S(1)}, u32[]{:S(2)}, u32[]{:S(2)}) %collective-permute-start.4) | collective-permute-done | bytes 131104 | tf_op jit(solution)/shard_map/ppermute | solution.py:25
  25.2 1.6 %collective-permute-done.5.refs_1_ = f32[256,128]{1,0:T(8,128)S(1)} collective-permute-done((f32[256,128]{1,0:T(8,128)S(1)}, f32[256,128]{1,0:T(8,128)S(1)}, u32[]{:S(2)}, u32[]{:S(2)}) %collective-permute-start.5) | collective-permute-done | bytes 131104 | tf_op jit(solution)/shard_map/ppermute | solution.py:25
  26.8 0.1 collective-permute-done.6.refs_2_
  26.9 0.6 early.1.refs_1_
  27.4 0.3 late.1
  27.8 0.1 collective-permute-start.7
  27.8 1.3 %collective-permute-done.7.refs_1_ = f32[256,128]{1,0:T(8,128)S(1)} collective-permute-done((f32[256,128]{1,0:T(8,128)S(1)}, f32[256,128]{1,0:T(8,128)S(1)}, u32[]{:S(2)}, u32[]{:S(2)}) %collective-permute-start.7) | collective-permute-done | bytes 131104 | tf_op jit(solution)/shard_map/ppermute | solution.py:29
  29.2 0.1 image.1
  29.3 2.4 %collective-permute-start.14 = (f32[128,128]{1,0:T(8,128)S(1)}, f32[128,128]{1,0:T(8,128)S(1)}, u32[]{:S(2)}, u32[]{:S(2)}) collective-permute-start(f32[128,128]{1,0:T(8,128)S(1)} %get-tuple-element.37.refs_0_), channel_id=1, source_target_pairs={{0,3},{1,2},{2,1},{3,0},{4,7},{5,6},{6,5},{7,4},{8,11},{9,10},{10,... | collective-permute-start | bytes 196616 | tf_op jit(solution)/shard_map/ppermute | solution.py:37
  31.7 2.0 %collective-permute-start.16 = (f32[128,128]{1,0:T(8,128)S(1)}, f32[128,128]{1,0:T(8,128)S(1)}, u32[]{:S(2)}, u32[]{:S(2)}) collective-permute-start(f32[128,128]{1,0:T(8,128)S(1)} %get-tuple-element.37.refs_0_), channel_id=1, source_target_pairs={{0,2},{1,3},{2,0},{3,1},{4,6},{5,7},{6,4},{7,5},{8,10},{9,11},{10,... | collective-permute-start | bytes 196616 | tf_op jit(solution)/shard_map/ppermute | solution.py:37
  33.8 2.3 %collective-permute-start.10 = (f32[128,128]{1,0:T(8,128)S(1)}, f32[128,128]{1,0:T(8,128)S(1)}, u32[]{:S(2)}, u32[]{:S(2)}) collective-permute-start(f32[128,128]{1,0:T(8,128)S(1)} %get-tuple-element.36.refs_0_), channel_id=1, source_target_pairs={{0,3},{1,2},{2,1},{3,0},{4,7},{5,6},{6,5},{7,4},{8,11},{9,10},{10,... | collective-permute-start | bytes 196616 | tf_op jit(solution)/shard_map/ppermute | solution.py:37
  36.1 0.1 collective-permute-done.14.refs_1_
  36.2 2.0 %collective-permute-start.9 = (f32[128,128]{1,0:T(8,128)S(1)}, f32[128,128]{1,0:T(8,128)S(1)}, u32[]{:S(2)}, u32[]{:S(2)}) collective-permute-start(f32[128,128]{1,0:T(8,128)S(1)} %get-tuple-element.36.refs_0_), channel_id=1, source_target_pairs={{0,2},{1,3},{2,0},{3,1},{4,6},{5,7},{6,4},{7,5},{8,10},{9,11},{10,... | collective-permute-start | bytes 196616 | tf_op jit(solution)/shard_map/ppermute | solution.py:37
  38.2 0.2 collective-permute-done.15.refs_2_
  38.4 2.4 %collective-permute-done.16.refs_3_ = f32[128,128]{1,0:T(8,128)S(1)} collective-permute-done((f32[128,128]{1,0:T(8,128)S(1)}, f32[128,128]{1,0:T(8,128)S(1)}, u32[]{:S(2)}, u32[]{:S(2)}) %collective-permute-start.16) | collective-permute-done | bytes 65568 | tf_op jit(solution)/shard_map/ppermute | solution.py:37
  40.8 0.3 steps.5.refs_0_
  41.1 1.5 %collective-permute-start.17 = (f32[128,128]{1,0:T(8,128)S(1)}, f32[128,128]{1,0:T(8,128)S(1)}, u32[]{:S(2)}, u32[]{:S(2)}) collective-permute-start(f32[128,128]{1,0:T(8,128)S(1)} %steps.5.refs_0_), channel_id=1, source_target_pairs={{0,8},{4,12},{8,0},{12,4},{16,24},{20,28},{24,16},{28,20},{1,9},{5... | collective-permute-start | bytes 196616 | tf_op jit(solution)/shard_map/ppermute | solution.py:25
  42.6 0.6 %collective-permute-start.18 = (f32[128,128]{1,0:T(8,128)S(1)}, f32[128,128]{1,0:T(8,128)S(1)}, u32[]{:S(2)}, u32[]{:S(2)}) collective-permute-start(f32[128,128]{1,0:T(8,128)S(1)} %steps.5.refs_0_), channel_id=1, source_target_pairs={{0,16},{4,20},{8,24},{12,28},{16,0},{20,4},{24,8},{28,12},{1,17},{... | collective-permute-start | bytes 196616 | tf_op jit(solution)/shard_map/ppermute | solution.py:25
  43.2 1.5 %collective-permute-start.19 = (f32[128,128]{1,0:T(8,128)S(1)}, f32[128,128]{1,0:T(8,128)S(1)}, u32[]{:S(2)}, u32[]{:S(2)}) collective-permute-start(f32[128,128]{1,0:T(8,128)S(1)} %steps.5.refs_0_), channel_id=1, source_target_pairs={{0,24},{4,28},{8,16},{12,20},{16,8},{20,12},{24,0},{28,4},{1,25},{... | collective-permute-start | bytes 196616 | tf_op jit(solution)/shard_map/ppermute | solution.py:25
  44.7 0.0 collective-permute-done.9.refs_2_
  44.7 0.3 steps.4.refs_0_
  45.0 1.5 %collective-permute-start.11 = (f32[128,128]{1,0:T(8,128)S(1)}, f32[128,128]{1,0:T(8,128)S(1)}, u32[]{:S(2)}, u32[]{:S(2)}) collective-permute-start(f32[128,128]{1,0:T(8,128)S(1)} %steps.4.refs_0_), channel_id=1, source_target_pairs={{0,8},{4,12},{8,0},{12,4},{16,24},{20,28},{24,16},{28,20},{1,9},{5... | collective-permute-start | bytes 196616 | tf_op jit(solution)/shard_map/ppermute | solution.py:25
  46.5 0.0 collective-permute-done.17.refs_1_
  46.5 0.6 %collective-permute-start.12 = (f32[128,128]{1,0:T(8,128)S(1)}, f32[128,128]{1,0:T(8,128)S(1)}, u32[]{:S(2)}, u32[]{:S(2)}) collective-permute-start(f32[128,128]{1,0:T(8,128)S(1)} %steps.4.refs_0_), channel_id=1, source_target_pairs={{0,16},{4,20},{8,24},{12,28},{16,0},{20,4},{24,8},{28,12},{1,17},{... | collective-permute-start | bytes 196616 | tf_op jit(solution)/shard_map/ppermute | solution.py:25
  47.1 0.0 collective-permute-done.18.refs_2_
  47.1 1.5 %collective-permute-start.13 = (f32[128,128]{1,0:T(8,128)S(1)}, f32[128,128]{1,0:T(8,128)S(1)}, u32[]{:S(2)}, u32[]{:S(2)}) collective-permute-start(f32[128,128]{1,0:T(8,128)S(1)} %steps.4.refs_0_), channel_id=1, source_target_pairs={{0,24},{4,28},{8,16},{12,20},{16,8},{20,12},{24,0},{28,4},{1,25},{... | collective-permute-start | bytes 196616 | tf_op jit(solution)/shard_map/ppermute | solution.py:25
  48.6 0.0 collective-permute-done.19.refs_3_
  48.6 0.4 early_rows.1.refs_4_
  49.1 0.9 %collective-permute-done.11.refs_1_ = f32[128,128]{1,0:T(8,128)S(1)} collective-permute-done((f32[128,128]{1,0:T(8,128)S(1)}, f32[128,128]{1,0:T(8,128)S(1)}, u32[]{:S(2)}, u32[]{:S(2)}) %collective-permute-start.11) | collective-permute-done | bytes 65568 | tf_op jit(solution)/shard_map/ppermute | solution.py:25
  50.0 1.5 %collective-permute-done.12.refs_2_ = f32[128,128]{1,0:T(8,128)S(1)} collective-permute-done((f32[128,128]{1,0:T(8,128)S(1)}, f32[128,128]{1,0:T(8,128)S(1)}, u32[]{:S(2)}, u32[]{:S(2)}) %collective-permute-start.12) | collective-permute-done | bytes 65568 | tf_op jit(solution)/shard_map/ppermute | solution.py:25
  51.4 0.8 %collective-permute-done.13.refs_3_ = f32[128,128]{1,0:T(8,128)S(1)} collective-permute-done((f32[128,128]{1,0:T(8,128)S(1)}, f32[128,128]{1,0:T(8,128)S(1)}, u32[]{:S(2)}, u32[]{:S(2)}) %collective-permute-start.13) | collective-permute-done | bytes 65568 | tf_op jit(solution)/shard_map/ppermute | solution.py:25
  52.3 0.5 late_rows.1
  52.8 0.1 collective-permute-start.21
  52.9 9.7 %all_to_all.5.parts_ref = f32[32,1,128]{2,1,0:T(1,128)S(1)} all-to-all(f32[32,1,128]{2,1,0:T(1,128)S(1)} %get-tuple-element.39), channel_id=1, replica_groups=mesh['cfg'=8,'tm'=4] {'cfg','tm'}, dimensions={0} | all-to-all | bytes 32768 | tf_op jit(solution)/shard_map/all_to_all | solution.py:319
  62.6 0.9 %finish.1 = (f32[256,128]{1,0:T(8,128)}, f32[256,128]{1,0:T(8,128)}) custom-call(f32[32,1,128]{2,1,0:T(1,128)S(1)} %all_to_all.5.parts_ref, f32[256,128]{1,0:T(8,128)S(1)} %get-tuple-element.25.refs_0_.refs_4_.refs_10_.residual_ref, f32[256,128]{1,0:T(8,128)S(1)} %get-tuple-element.40.own_ref, f32[256,128]{1,0:T(8,128)S(1)} %collective-permute-done.21.near_ref, ...), custom_call_target="tpu_custom_call" | custom-call | tf_op jit(solution)/shard_map/finish/pallas_call | solution.py:41
  (12 shorter events, 0.0 us)
Async XLA Ops:
  0.6 16.1 %copy-start = (f32[128,512]{1,0:T(8,128)S(1)}, f32[128,512]{1,0:T(8,128)}, u32[]{:S(2)}) copy-start(f32[128,512]{1,0:T(8,128)} %steps_ref.1) | copy-start | bytes 786436
  1.9 15.0 %collective-permute-start.1 = (f32[256,128]{1,0:T(8,128)S(1)}, f32[256,128]{1,0:T(8,128)S(1)}, u32[]{:S(2)}, u32[]{:S(2)}) collective-permute-start(f32[256,128]{1,0:T(8,128)S(1)} %get-tuple-element.25.refs_0_.refs_4_.refs_10_.residual_ref), channel_id=1, source_target_pairs={{0,3},{1,2},{2,1},{3,0},{4,7},{5,6},{6,5},{7,4},{8,11},{9,10},{10,... | collective-permute-start | bytes 393224 | tf_op jit(solution)/shard_map/ppermute | solution.py:37
  7.0 9.9 %collective-permute-start.2 = (f32[256,128]{1,0:T(8,128)S(1)}, f32[256,128]{1,0:T(8,128)S(1)}, u32[]{:S(2)}, u32[]{:S(2)}) collective-permute-start(f32[256,128]{1,0:T(8,128)S(1)} %get-tuple-element.25.refs_0_.refs_4_.refs_10_.residual_ref), channel_id=1, source_target_pairs={{0,1},{1,0},{2,3},{3,2},{4,5},{5,4},{6,7},{7,6},{8,9},{9,8},{10,11... | collective-permute-start | bytes 393224 | tf_op jit(solution)/shard_map/ppermute | solution.py:37
  7.0 11.1 %collective-permute-start.3 = (f32[256,128]{1,0:T(8,128)S(1)}, f32[256,128]{1,0:T(8,128)S(1)}, u32[]{:S(2)}, u32[]{:S(2)}) collective-permute-start(f32[256,128]{1,0:T(8,128)S(1)} %get-tuple-element.25.refs_0_.refs_4_.refs_10_.residual_ref), channel_id=1, source_target_pairs={{0,2},{1,3},{2,0},{3,1},{4,6},{5,7},{6,4},{7,5},{8,10},{9,11},{10,... | collective-permute-start | bytes 393224 | tf_op jit(solution)/shard_map/ppermute | solution.py:37
  7.6 9.1 %collective-permute-start = (f32[64,256]{1,0:T(8,128)S(1)}, f32[64,256]{1,0:T(8,128)S(1)}, u32[]{:S(2)}, u32[]{:S(2)}) collective-permute-start(f32[64,256]{1,0:T(8,128)S(1)} %get-tuple-element.22), channel_id=1, source_target_pairs={{0,4},{4,0},{8,12},{12,8},{16,20},{20,16},{24,28},{28,24},{1,5},{5... | collective-permute-start | bytes 196616 | tf_op jit(solution)/shard_map/ppermute | solution.py:29
  18.5 6.7 %collective-permute-start.4 = (f32[256,128]{1,0:T(8,128)S(1)}, f32[256,128]{1,0:T(8,128)S(1)}, u32[]{:S(2)}, u32[]{:S(2)}) collective-permute-start(f32[256,128]{1,0:T(8,128)S(1)} %steps.3._.refs_0_), channel_id=1, source_target_pairs={{0,24},{4,28},{8,16},{12,20},{16,8},{20,12},{24,0},{28,4},{1,25},{... | collective-permute-start | bytes 393224 | tf_op jit(solution)/shard_map/ppermute | solution.py:25
  21.0 5.8 %collective-permute-start.5 = (f32[256,128]{1,0:T(8,128)S(1)}, f32[256,128]{1,0:T(8,128)S(1)}, u32[]{:S(2)}, u32[]{:S(2)}) collective-permute-start(f32[256,128]{1,0:T(8,128)S(1)} %steps.3._.refs_0_), channel_id=1, source_target_pairs={{0,16},{4,20},{8,24},{12,28},{16,0},{20,4},{24,8},{28,12},{1,17},{... | collective-permute-start | bytes 393224 | tf_op jit(solution)/shard_map/ppermute | solution.py:25
  21.5 5.4 %collective-permute-start.6 = (f32[256,128]{1,0:T(8,128)S(1)}, f32[256,128]{1,0:T(8,128)S(1)}, u32[]{:S(2)}, u32[]{:S(2)}) collective-permute-start(f32[256,128]{1,0:T(8,128)S(1)} %steps.3._.refs_0_), channel_id=1, source_target_pairs={{0,8},{4,12},{8,0},{12,4},{16,24},{20,28},{24,16},{28,20},{1,9},{5... | collective-permute-start | bytes 393224 | tf_op jit(solution)/shard_map/ppermute | solution.py:25
  27.8 1.4 %collective-permute-start.7 = (f32[256,128]{1,0:T(8,128)S(1)}, f32[256,128]{1,0:T(8,128)S(1)}, u32[]{:S(2)}, u32[]{:S(2)}) collective-permute-start(f32[256,128]{1,0:T(8,128)S(1)} %get-tuple-element.33), channel_id=1, source_target_pairs={{0,4},{4,0},{8,12},{12,8},{16,20},{20,16},{24,28},{28,24},{1,5},{5... | collective-permute-start | bytes 393224 | tf_op jit(solution)/shard_map/ppermute | solution.py:29
  29.3 6.9 %collective-permute-start.14 = (f32[128,128]{1,0:T(8,128)S(1)}, f32[128,128]{1,0:T(8,128)S(1)}, u32[]{:S(2)}, u32[]{:S(2)}) collective-permute-start(f32[128,128]{1,0:T(8,128)S(1)} %get-tuple-element.37.refs_0_), channel_id=1, source_target_pairs={{0,3},{1,2},{2,1},{3,0},{4,7},{5,6},{6,5},{7,4},{8,11},{9,10},{10,... | collective-permute-start | bytes 196616 | tf_op jit(solution)/shard_map/ppermute | solution.py:37
  31.7 6.7 %collective-permute-start.15 = (f32[128,128]{1,0:T(8,128)S(1)}, f32[128,128]{1,0:T(8,128)S(1)}, u32[]{:S(2)}, u32[]{:S(2)}) collective-permute-start(f32[128,128]{1,0:T(8,128)S(1)} %get-tuple-element.37.refs_0_), channel_id=1, source_target_pairs={{0,1},{1,0},{2,3},{3,2},{4,5},{5,4},{6,7},{7,6},{8,9},{9,8},{10,11... | collective-permute-start | bytes 196616 | tf_op jit(solution)/shard_map/ppermute | solution.py:37
  31.7 9.1 %collective-permute-start.16 = (f32[128,128]{1,0:T(8,128)S(1)}, f32[128,128]{1,0:T(8,128)S(1)}, u32[]{:S(2)}, u32[]{:S(2)}) collective-permute-start(f32[128,128]{1,0:T(8,128)S(1)} %get-tuple-element.37.refs_0_), channel_id=1, source_target_pairs={{0,2},{1,3},{2,0},{3,1},{4,6},{5,7},{6,4},{7,5},{8,10},{9,11},{10,... | collective-permute-start | bytes 196616 | tf_op jit(solution)/shard_map/ppermute | solution.py:37
  33.8 9.4 %collective-permute-start.10 = (f32[128,128]{1,0:T(8,128)S(1)}, f32[128,128]{1,0:T(8,128)S(1)}, u32[]{:S(2)}, u32[]{:S(2)}) collective-permute-start(f32[128,128]{1,0:T(8,128)S(1)} %get-tuple-element.36.refs_0_), channel_id=1, source_target_pairs={{0,3},{1,2},{2,1},{3,0},{4,7},{5,6},{6,5},{7,4},{8,11},{9,10},{10,... | collective-permute-start | bytes 196616 | tf_op jit(solution)/shard_map/ppermute | solution.py:37
  36.1 7.1 %collective-permute-start.8 = (f32[128,128]{1,0:T(8,128)S(1)}, f32[128,128]{1,0:T(8,128)S(1)}, u32[]{:S(2)}, u32[]{:S(2)}) collective-permute-start(f32[128,128]{1,0:T(8,128)S(1)} %get-tuple-element.36.refs_0_), channel_id=1, source_target_pairs={{0,1},{1,0},{2,3},{3,2},{4,5},{5,4},{6,7},{7,6},{8,9},{9,8},{10,11... | collective-permute-start | bytes 196616 | tf_op jit(solution)/shard_map/ppermute | solution.py:37
  36.2 8.6 %collective-permute-start.9 = (f32[128,128]{1,0:T(8,128)S(1)}, f32[128,128]{1,0:T(8,128)S(1)}, u32[]{:S(2)}, u32[]{:S(2)}) collective-permute-start(f32[128,128]{1,0:T(8,128)S(1)} %get-tuple-element.36.refs_0_), channel_id=1, source_target_pairs={{0,2},{1,3},{2,0},{3,1},{4,6},{5,7},{6,4},{7,5},{8,10},{9,11},{10,... | collective-permute-start | bytes 196616 | tf_op jit(solution)/shard_map/ppermute | solution.py:37
  41.1 5.4 %collective-permute-start.17 = (f32[128,128]{1,0:T(8,128)S(1)}, f32[128,128]{1,0:T(8,128)S(1)}, u32[]{:S(2)}, u32[]{:S(2)}) collective-permute-start(f32[128,128]{1,0:T(8,128)S(1)} %steps.5.refs_0_), channel_id=1, source_target_pairs={{0,8},{4,12},{8,0},{12,4},{16,24},{20,28},{24,16},{28,20},{1,9},{5... | collective-permute-start | bytes 196616 | tf_op jit(solution)/shard_map/ppermute | solution.py:25
  42.6 4.5 %collective-permute-start.18 = (f32[128,128]{1,0:T(8,128)S(1)}, f32[128,128]{1,0:T(8,128)S(1)}, u32[]{:S(2)}, u32[]{:S(2)}) collective-permute-start(f32[128,128]{1,0:T(8,128)S(1)} %steps.5.refs_0_), channel_id=1, source_target_pairs={{0,16},{4,20},{8,24},{12,28},{16,0},{20,4},{24,8},{28,12},{1,17},{... | collective-permute-start | bytes 196616 | tf_op jit(solution)/shard_map/ppermute | solution.py:25
  43.2 9.1 %collective-permute-start.20 = (f32[256,128]{1,0:T(8,128)S(1)}, f32[256,128]{1,0:T(8,128)S(1)}, u32[]{:S(2)}, u32[]{:S(2)}) collective-permute-start(f32[256,128]{1,0:T(8,128)S(1)} %get-tuple-element.38.refs_8_.image_ref), channel_id=1, source_target_pairs={{0,4},{4,0},{8,12},{12,8},{16,20},{20,16},{24,28},{28,24},{1,5},{5... | collective-permute-start | bytes 393224 | tf_op jit(solution)/shard_map/ppermute | solution.py:29
  43.2 5.4 %collective-permute-start.19 = (f32[128,128]{1,0:T(8,128)S(1)}, f32[128,128]{1,0:T(8,128)S(1)}, u32[]{:S(2)}, u32[]{:S(2)}) collective-permute-start(f32[128,128]{1,0:T(8,128)S(1)} %steps.5.refs_0_), channel_id=1, source_target_pairs={{0,24},{4,28},{8,16},{12,20},{16,8},{20,12},{24,0},{28,4},{1,25},{... | collective-permute-start | bytes 196616 | tf_op jit(solution)/shard_map/ppermute | solution.py:25
  45.0 4.9 %collective-permute-start.11 = (f32[128,128]{1,0:T(8,128)S(1)}, f32[128,128]{1,0:T(8,128)S(1)}, u32[]{:S(2)}, u32[]{:S(2)}) collective-permute-start(f32[128,128]{1,0:T(8,128)S(1)} %steps.4.refs_0_), channel_id=1, source_target_pairs={{0,8},{4,12},{8,0},{12,4},{16,24},{20,28},{24,16},{28,20},{1,9},{5... | collective-permute-start | bytes 196616 | tf_op jit(solution)/shard_map/ppermute | solution.py:25
  46.5 5.0 %collective-permute-start.12 = (f32[128,128]{1,0:T(8,128)S(1)}, f32[128,128]{1,0:T(8,128)S(1)}, u32[]{:S(2)}, u32[]{:S(2)}) collective-permute-start(f32[128,128]{1,0:T(8,128)S(1)} %steps.4.refs_0_), channel_id=1, source_target_pairs={{0,16},{4,20},{8,24},{12,28},{16,0},{20,4},{24,8},{28,12},{1,17},{... | collective-permute-start | bytes 196616 | tf_op jit(solution)/shard_map/ppermute | solution.py:25
  47.1 5.2 %collective-permute-start.13 = (f32[128,128]{1,0:T(8,128)S(1)}, f32[128,128]{1,0:T(8,128)S(1)}, u32[]{:S(2)}, u32[]{:S(2)}) collective-permute-start(f32[128,128]{1,0:T(8,128)S(1)} %steps.4.refs_0_), channel_id=1, source_target_pairs={{0,24},{4,28},{8,16},{12,20},{16,8},{20,12},{24,0},{28,4},{1,25},{... | collective-permute-start | bytes 196616 | tf_op jit(solution)/shard_map/ppermute | solution.py:25
  52.8 9.8 %collective-permute-start.21 = (f32[256,128]{1,0:T(8,128)S(1)}, f32[256,128]{1,0:T(8,128)S(1)}, u32[]{:S(2)}, u32[]{:S(2)}) collective-permute-start(f32[256,128]{1,0:T(8,128)S(1)} %get-tuple-element.41), channel_id=1, source_target_pairs={{0,4},{4,0},{8,12},{12,8},{16,20},{20,16},{24,28},{28,24},{1,5},{5... | collective-permute-start | bytes 393224 | tf_op jit(solution)/shard_map/ppermute | solution.py:29

commit v8 on v7

--- a/solution.py
+++ b/solution.py
@@ -276,7 +276,7 @@
                 *[pieces[at] for at in places], steps_high, steps_low,
             )
 
-        def over_cfg(pieces, high, low, early):
+        def over_cfg(pieces, high, low, early, late):
             partial = call(
                 functools.partial(early_kernel, early),
                 "early",
@@ -284,11 +284,14 @@
                 *[pieces[at] for at in early], high, low,
             )
             own, theirs = call(
-                functools.partial(late_kernel, (last,)), "late", (block, block), pieces[last], partial, high, low
+                functools.partial(late_kernel, late),
+                "late",
+                (block, block),
+                *[pieces[at] for at in late], partial, high, low,
             )
             return own, near_cfg(theirs), flag, ridge
 
-        timed = over_time(residual)
+        timed = over_time(residual, 0, 1, *range(tm - 1, 1, -1))
         pieces = far_cfg(timed)
         high, low, flag, ridge = call(
             tile_kernel,
@@ -305,7 +308,7 @@
             image_kernel,
             "image",
             (block, shape(first, width), shape(rows - first, width)),
-            *over_cfg(pieces, high, low, (0, *range(last - 1, 0, -1))), residual,
+            *over_cfg(pieces, high, low, (0, last), tuple(range(last - 1, 0, -1))), residual,
         )
 
         ones, twos = far_cfg(over_time(one)), far_cfg(over_time(two, 0, *range(2, tm), 1))

time: 63.7 us -> 63.3 us (level)
  transfers between devices with their start and end apart: 22 -> 22, of which waited for: 11 -> 12; matrix products, arithmetic and copies ran while one was open for 0% -> 0% of each run, Pallas kernels for 4% -> 5%
where the time goes in v8:
time: 63.3 us; the launch traced here: 63.1 us
  starting transfers between devices  25.4 us (40%)
  blocking collectives  18.7 us (30%)
  waiting for transfers between devices  11.6 us (18%)
  Pallas kernels  6.69 us (11%)
  between operations  0.77 us (1%)
    ppermute x9, starting transfers between devices, gather_tm(): lax.ppermute(block, 'tm', partners('tm', d))  14.5 us
    ppermute x9, starting transfers between devices, far_cfg(): lax.ppermute(block, 'cfg', partners('cfg', d))  10.7 us
    all_to_all x1, blocking collectives, body(): sums = lax.all_to_all(sums, ('cfg', 'tm'), 0, 0, tiled=True)  9.53 us
    all_gather x1, blocking collectives, body(): lax.all_gather(scaled, 'cfg', axis_index_groups=groups)  9.13 us
    pallas_call x12, Pallas kernels, call(): pl.pallas_call(kernel, out_shape=outs, in_specs=[SMEM] * scalars + [space...  6.69 us
    ppermute x9, waiting for transfers between devices, far_cfg(): lax.ppermute(block, 'cfg', partners('cfg', d))  6.24 us
    ppermute x9, waiting for transfers between devices, gather_tm(): lax.ppermute(block, 'tm', partners('tm', d))  3.99 us
    ppermute x4, waiting for transfers between devices, near_cfg(): return lax.ppermute(block, 'cfg', partners('cfg', 1))  1.34 us
  transfers between devices with their start and end apart: 22, of which 12 were waited for; matrix products, arithmetic and copies ran while one was open for 0% of the time, Pallas kernels for 5%

profile of v8, /device:TPU:0, one launch (start us, length us, event | category | flops | bytes accessed | tf_op | source)
XLA Modules:
  0.0 63.1 jit_solution(8673257584829169153)
XLA Ops:
  0.6 1.2 %begin.1 = (f32[256,128]{1,0:T(8,128)S(1)}, f32[64,256]{1,0:T(8,128)S(1)}, f32[1,256]{1,0:T(1,128)S(1)}, f32[1,256]{1,0:T(1,128)S(1)}) custom-call(f32[256,128]{1,0:T(8,128)} %targets_hbm.1, f32[64,256]{1,0:T(8,128)} %bitcast.9, f32[1,64]{1,0:T(1,128)} %bitcast.12, s32[1,256]{1,0:T(1,128)} %bitcast.10, f32[1,256]{1,0:T(1,128)} %bitcast.11), custom_call_target="tpu_custom_call" | custom-call | tf_op jit(solution)/shard_map/begin/pallas_call | solution.py:41
  1.9 5.1 %collective-permute-start = (f32[256,128]{1,0:T(8,128)S(1)}, f32[256,128]{1,0:T(8,128)S(1)}, u32[]{:S(2)}, u32[]{:S(2)}) collective-permute-start(f32[256,128]{1,0:T(8,128)S(1)} %get-tuple-element.22.refs_0_.refs_4_.refs_10_.residual_ref), channel_id=1, source_target_pairs={{0,3},{1,2},{2,1},{3,0},{4,7},{5,6},{6,5},{7,4},{8,11},{9,10},{10,... | collective-permute-start | bytes 393224 | tf_op jit(solution)/shard_map/ppermute | solution.py:37
  7.0 0.6 %collective-permute-start.2 = (f32[256,128]{1,0:T(8,128)S(1)}, f32[256,128]{1,0:T(8,128)S(1)}, u32[]{:S(2)}, u32[]{:S(2)}) collective-permute-start(f32[256,128]{1,0:T(8,128)S(1)} %get-tuple-element.22.refs_0_.refs_4_.refs_10_.residual_ref), channel_id=1, source_target_pairs={{0,1},{1,0},{2,3},{3,2},{4,5},{5,4},{6,7},{7,6},{8,9},{9,8},{10,11... | collective-permute-start | bytes 393224 | tf_op jit(solution)/shard_map/ppermute | solution.py:37
  7.6 9.1 %all-gather = f32[256,256]{1,0:T(8,128)S(1)} all-gather(f32[64,256]{1,0:T(8,128)S(1)} %get-tuple-element.23), channel_id=2, replica_groups={{0,8,16,24},{4,12,20,28},{1,9,17,25},{5,13,21,29},{2,10,18,26},{6,14,22..., dimensions={0}, use_global_device_ids=true | all-gather | bytes 327680 | tf_op jit(solution)/shard_map/all_gather | solution.py:266
  16.8 0.0 collective-permute-done.3.__.near_ref
  16.8 0.1 layers.1
  16.9 1.2 %collective-permute-done.1.refs_2_ = f32[256,128]{1,0:T(8,128)S(1)} collective-permute-done((f32[256,128]{1,0:T(8,128)S(1)}, f32[256,128]{1,0:T(8,128)S(1)}, u32[]{:S(2)}, u32[]{:S(2)}) %collective-permute-start.1) | collective-permute-done | bytes 131104 | tf_op jit(solution)/shard_map/ppermute | solution.py:37
  18.1 0.4 steps.3._.refs_0_
  18.4 2.5 %collective-permute-start.6 = (f32[256,128]{1,0:T(8,128)S(1)}, f32[256,128]{1,0:T(8,128)S(1)}, u32[]{:S(2)}, u32[]{:S(2)}) collective-permute-start(f32[256,128]{1,0:T(8,128)S(1)} %steps.3._.refs_0_), channel_id=1, source_target_pairs={{0,24},{4,28},{8,16},{12,20},{16,8},{20,12},{24,0},{28,4},{1,25},{... | collective-permute-start | bytes 393224 | tf_op jit(solution)/shard_map/ppermute | solution.py:25
  21.0 0.5 collective-permute-start.4
  21.5 0.5 collective-permute-start.5
  22.0 1.6 %tile.1 = (bf16[512,1024]{1,0:T(8,128)(2,1)S(1)}, bf16[512,1024]{1,0:T(8,128)(2,1)S(1)}, f32[256,1]{1,0:T(8,128)S(1)}, f32[256,1]{1,0:T(8,128)S(1)}) custom-call(s32[1]{0:T(128)} %bitcast.6.pair_ref, f32[64,256]{1,0:T(8,128)S(1)} %collective-permute-done.3.__.near_ref, f32[4,64,256]{2,1,0:T(8,128)S(1)} %bitcast.8, f32[1,256]{1,0:T(1,128)S(1)} %get-tuple-element.26.mask_ref, ...), custom_call_target="tpu_custom_call" | custom-call | tf_op jit(solution)/shard_map/tile/pallas_call | solution.py:41
  23.6 1.6 %collective-permute-done.6.refs_1_ = f32[256,128]{1,0:T(8,128)S(1)} collective-permute-done((f32[256,128]{1,0:T(8,128)S(1)}, f32[256,128]{1,0:T(8,128)S(1)}, u32[]{:S(2)}, u32[]{:S(2)}) %collective-permute-start.6) | collective-permute-done | bytes 131104 | tf_op jit(solution)/shard_map/ppermute | solution.py:25
  25.2 0.4 early.1.refs_2_
  25.7 1.1 %collective-permute-done.4.refs_0_ = f32[256,128]{1,0:T(8,128)S(1)} collective-permute-done((f32[256,128]{1,0:T(8,128)S(1)}, f32[256,128]{1,0:T(8,128)S(1)}, u32[]{:S(2)}, u32[]{:S(2)}) %collective-permute-start.4) | collective-permute-done | bytes 131104 | tf_op jit(solution)/shard_map/ppermute | solution.py:25
  26.8 0.1 collective-permute-done.5.refs_1_
  26.9 0.4 late.1
  27.3 0.1 collective-permute-start.7
  27.4 1.3 %collective-permute-done.7.refs_1_ = f32[256,128]{1,0:T(8,128)S(1)} collective-permute-done((f32[256,128]{1,0:T(8,128)S(1)}, f32[256,128]{1,0:T(8,128)S(1)}, u32[]{:S(2)}, u32[]{:S(2)}) %collective-permute-start.7) | collective-permute-done | bytes 131104 | tf_op jit(solution)/shard_map/ppermute | solution.py:29
  28.7 0.1 image.1
  28.9 2.4 %collective-permute-start.14 = (f32[128,128]{1,0:T(8,128)S(1)}, f32[128,128]{1,0:T(8,128)S(1)}, u32[]{:S(2)}, u32[]{:S(2)}) collective-permute-start(f32[128,128]{1,0:T(8,128)S(1)} %get-tuple-element.37.refs_0_), channel_id=1, source_target_pairs={{0,3},{1,2},{2,1},{3,0},{4,7},{5,6},{6,5},{7,4},{8,11},{9,10},{10,... | collective-permute-start | bytes 196616 | tf_op jit(solution)/shard_map/ppermute | solution.py:37
  31.3 0.0 collective-permute-start.15
  31.3 2.0 %collective-permute-start.16 = (f32[128,128]{1,0:T(8,128)S(1)}, f32[128,128]{1,0:T(8,128)S(1)}, u32[]{:S(2)}, u32[]{:S(2)}) collective-permute-start(f32[128,128]{1,0:T(8,128)S(1)} %get-tuple-element.37.refs_0_), channel_id=1, source_target_pairs={{0,2},{1,3},{2,0},{3,1},{4,6},{5,7},{6,4},{7,5},{8,10},{9,11},{10,... | collective-permute-start | bytes 196616 | tf_op jit(solution)/shard_map/ppermute | solution.py:37
  33.3 2.3 %collective-permute-start.10 = (f32[128,128]{1,0:T(8,128)S(1)}, f32[128,128]{1,0:T(8,128)S(1)}, u32[]{:S(2)}, u32[]{:S(2)}) collective-permute-start(f32[128,128]{1,0:T(8,128)S(1)} %get-tuple-element.36.refs_0_), channel_id=1, source_target_pairs={{0,3},{1,2},{2,1},{3,0},{4,7},{5,6},{6,5},{7,4},{8,11},{9,10},{10,... | collective-permute-start | bytes 196616 | tf_op jit(solution)/shard_map/ppermute | solution.py:37
  35.7 0.0 collective-permute-start.8
  35.7 0.1 collective-permute-done.14.refs_1_
  35.7 2.0 %collective-permute-start.9 = (f32[128,128]{1,0:T(8,128)S(1)}, f32[128,128]{1,0:T(8,128)S(1)}, u32[]{:S(2)}, u32[]{:S(2)}) collective-permute-start(f32[128,128]{1,0:T(8,128)S(1)} %get-tuple-element.36.refs_0_), channel_id=1, source_target_pairs={{0,2},{1,3},{2,0},{3,1},{4,6},{5,7},{6,4},{7,5},{8,10},{9,11},{10,... | collective-permute-start | bytes 196616 | tf_op jit(solution)/shard_map/ppermute | solution.py:37
  37.7 0.2 collective-permute-done.15.refs_2_
  38.0 2.4 %collective-permute-done.16.refs_3_ = f32[128,128]{1,0:T(8,128)S(1)} collective-permute-done((f32[128,128]{1,0:T(8,128)S(1)}, f32[128,128]{1,0:T(8,128)S(1)}, u32[]{:S(2)}, u32[]{:S(2)}) %collective-permute-start.16) | collective-permute-done | bytes 65568 | tf_op jit(solution)/shard_map/ppermute | solution.py:37
  40.4 0.3 steps.5.refs_0_
  40.7 1.5 %collective-permute-start.17 = (f32[128,128]{1,0:T(8,128)S(1)}, f32[128,128]{1,0:T(8,128)S(1)}, u32[]{:S(2)}, u32[]{:S(2)}) collective-permute-start(f32[128,128]{1,0:T(8,128)S(1)} %steps.5.refs_0_), channel_id=1, source_target_pairs={{0,8},{4,12},{8,0},{12,4},{16,24},{20,28},{24,16},{28,20},{1,9},{5... | collective-permute-start | bytes 196616 | tf_op jit(solution)/shard_map/ppermute | solution.py:25
  42.2 0.8 %collective-permute-start.18 = (f32[128,128]{1,0:T(8,128)S(1)}, f32[128,128]{1,0:T(8,128)S(1)}, u32[]{:S(2)}, u32[]{:S(2)}) collective-permute-start(f32[128,128]{1,0:T(8,128)S(1)} %steps.5.refs_0_), channel_id=1, source_target_pairs={{0,16},{4,20},{8,24},{12,28},{16,0},{20,4},{24,8},{28,12},{1,17},{... | collective-permute-start | bytes 196616 | tf_op jit(solution)/shard_map/ppermute | solution.py:25
  43.0 0.0 collective-permute-done.8.refs_1_
  43.0 1.4 %collective-permute-start.19 = (f32[128,128]{1,0:T(8,128)S(1)}, f32[128,128]{1,0:T(8,128)S(1)}, u32[]{:S(2)}, u32[]{:S(2)}) collective-permute-start(f32[128,128]{1,0:T(8,128)S(1)} %steps.5.refs_0_), channel_id=1, source_target_pairs={{0,24},{4,28},{8,16},{12,20},{16,8},{20,12},{24,0},{28,4},{1,25},{... | collective-permute-start | bytes 196616 | tf_op jit(solution)/shard_map/ppermute | solution.py:25
  44.3 0.0 collective-permute-done.9.refs_2_
  44.3 0.3 steps.4.refs_0_
  44.6 1.5 %collective-permute-start.11 = (f32[128,128]{1,0:T(8,128)S(1)}, f32[128,128]{1,0:T(8,128)S(1)}, u32[]{:S(2)}, u32[]{:S(2)}) collective-permute-start(f32[128,128]{1,0:T(8,128)S(1)} %steps.4.refs_0_), channel_id=1, source_target_pairs={{0,8},{4,12},{8,0},{12,4},{16,24},{20,28},{24,16},{28,20},{1,9},{5... | collective-permute-start | bytes 196616 | tf_op jit(solution)/shard_map/ppermute | solution.py:25
  46.1 0.8 %collective-permute-start.12 = (f32[128,128]{1,0:T(8,128)S(1)}, f32[128,128]{1,0:T(8,128)S(1)}, u32[]{:S(2)}, u32[]{:S(2)}) collective-permute-start(f32[128,128]{1,0:T(8,128)S(1)} %steps.4.refs_0_), channel_id=1, source_target_pairs={{0,16},{4,20},{8,24},{12,28},{16,0},{20,4},{24,8},{28,12},{1,17},{... | collective-permute-start | bytes 196616 | tf_op jit(solution)/shard_map/ppermute | solution.py:25
  46.9 1.3 %collective-permute-start.13 = (f32[128,128]{1,0:T(8,128)S(1)}, f32[128,128]{1,0:T(8,128)S(1)}, u32[]{:S(2)}, u32[]{:S(2)}) collective-permute-start(f32[128,128]{1,0:T(8,128)S(1)} %steps.4.refs_0_), channel_id=1, source_target_pairs={{0,24},{4,28},{8,16},{12,20},{16,8},{20,12},{24,0},{28,4},{1,25},{... | collective-permute-start | bytes 196616 | tf_op jit(solution)/shard_map/ppermute | solution.py:25
  48.1 0.4 collective-permute-done.19.refs_3_
  48.6 0.4 early_rows.1.refs_4_
  49.0 0.5 collective-permute-done.11.refs_1_
  49.5 1.5 %collective-permute-done.12.refs_2_ = f32[128,128]{1,0:T(8,128)S(1)} collective-permute-done((f32[128,128]{1,0:T(8,128)S(1)}, f32[128,128]{1,0:T(8,128)S(1)}, u32[]{:S(2)}, u32[]{:S(2)}) %collective-permute-start.12) | collective-permute-done | bytes 65568 | tf_op jit(solution)/shard_map/ppermute | solution.py:25
  51.0 1.0 %collective-permute-done.13.refs_3_ = f32[128,128]{1,0:T(8,128)S(1)} collective-permute-done((f32[128,128]{1,0:T(8,128)S(1)}, f32[128,128]{1,0:T(8,128)S(1)}, u32[]{:S(2)}, u32[]{:S(2)}) %collective-permute-start.13) | collective-permute-done | bytes 65568 | tf_op jit(solution)/shard_map/ppermute | solution.py:25
  52.0 0.5 late_rows.1
  52.6 0.1 collective-permute-start.21
  52.7 9.5 %all_to_all.5.parts_ref = f32[32,1,128]{2,1,0:T(1,128)S(1)} all-to-all(f32[32,1,128]{2,1,0:T(1,128)S(1)} %get-tuple-element.39), channel_id=1, replica_groups=mesh['cfg'=8,'tm'=4] {'cfg','tm'}, dimensions={0} | all-to-all | bytes 32768 | tf_op jit(solution)/shard_map/all_to_all | solution.py:322
  62.2 0.9 %finish.1 = (f32[256,128]{1,0:T(8,128)}, f32[256,128]{1,0:T(8,128)}) custom-call(f32[32,1,128]{2,1,0:T(1,128)S(1)} %all_to_all.5.parts_ref, f32[256,128]{1,0:T(8,128)S(1)} %get-tuple-element.22.refs_0_.refs_4_.refs_10_.residual_ref, f32[256,128]{1,0:T(8,128)S(1)} %get-tuple-element.40.own_ref, f32[256,128]{1,0:T(8,128)S(1)} %collective-permute-done.21.near_ref, ...), custom_call_target="tpu_custom_call" | custom-call | tf_op jit(solution)/shard_map/finish/pallas_call | solution.py:41
  (12 shorter events, 0.0 us)
Async XLA Ops:
  0.6 16.1 %copy-start = (f32[128,512]{1,0:T(8,128)S(1)}, f32[128,512]{1,0:T(8,128)}, u32[]{:S(2)}) copy-start(f32[128,512]{1,0:T(8,128)} %steps_ref.1) | copy-start | bytes 786436
  1.9 15.0 %collective-permute-start = (f32[256,128]{1,0:T(8,128)S(1)}, f32[256,128]{1,0:T(8,128)S(1)}, u32[]{:S(2)}, u32[]{:S(2)}) collective-permute-start(f32[256,128]{1,0:T(8,128)S(1)} %get-tuple-element.22.refs_0_.refs_4_.refs_10_.residual_ref), channel_id=1, source_target_pairs={{0,3},{1,2},{2,1},{3,0},{4,7},{5,6},{6,5},{7,4},{8,11},{9,10},{10,... | collective-permute-start | bytes 393224 | tf_op jit(solution)/shard_map/ppermute | solution.py:37
  7.0 11.1 %collective-permute-start.1 = (f32[256,128]{1,0:T(8,128)S(1)}, f32[256,128]{1,0:T(8,128)S(1)}, u32[]{:S(2)}, u32[]{:S(2)}) collective-permute-start(f32[256,128]{1,0:T(8,128)S(1)} %get-tuple-element.22.refs_0_.refs_4_.refs_10_.residual_ref), channel_id=1, source_target_pairs={{0,2},{1,3},{2,0},{3,1},{4,6},{5,7},{6,4},{7,5},{8,10},{9,11},{10,... | collective-permute-start | bytes 393224 | tf_op jit(solution)/shard_map/ppermute | solution.py:37
  7.0 11.1 %collective-permute-start.2 = (f32[256,128]{1,0:T(8,128)S(1)}, f32[256,128]{1,0:T(8,128)S(1)}, u32[]{:S(2)}, u32[]{:S(2)}) collective-permute-start(f32[256,128]{1,0:T(8,128)S(1)} %get-tuple-element.22.refs_0_.refs_4_.refs_10_.residual_ref), channel_id=1, source_target_pairs={{0,1},{1,0},{2,3},{3,2},{4,5},{5,4},{6,7},{7,6},{8,9},{9,8},{10,11... | collective-permute-start | bytes 393224 | tf_op jit(solution)/shard_map/ppermute | solution.py:37
  7.6 9.1 %collective-permute-start.3 = (f32[64,256]{1,0:T(8,128)S(1)}, f32[64,256]{1,0:T(8,128)S(1)}, u32[]{:S(2)}, u32[]{:S(2)}) collective-permute-start(f32[64,256]{1,0:T(8,128)S(1)} %get-tuple-element.23), channel_id=1, source_target_pairs={{0,4},{4,0},{8,12},{12,8},{16,20},{20,16},{24,28},{28,24},{1,5},{5... | collective-permute-start | bytes 196616 | tf_op jit(solution)/shard_map/ppermute | solution.py:29
  18.4 6.8 %collective-permute-start.6 = (f32[256,128]{1,0:T(8,128)S(1)}, f32[256,128]{1,0:T(8,128)S(1)}, u32[]{:S(2)}, u32[]{:S(2)}) collective-permute-start(f32[256,128]{1,0:T(8,128)S(1)} %steps.3._.refs_0_), channel_id=1, source_target_pairs={{0,24},{4,28},{8,16},{12,20},{16,8},{20,12},{24,0},{28,4},{1,25},{... | collective-permute-start | bytes 393224 | tf_op jit(solution)/shard_map/ppermute | solution.py:25
  21.0 5.8 %collective-permute-start.4 = (f32[256,128]{1,0:T(8,128)S(1)}, f32[256,128]{1,0:T(8,128)S(1)}, u32[]{:S(2)}, u32[]{:S(2)}) collective-permute-start(f32[256,128]{1,0:T(8,128)S(1)} %steps.3._.refs_0_), channel_id=1, source_target_pairs={{0,16},{4,20},{8,24},{12,28},{16,0},{20,4},{24,8},{28,12},{1,17},{... | collective-permute-start | bytes 393224 | tf_op jit(solution)/shard_map/ppermute | solution.py:25
  21.5 5.4 %collective-permute-start.5 = (f32[256,128]{1,0:T(8,128)S(1)}, f32[256,128]{1,0:T(8,128)S(1)}, u32[]{:S(2)}, u32[]{:S(2)}) collective-permute-start(f32[256,128]{1,0:T(8,128)S(1)} %steps.3._.refs_0_), channel_id=1, source_target_pairs={{0,8},{4,12},{8,0},{12,4},{16,24},{20,28},{24,16},{28,20},{1,9},{5... | collective-permute-start | bytes 393224 | tf_op jit(solution)/shard_map/ppermute | solution.py:25
  27.3 1.4 %collective-permute-start.7 = (f32[256,128]{1,0:T(8,128)S(1)}, f32[256,128]{1,0:T(8,128)S(1)}, u32[]{:S(2)}, u32[]{:S(2)}) collective-permute-start(f32[256,128]{1,0:T(8,128)S(1)} %get-tuple-element.33), channel_id=1, source_target_pairs={{0,4},{4,0},{8,12},{12,8},{16,20},{20,16},{24,28},{28,24},{1,5},{5... | collective-permute-start | bytes 393224 | tf_op jit(solution)/shard_map/ppermute | solution.py:29
  28.9 6.9 %collective-permute-start.14 = (f32[128,128]{1,0:T(8,128)S(1)}, f32[128,128]{1,0:T(8,128)S(1)}, u32[]{:S(2)}, u32[]{:S(2)}) collective-permute-start(f32[128,128]{1,0:T(8,128)S(1)} %get-tuple-element.37.refs_0_), channel_id=1, source_target_pairs={{0,3},{1,2},{2,1},{3,0},{4,7},{5,6},{6,5},{7,4},{8,11},{9,10},{10,... | collective-permute-start | bytes 196616 | tf_op jit(solution)/shard_map/ppermute | solution.py:37
  31.3 6.7 %collective-permute-start.15 = (f32[128,128]{1,0:T(8,128)S(1)}, f32[128,128]{1,0:T(8,128)S(1)}, u32[]{:S(2)}, u32[]{:S(2)}) collective-permute-start(f32[128,128]{1,0:T(8,128)S(1)} %get-tuple-element.37.refs_0_), channel_id=1, source_target_pairs={{0,1},{1,0},{2,3},{3,2},{4,5},{5,4},{6,7},{7,6},{8,9},{9,8},{10,11... | collective-permute-start | bytes 196616 | tf_op jit(solution)/shard_map/ppermute | solution.py:37
  31.3 9.1 %collective-permute-start.16 = (f32[128,128]{1,0:T(8,128)S(1)}, f32[128,128]{1,0:T(8,128)S(1)}, u32[]{:S(2)}, u32[]{:S(2)}) collective-permute-start(f32[128,128]{1,0:T(8,128)S(1)} %get-tuple-element.37.refs_0_), channel_id=1, source_target_pairs={{0,2},{1,3},{2,0},{3,1},{4,6},{5,7},{6,4},{7,5},{8,10},{9,11},{10,... | collective-permute-start | bytes 196616 | tf_op jit(solution)/shard_map/ppermute | solution.py:37
  33.3 9.6 %collective-permute-start.10 = (f32[128,128]{1,0:T(8,128)S(1)}, f32[128,128]{1,0:T(8,128)S(1)}, u32[]{:S(2)}, u32[]{:S(2)}) collective-permute-start(f32[128,128]{1,0:T(8,128)S(1)} %get-tuple-element.36.refs_0_), channel_id=1, source_target_pairs={{0,3},{1,2},{2,1},{3,0},{4,7},{5,6},{6,5},{7,4},{8,11},{9,10},{10,... | collective-permute-start | bytes 196616 | tf_op jit(solution)/shard_map/ppermute | solution.py:37
  35.7 7.3 %collective-permute-start.8 = (f32[128,128]{1,0:T(8,128)S(1)}, f32[128,128]{1,0:T(8,128)S(1)}, u32[]{:S(2)}, u32[]{:S(2)}) collective-permute-start(f32[128,128]{1,0:T(8,128)S(1)} %get-tuple-element.36.refs_0_), channel_id=1, source_target_pairs={{0,1},{1,0},{2,3},{3,2},{4,5},{5,4},{6,7},{7,6},{8,9},{9,8},{10,11... | collective-permute-start | bytes 196616 | tf_op jit(solution)/shard_map/ppermute | solution.py:37
  35.7 8.6 %collective-permute-start.9 = (f32[128,128]{1,0:T(8,128)S(1)}, f32[128,128]{1,0:T(8,128)S(1)}, u32[]{:S(2)}, u32[]{:S(2)}) collective-permute-start(f32[128,128]{1,0:T(8,128)S(1)} %get-tuple-element.36.refs_0_), channel_id=1, source_target_pairs={{0,2},{1,3},{2,0},{3,1},{4,6},{5,7},{6,4},{7,5},{8,10},{9,11},{10,... | collective-permute-start | bytes 196616 | tf_op jit(solution)/shard_map/ppermute | solution.py:37
  40.7 5.4 %collective-permute-start.17 = (f32[128,128]{1,0:T(8,128)S(1)}, f32[128,128]{1,0:T(8,128)S(1)}, u32[]{:S(2)}, u32[]{:S(2)}) collective-permute-start(f32[128,128]{1,0:T(8,128)S(1)} %steps.5.refs_0_), channel_id=1, source_target_pairs={{0,8},{4,12},{8,0},{12,4},{16,24},{20,28},{24,16},{28,20},{1,9},{5... | collective-permute-start | bytes 196616 | tf_op jit(solution)/shard_map/ppermute | solution.py:25
  42.2 4.7 %collective-permute-start.18 = (f32[128,128]{1,0:T(8,128)S(1)}, f32[128,128]{1,0:T(8,128)S(1)}, u32[]{:S(2)}, u32[]{:S(2)}) collective-permute-start(f32[128,128]{1,0:T(8,128)S(1)} %steps.5.refs_0_), channel_id=1, source_target_pairs={{0,16},{4,20},{8,24},{12,28},{16,0},{20,4},{24,8},{28,12},{1,17},{... | collective-permute-start | bytes 196616 | tf_op jit(solution)/shard_map/ppermute | solution.py:25
  42.9 9.1 %collective-permute-start.20 = (f32[256,128]{1,0:T(8,128)S(1)}, f32[256,128]{1,0:T(8,128)S(1)}, u32[]{:S(2)}, u32[]{:S(2)}) collective-permute-start(f32[256,128]{1,0:T(8,128)S(1)} %get-tuple-element.38.refs_8_.image_ref), channel_id=1, source_target_pairs={{0,4},{4,0},{8,12},{12,8},{16,20},{20,16},{24,28},{28,24},{1,5},{5... | collective-permute-start | bytes 393224 | tf_op jit(solution)/shard_map/ppermute | solution.py:29
  43.0 5.6 %collective-permute-start.19 = (f32[128,128]{1,0:T(8,128)S(1)}, f32[128,128]{1,0:T(8,128)S(1)}, u32[]{:S(2)}, u32[]{:S(2)}) collective-permute-start(f32[128,128]{1,0:T(8,128)S(1)} %steps.5.refs_0_), channel_id=1, source_target_pairs={{0,24},{4,28},{8,16},{12,20},{16,8},{20,12},{24,0},{28,4},{1,25},{... | collective-permute-start | bytes 196616 | tf_op jit(solution)/shard_map/ppermute | solution.py:25
  44.6 5.0 %collective-permute-start.11 = (f32[128,128]{1,0:T(8,128)S(1)}, f32[128,128]{1,0:T(8,128)S(1)}, u32[]{:S(2)}, u32[]{:S(2)}) collective-permute-start(f32[128,128]{1,0:T(8,128)S(1)} %steps.4.refs_0_), channel_id=1, source_target_pairs={{0,8},{4,12},{8,0},{12,4},{16,24},{20,28},{24,16},{28,20},{1,9},{5... | collective-permute-start | bytes 196616 | tf_op jit(solution)/shard_map/ppermute | solution.py:25
  46.1 5.0 %collective-permute-start.12 = (f32[128,128]{1,0:T(8,128)S(1)}, f32[128,128]{1,0:T(8,128)S(1)}, u32[]{:S(2)}, u32[]{:S(2)}) collective-permute-start(f32[128,128]{1,0:T(8,128)S(1)} %steps.4.refs_0_), channel_id=1, source_target_pairs={{0,16},{4,20},{8,24},{12,28},{16,0},{20,4},{24,8},{28,12},{1,17},{... | collective-permute-start | bytes 196616 | tf_op jit(solution)/shard_map/ppermute | solution.py:25
  46.9 5.2 %collective-permute-start.13 = (f32[128,128]{1,0:T(8,128)S(1)}, f32[128,128]{1,0:T(8,128)S(1)}, u32[]{:S(2)}, u32[]{:S(2)}) collective-permute-start(f32[128,128]{1,0:T(8,128)S(1)} %steps.4.refs_0_), channel_id=1, source_target_pairs={{0,24},{4,28},{8,16},{12,20},{16,8},{20,12},{24,0},{28,4},{1,25},{... | collective-permute-start | bytes 196616 | tf_op jit(solution)/shard_map/ppermute | solution.py:25
  52.6 9.6 %collective-permute-start.21 = (f32[256,128]{1,0:T(8,128)S(1)}, f32[256,128]{1,0:T(8,128)S(1)}, u32[]{:S(2)}, u32[]{:S(2)}) collective-permute-start(f32[256,128]{1,0:T(8,128)S(1)} %get-tuple-element.41), channel_id=1, source_target_pairs={{0,4},{4,0},{8,12},{12,8},{16,20},{20,16},{24,28},{28,24},{1,5},{5... | collective-permute-start | bytes 393224 | tf_op jit(solution)/shard_map/ppermute | solution.py:29

commit v9 on v8

--- a/solution.py
+++ b/solution.py
@@ -118,7 +118,7 @@
     return both[:, :width] + (both[:, width:] + mul(low, field_high))
 
 
-def layers_kernel(layer_ref, steps_ref, _, __, high_ref, low_ref):
+def layers_kernel(layer_ref, steps_ref, _, high_ref, low_ref):
     width = steps_ref.shape[0]
     for place, offset in enumerate(offsets_tm(steps_ref.shape[1] // width)):
         at = pl.ds(place * width, width)
@@ -177,10 +177,10 @@
     near_ref[...] = mixed[own_ref.shape[0] :]
 
 
-def rows_share(at, size, pieces, high_ref, low_ref):
-    step = high_ref.shape[1] // len(pieces)
+def rows_share(at, size, places, blocks, pieces, high_ref, low_ref):
+    step = high_ref.shape[1] // blocks
     high, low = (
-        jnp.concatenate([ref[:, pl.ds(place * step + at, size)] for place in range(len(pieces))], axis=1)
+        jnp.concatenate([ref[:, pl.ds(place * step + at, size)] for place in places], axis=1)
         for ref in (high_ref, low_ref)
     )
     return mul_tile(high, low, jnp.concatenate([piece[...] for piece in pieces], axis=0))
@@ -188,14 +188,23 @@
 
 def early_rows_kernel(*refs):
     pieces, (high_ref, low_ref, out_ref) = refs[:-3], refs[-3:]
-    out_ref[...] = rows_share(0, pieces[0].shape[0], pieces, high_ref, low_ref)
-
-
-def late_rows_kernel(*refs):
+    out_ref[...] = rows_share(0, pieces[0].shape[0], range(len(pieces)), len(pieces), pieces, high_ref, low_ref)
+
+
+def middle_rows_kernel(blocks, *refs):
+    pieces, (early_ref, high_ref, low_ref, out_ref) = refs[:-4], refs[-4:]
+    size = pieces[0].shape[0]
+    share_of = rows_share(out_ref.shape[0] // 2 - size, size, range(len(pieces)), blocks, pieces, high_ref, low_ref)
+    out_ref[...] = early_ref[...] + share_of
+
+
+def late_rows_kernel(blocks, *refs):
     pieces, (early_ref, high_ref, low_ref, ridge_ref, image_ref, image_near_ref, residual_ref) = refs[:-10], refs[-10:-3]
     own_ref, near_ref, parts_ref = refs[-3:]
     size = pieces[0].shape[0]
-    mixed = early_ref[...] + rows_share(own_ref.shape[0] - size, size, pieces, high_ref, low_ref)
+    mixed = early_ref[...] + rows_share(
+        own_ref.shape[0] - size, size, range(blocks - len(pieces), blocks), blocks, pieces, high_ref, low_ref
+    )
     own, near = mixed[: own_ref.shape[0]], mixed[own_ref.shape[0] :]
     own_ref[...], near_ref[...] = own, near
     image, residual = image_ref[...], residual_ref[...]
@@ -265,7 +274,7 @@
         groups = [[first + core for first in range(0, cfg, 2)] for core in range(2)]
         every, near = lax.all_gather(scaled, "cfg", axis_index_groups=groups), near_cfg(scaled)
         steps_high, steps_low = call(
-            layers_kernel, "layers", (steps, steps), layer, time_kernel, every, near, scalars=1, unread=2
+            layers_kernel, "layers", (steps, steps), layer, time_kernel, every, scalars=1, unread=1
         )
         def over_time(field, *places):
             pieces, places = gather_tm(field), places or tuple(range(tm))
@@ -313,11 +322,18 @@
 
         ones, twos = far_cfg(over_time(one)), far_cfg(over_time(two, 0, *range(2, tm), 1))
         partial = call(early_rows_kernel, "early_rows", shape(2 * rows, width), *ones, high, low)
+        soon = (last + 1) // 2
+        partial = call(
+            functools.partial(middle_rows_kernel, last + 1),
+            "middle_rows",
+            shape(2 * rows, width),
+            *twos[:soon], partial, high, low,
+        )
         own, theirs, sums = call(
-            late_rows_kernel,
+            functools.partial(late_rows_kernel, last + 1),
             "late_rows",
             (block, block, shape(cfg * tm, 1, width)),
-            *twos, partial, high, low, ridge, image, near_cfg(image), residual,
+            *twos[soon:], partial, high, low, ridge, image, near_cfg(image), residual,
         )
         sums = lax.all_to_all(sums, ("cfg", "tm"), 0, 0, tiled=True)
         return call(

time: 63.3 us -> 63.1 us (level)
    ppermute x9, waiting for transfers between devices: 6.24 us -> 4.64 us  [far_cfg(): lax.ppermute(block, 'cfg', partners('cfg', d))]
    ppermute x4, waiting for transfers between devices: 1.34 us -> 2.59 us  [near_cfg(): return lax.ppermute(block, 'cfg', partners('cfg', 1))]
    pallas_call x12 -> x13, Pallas kernels: 6.69 us -> 6.86 us  [call(): pl.pallas_call(kernel, out_shape=outs, in_specs=[SMEM] * scalars + [space...]
  transfers between devices with their start and end apart: 22 -> 22, of which waited for: 12 -> 13; matrix products, arithmetic and copies ran while one was open for 0% -> 0% of each run, Pallas kernels for 5% -> 5%
where the time goes in v9:
time: 63.1 us; the launch traced here: 63 us
  starting transfers between devices  25.4 us (40%)
  blocking collectives  18.7 us (30%)
  waiting for transfers between devices  11.2 us (18%)
  Pallas kernels  6.86 us (11%)
  between operations  0.77 us (1%)
    ppermute x9, starting transfers between devices, gather_tm(): lax.ppermute(block, 'tm', partners('tm', d))  14.5 us
    ppermute x9, starting transfers between devices, far_cfg(): lax.ppermute(block, 'cfg', partners('cfg', d))  10.7 us
    all_to_all x1, blocking collectives, body(): sums = lax.all_to_all(sums, ('cfg', 'tm'), 0, 0, tiled=True)  9.62 us
    all_gather x1, blocking collectives, body(): lax.all_gather(scaled, 'cfg', axis_index_groups=groups)  9.13 us
    pallas_call x13, Pallas kernels, call(): pl.pallas_call(kernel, out_shape=outs, in_specs=[SMEM] * scalars + [space...  6.86 us
    ppermute x9, waiting for transfers between devices, far_cfg(): lax.ppermute(block, 'cfg', partners('cfg', d))  4.64 us
    ppermute x9, waiting for transfers between devices, gather_tm(): lax.ppermute(block, 'tm', partners('tm', d))  3.97 us
    ppermute x4, waiting for transfers between devices, near_cfg(): return lax.ppermute(block, 'cfg', partners('cfg', 1))  2.59 us
  transfers between devices with their start and end apart: 22, of which 13 were waited for; matrix products, arithmetic and copies ran while one was open for 0% of the time, Pallas kernels for 5%

profile of v9, /device:TPU:0, one launch (start us, length us, event | category | flops | bytes accessed | tf_op | source)
XLA Modules:
  0.0 63.0 jit_solution(3361432198279100507)
XLA Ops:
  0.6 1.2 %begin.1 = (f32[256,128]{1,0:T(8,128)S(1)}, f32[64,256]{1,0:T(8,128)S(1)}, f32[1,256]{1,0:T(1,128)S(1)}, f32[1,256]{1,0:T(1,128)S(1)}) custom-call(f32[256,128]{1,0:T(8,128)} %targets_hbm.1, f32[64,256]{1,0:T(8,128)} %bitcast.9, f32[1,64]{1,0:T(1,128)} %bitcast.12, s32[1,256]{1,0:T(1,128)} %bitcast.10, f32[1,256]{1,0:T(1,128)} %bitcast.11), custom_call_target="tpu_custom_call" | custom-call | tf_op jit(solution)/shard_map/begin/pallas_call | solution.py:41
  1.9 5.1 %collective-permute-start = (f32[256,128]{1,0:T(8,128)S(1)}, f32[256,128]{1,0:T(8,128)S(1)}, u32[]{:S(2)}, u32[]{:S(2)}) collective-permute-start(f32[256,128]{1,0:T(8,128)S(1)} %get-tuple-element.22.refs_0_.refs_4_.refs_8_.residual_ref), channel_id=1, source_target_pairs={{0,3},{1,2},{2,1},{3,0},{4,7},{5,6},{6,5},{7,4},{8,11},{9,10},{10,... | collective-permute-start | bytes 393224 | tf_op jit(solution)/shard_map/ppermute | solution.py:37
  7.0 0.6 %collective-permute-start.2 = (f32[256,128]{1,0:T(8,128)S(1)}, f32[256,128]{1,0:T(8,128)S(1)}, u32[]{:S(2)}, u32[]{:S(2)}) collective-permute-start(f32[256,128]{1,0:T(8,128)S(1)} %get-tuple-element.22.refs_0_.refs_4_.refs_8_.residual_ref), channel_id=1, source_target_pairs={{0,1},{1,0},{2,3},{3,2},{4,5},{5,4},{6,7},{7,6},{8,9},{9,8},{10,11... | collective-permute-start | bytes 393224 | tf_op jit(solution)/shard_map/ppermute | solution.py:37
  7.6 9.1 %all-gather = f32[256,256]{1,0:T(8,128)S(1)} all-gather(f32[64,256]{1,0:T(8,128)S(1)} %get-tuple-element.23), channel_id=2, replica_groups={{0,8,16,24},{4,12,20,28},{1,9,17,25},{5,13,21,29},{2,10,18,26},{6,14,22..., dimensions={0}, use_global_device_ids=true | all-gather | bytes 327680 | tf_op jit(solution)/shard_map/all_gather | solution.py:275
  16.8 0.1 layers.1
  16.8 0.0 collective-permute-done.refs_1_
  16.8 1.2 %collective-permute-done.1.refs_2_ = f32[256,128]{1,0:T(8,128)S(1)} collective-permute-done((f32[256,128]{1,0:T(8,128)S(1)}, f32[256,128]{1,0:T(8,128)S(1)}, u32[]{:S(2)}, u32[]{:S(2)}) %collective-permute-start.1) | collective-permute-done | bytes 131104 | tf_op jit(solution)/shard_map/ppermute | solution.py:37
  18.1 0.4 steps.3._.refs_0_
  18.4 2.5 %collective-permute-start.6 = (f32[256,128]{1,0:T(8,128)S(1)}, f32[256,128]{1,0:T(8,128)S(1)}, u32[]{:S(2)}, u32[]{:S(2)}) collective-permute-start(f32[256,128]{1,0:T(8,128)S(1)} %steps.3._.refs_0_), channel_id=1, source_target_pairs={{0,24},{4,28},{8,16},{12,20},{16,8},{20,12},{24,0},{28,4},{1,25},{... | collective-permute-start | bytes 393224 | tf_op jit(solution)/shard_map/ppermute | solution.py:25
  21.0 0.5 collective-permute-start.3
  21.5 0.5 collective-permute-start.4
  22.0 0.0 collective-permute-start.5
  22.0 1.3 %collective-permute-done.5.near_ref = f32[64,256]{1,0:T(8,128)S(1)} collective-permute-done((f32[64,256]{1,0:T(8,128)S(1)}, f32[64,256]{1,0:T(8,128)S(1)}, u32[]{:S(2)}, u32[]{:S(2)}) %collective-permute-start.5) | collective-permute-done | bytes 65568 | tf_op jit(solution)/shard_map/ppermute | solution.py:29
  23.3 1.6 %tile.1 = (bf16[512,1024]{1,0:T(8,128)(2,1)S(1)}, bf16[512,1024]{1,0:T(8,128)(2,1)S(1)}, f32[256,1]{1,0:T(8,128)S(1)}, f32[256,1]{1,0:T(8,128)S(1)}) custom-call(s32[1]{0:T(128)} %bitcast.6.pair_ref, f32[64,256]{1,0:T(8,128)S(1)} %collective-permute-done.5.near_ref, f32[4,64,256]{2,1,0:T(8,128)S(1)} %bitcast.8, f32[1,256]{1,0:T(1,128)S(1)} %get-tuple-element.26.mask_ref, ...), custom_call_target="tpu_custom_call" | custom-call | tf_op jit(solution)/shard_map/tile/pallas_call | solution.py:41
  24.9 0.3 collective-permute-done.6.refs_1_
  25.2 0.4 early.1.refs_2_
  25.7 1.1 %collective-permute-done.3.refs_0_ = f32[256,128]{1,0:T(8,128)S(1)} collective-permute-done((f32[256,128]{1,0:T(8,128)S(1)}, f32[256,128]{1,0:T(8,128)S(1)}, u32[]{:S(2)}, u32[]{:S(2)}) %collective-permute-start.3) | collective-permute-done | bytes 131104 | tf_op jit(solution)/shard_map/ppermute | solution.py:25
  26.8 0.1 collective-permute-done.4.refs_1_
  26.9 0.4 late.1
  27.3 0.1 collective-permute-start.7
  27.4 1.3 %collective-permute-done.7.refs_1_ = f32[256,128]{1,0:T(8,128)S(1)} collective-permute-done((f32[256,128]{1,0:T(8,128)S(1)}, f32[256,128]{1,0:T(8,128)S(1)}, u32[]{:S(2)}, u32[]{:S(2)}) %collective-permute-start.7) | collective-permute-done | bytes 131104 | tf_op jit(solution)/shard_map/ppermute | solution.py:29
  28.7 0.1 image.1
  28.9 2.4 %collective-permute-start.14 = (f32[128,128]{1,0:T(8,128)S(1)}, f32[128,128]{1,0:T(8,128)S(1)}, u32[]{:S(2)}, u32[]{:S(2)}) collective-permute-start(f32[128,128]{1,0:T(8,128)S(1)} %get-tuple-element.37.refs_0_), channel_id=1, source_target_pairs={{0,3},{1,2},{2,1},{3,0},{4,7},{5,6},{6,5},{7,4},{8,11},{9,10},{10,... | collective-permute-start | bytes 196616 | tf_op jit(solution)/shard_map/ppermute | solution.py:37
  31.3 2.1 %collective-permute-start.16 = (f32[128,128]{1,0:T(8,128)S(1)}, f32[128,128]{1,0:T(8,128)S(1)}, u32[]{:S(2)}, u32[]{:S(2)}) collective-permute-start(f32[128,128]{1,0:T(8,128)S(1)} %get-tuple-element.37.refs_0_), channel_id=1, source_target_pairs={{0,2},{1,3},{2,0},{3,1},{4,6},{5,7},{6,4},{7,5},{8,10},{9,11},{10,... | collective-permute-start | bytes 196616 | tf_op jit(solution)/shard_map/ppermute | solution.py:37
  33.3 2.3 %collective-permute-start.10 = (f32[128,128]{1,0:T(8,128)S(1)}, f32[128,128]{1,0:T(8,128)S(1)}, u32[]{:S(2)}, u32[]{:S(2)}) collective-permute-start(f32[128,128]{1,0:T(8,128)S(1)} %get-tuple-element.36.refs_0_), channel_id=1, source_target_pairs={{0,3},{1,2},{2,1},{3,0},{4,7},{5,6},{6,5},{7,4},{8,11},{9,10},{10,... | collective-permute-start | bytes 196616 | tf_op jit(solution)/shard_map/ppermute | solution.py:37
  35.6 0.1 collective-permute-done.14.refs_1_
  35.7 2.0 %collective-permute-start.9 = (f32[128,128]{1,0:T(8,128)S(1)}, f32[128,128]{1,0:T(8,128)S(1)}, u32[]{:S(2)}, u32[]{:S(2)}) collective-permute-start(f32[128,128]{1,0:T(8,128)S(1)} %get-tuple-element.36.refs_0_), channel_id=1, source_target_pairs={{0,2},{1,3},{2,0},{3,1},{4,6},{5,7},{6,4},{7,5},{8,10},{9,11},{10,... | collective-permute-start | bytes 196616 | tf_op jit(solution)/shard_map/ppermute | solution.py:37
  37.7 0.3 collective-permute-done.15.refs_2_
  38.0 2.4 %collective-permute-done.16.refs_3_ = f32[128,128]{1,0:T(8,128)S(1)} collective-permute-done((f32[128,128]{1,0:T(8,128)S(1)}, f32[128,128]{1,0:T(8,128)S(1)}, u32[]{:S(2)}, u32[]{:S(2)}) %collective-permute-start.16) | collective-permute-done | bytes 65568 | tf_op jit(solution)/shard_map/ppermute | solution.py:37
  40.4 0.3 steps.5.refs_0_
  40.6 1.5 %collective-permute-start.17 = (f32[128,128]{1,0:T(8,128)S(1)}, f32[128,128]{1,0:T(8,128)S(1)}, u32[]{:S(2)}, u32[]{:S(2)}) collective-permute-start(f32[128,128]{1,0:T(8,128)S(1)} %steps.5.refs_0_), channel_id=1, source_target_pairs={{0,8},{4,12},{8,0},{12,4},{16,24},{20,28},{24,16},{28,20},{1,9},{5... | collective-permute-start | bytes 196616 | tf_op jit(solution)/shard_map/ppermute | solution.py:25
  42.2 0.7 %collective-permute-start.18 = (f32[128,128]{1,0:T(8,128)S(1)}, f32[128,128]{1,0:T(8,128)S(1)}, u32[]{:S(2)}, u32[]{:S(2)}) collective-permute-start(f32[128,128]{1,0:T(8,128)S(1)} %steps.5.refs_0_), channel_id=1, source_target_pairs={{0,16},{4,20},{8,24},{12,28},{16,0},{20,4},{24,8},{28,12},{1,17},{... | collective-permute-start | bytes 196616 | tf_op jit(solution)/shard_map/ppermute | solution.py:25
  42.9 0.0 collective-permute-start.20
  42.9 1.4 %collective-permute-start.19 = (f32[128,128]{1,0:T(8,128)S(1)}, f32[128,128]{1,0:T(8,128)S(1)}, u32[]{:S(2)}, u32[]{:S(2)}) collective-permute-start(f32[128,128]{1,0:T(8,128)S(1)} %steps.5.refs_0_), channel_id=1, source_target_pairs={{0,24},{4,28},{8,16},{12,20},{16,8},{20,12},{24,0},{28,4},{1,25},{... | collective-permute-start | bytes 196616 | tf_op jit(solution)/shard_map/ppermute | solution.py:25
  44.3 0.3 steps.4.refs_0_
  44.5 1.5 %collective-permute-start.13 = (f32[128,128]{1,0:T(8,128)S(1)}, f32[128,128]{1,0:T(8,128)S(1)}, u32[]{:S(2)}, u32[]{:S(2)}) collective-permute-start(f32[128,128]{1,0:T(8,128)S(1)} %steps.4.refs_0_), channel_id=1, source_target_pairs={{0,8},{4,12},{8,0},{12,4},{16,24},{20,28},{24,16},{28,20},{1,9},{5... | collective-permute-start | bytes 196616 | tf_op jit(solution)/shard_map/ppermute | solution.py:25
  46.1 0.7 %collective-permute-start.11 = (f32[128,128]{1,0:T(8,128)S(1)}, f32[128,128]{1,0:T(8,128)S(1)}, u32[]{:S(2)}, u32[]{:S(2)}) collective-permute-start(f32[128,128]{1,0:T(8,128)S(1)} %steps.4.refs_0_), channel_id=1, source_target_pairs={{0,16},{4,20},{8,24},{12,28},{16,0},{20,4},{24,8},{28,12},{1,17},{... | collective-permute-start | bytes 196616 | tf_op jit(solution)/shard_map/ppermute | solution.py:25
  46.8 1.3 %collective-permute-start.12 = (f32[128,128]{1,0:T(8,128)S(1)}, f32[128,128]{1,0:T(8,128)S(1)}, u32[]{:S(2)}, u32[]{:S(2)}) collective-permute-start(f32[128,128]{1,0:T(8,128)S(1)} %steps.4.refs_0_), channel_id=1, source_target_pairs={{0,24},{4,28},{8,16},{12,20},{16,8},{20,12},{24,0},{28,4},{1,25},{... | collective-permute-start | bytes 196616 | tf_op jit(solution)/shard_map/ppermute | solution.py:25
  48.1 0.3 collective-permute-done.19.refs_3_
  48.4 0.4 early_rows.1.refs_2_
  48.9 0.7 %collective-permute-done.13.refs_1_ = f32[128,128]{1,0:T(8,128)S(1)} collective-permute-done((f32[128,128]{1,0:T(8,128)S(1)}, f32[128,128]{1,0:T(8,128)S(1)}, u32[]{:S(2)}, u32[]{:S(2)}) %collective-permute-start.13) | collective-permute-done | bytes 65568 | tf_op jit(solution)/shard_map/ppermute | solution.py:25
  49.5 0.3 middle_rows.1.refs_2_
  49.8 1.2 %collective-permute-done.11.refs_0_ = f32[128,128]{1,0:T(8,128)S(1)} collective-permute-done((f32[128,128]{1,0:T(8,128)S(1)}, f32[128,128]{1,0:T(8,128)S(1)}, u32[]{:S(2)}, u32[]{:S(2)}) %collective-permute-start.11) | collective-permute-done | bytes 65568 | tf_op jit(solution)/shard_map/ppermute | solution.py:25
  51.0 0.9 %collective-permute-done.12.refs_1_ = f32[128,128]{1,0:T(8,128)S(1)} collective-permute-done((f32[128,128]{1,0:T(8,128)S(1)}, f32[128,128]{1,0:T(8,128)S(1)}, u32[]{:S(2)}, u32[]{:S(2)}) %collective-permute-start.12) | collective-permute-done | bytes 65568 | tf_op jit(solution)/shard_map/ppermute | solution.py:25
  51.9 0.4 late_rows.1
  52.3 0.1 collective-permute-start.21
  52.4 9.6 %all_to_all.5.parts_ref = f32[32,1,128]{2,1,0:T(1,128)S(1)} all-to-all(f32[32,1,128]{2,1,0:T(1,128)S(1)} %get-tuple-element.39), channel_id=1, replica_groups=mesh['cfg'=8,'tm'=4] {'cfg','tm'}, dimensions={0} | all-to-all | bytes 32768 | tf_op jit(solution)/shard_map/all_to_all | solution.py:338
  62.0 0.9 %finish.1 = (f32[256,128]{1,0:T(8,128)}, f32[256,128]{1,0:T(8,128)}) custom-call(f32[32,1,128]{2,1,0:T(1,128)S(1)} %all_to_all.5.parts_ref, f32[256,128]{1,0:T(8,128)S(1)} %get-tuple-element.22.refs_0_.refs_4_.refs_8_.residual_ref, f32[256,128]{1,0:T(8,128)S(1)} %get-tuple-element.40.own_ref, f32[256,128]{1,0:T(8,128)S(1)} %collective-permute-done.21.near_ref, ...), custom_call_target="tpu_custom_call" | custom-call | tf_op jit(solution)/shard_map/finish/pallas_call | solution.py:41
  (13 shorter events, 0.0 us)
Async XLA Ops:
  0.6 16.1 %copy-start = (f32[128,512]{1,0:T(8,128)S(1)}, f32[128,512]{1,0:T(8,128)}, u32[]{:S(2)}) copy-start(f32[128,512]{1,0:T(8,128)} %steps_ref.1) | copy-start | bytes 786436
  1.9 15.0 %collective-permute-start = (f32[256,128]{1,0:T(8,128)S(1)}, f32[256,128]{1,0:T(8,128)S(1)}, u32[]{:S(2)}, u32[]{:S(2)}) collective-permute-start(f32[256,128]{1,0:T(8,128)S(1)} %get-tuple-element.22.refs_0_.refs_4_.refs_8_.residual_ref), channel_id=1, source_target_pairs={{0,3},{1,2},{2,1},{3,0},{4,7},{5,6},{6,5},{7,4},{8,11},{9,10},{10,... | collective-permute-start | bytes 393224 | tf_op jit(solution)/shard_map/ppermute | solution.py:37
  7.0 11.1 %collective-permute-start.1 = (f32[256,128]{1,0:T(8,128)S(1)}, f32[256,128]{1,0:T(8,128)S(1)}, u32[]{:S(2)}, u32[]{:S(2)}) collective-permute-start(f32[256,128]{1,0:T(8,128)S(1)} %get-tuple-element.22.refs_0_.refs_4_.refs_8_.residual_ref), channel_id=1, source_target_pairs={{0,2},{1,3},{2,0},{3,1},{4,6},{5,7},{6,4},{7,5},{8,10},{9,11},{10,... | collective-permute-start | bytes 393224 | tf_op jit(solution)/shard_map/ppermute | solution.py:37
  7.0 11.1 %collective-permute-start.2 = (f32[256,128]{1,0:T(8,128)S(1)}, f32[256,128]{1,0:T(8,128)S(1)}, u32[]{:S(2)}, u32[]{:S(2)}) collective-permute-start(f32[256,128]{1,0:T(8,128)S(1)} %get-tuple-element.22.refs_0_.refs_4_.refs_8_.residual_ref), channel_id=1, source_target_pairs={{0,1},{1,0},{2,3},{3,2},{4,5},{5,4},{6,7},{7,6},{8,9},{9,8},{10,11... | collective-permute-start | bytes 393224 | tf_op jit(solution)/shard_map/ppermute | solution.py:37
  18.4 6.8 %collective-permute-start.6 = (f32[256,128]{1,0:T(8,128)S(1)}, f32[256,128]{1,0:T(8,128)S(1)}, u32[]{:S(2)}, u32[]{:S(2)}) collective-permute-start(f32[256,128]{1,0:T(8,128)S(1)} %steps.3._.refs_0_), channel_id=1, source_target_pairs={{0,24},{4,28},{8,16},{12,20},{16,8},{20,12},{24,0},{28,4},{1,25},{... | collective-permute-start | bytes 393224 | tf_op jit(solution)/shard_map/ppermute | solution.py:25
  21.0 5.8 %collective-permute-start.3 = (f32[256,128]{1,0:T(8,128)S(1)}, f32[256,128]{1,0:T(8,128)S(1)}, u32[]{:S(2)}, u32[]{:S(2)}) collective-permute-start(f32[256,128]{1,0:T(8,128)S(1)} %steps.3._.refs_0_), channel_id=1, source_target_pairs={{0,16},{4,20},{8,24},{12,28},{16,0},{20,4},{24,8},{28,12},{1,17},{... | collective-permute-start | bytes 393224 | tf_op jit(solution)/shard_map/ppermute | solution.py:25
  21.5 5.4 %collective-permute-start.4 = (f32[256,128]{1,0:T(8,128)S(1)}, f32[256,128]{1,0:T(8,128)S(1)}, u32[]{:S(2)}, u32[]{:S(2)}) collective-permute-start(f32[256,128]{1,0:T(8,128)S(1)} %steps.3._.refs_0_), channel_id=1, source_target_pairs={{0,8},{4,12},{8,0},{12,4},{16,24},{20,28},{24,16},{28,20},{1,9},{5... | collective-permute-start | bytes 393224 | tf_op jit(solution)/shard_map/ppermute | solution.py:25
  22.0 1.3 %collective-permute-start.5 = (f32[64,256]{1,0:T(8,128)S(1)}, f32[64,256]{1,0:T(8,128)S(1)}, u32[]{:S(2)}, u32[]{:S(2)}) collective-permute-start(f32[64,256]{1,0:T(8,128)S(1)} %get-tuple-element.23), channel_id=1, source_target_pairs={{0,4},{4,0},{8,12},{12,8},{16,20},{20,16},{24,28},{28,24},{1,5},{5... | collective-permute-start | bytes 196616 | tf_op jit(solution)/shard_map/ppermute | solution.py:29
  27.3 1.4 %collective-permute-start.7 = (f32[256,128]{1,0:T(8,128)S(1)}, f32[256,128]{1,0:T(8,128)S(1)}, u32[]{:S(2)}, u32[]{:S(2)}) collective-permute-start(f32[256,128]{1,0:T(8,128)S(1)} %get-tuple-element.33), channel_id=1, source_target_pairs={{0,4},{4,0},{8,12},{12,8},{16,20},{20,16},{24,28},{28,24},{1,5},{5... | collective-permute-start | bytes 393224 | tf_op jit(solution)/shard_map/ppermute | solution.py:29
  28.9 6.9 %collective-permute-start.14 = (f32[128,128]{1,0:T(8,128)S(1)}, f32[128,128]{1,0:T(8,128)S(1)}, u32[]{:S(2)}, u32[]{:S(2)}) collective-permute-start(f32[128,128]{1,0:T(8,128)S(1)} %get-tuple-element.37.refs_0_), channel_id=1, source_target_pairs={{0,3},{1,2},{2,1},{3,0},{4,7},{5,6},{6,5},{7,4},{8,11},{9,10},{10,... | collective-permute-start | bytes 196616 | tf_op jit(solution)/shard_map/ppermute | solution.py:37
  31.3 6.7 %collective-permute-start.15 = (f32[128,128]{1,0:T(8,128)S(1)}, f32[128,128]{1,0:T(8,128)S(1)}, u32[]{:S(2)}, u32[]{:S(2)}) collective-permute-start(f32[128,128]{1,0:T(8,128)S(1)} %get-tuple-element.37.refs_0_), channel_id=1, source_target_pairs={{0,1},{1,0},{2,3},{3,2},{4,5},{5,4},{6,7},{7,6},{8,9},{9,8},{10,11... | collective-permute-start | bytes 196616 | tf_op jit(solution)/shard_map/ppermute | solution.py:37
  31.3 9.1 %collective-permute-start.16 = (f32[128,128]{1,0:T(8,128)S(1)}, f32[128,128]{1,0:T(8,128)S(1)}, u32[]{:S(2)}, u32[]{:S(2)}) collective-permute-start(f32[128,128]{1,0:T(8,128)S(1)} %get-tuple-element.37.refs_0_), channel_id=1, source_target_pairs={{0,2},{1,3},{2,0},{3,1},{4,6},{5,7},{6,4},{7,5},{8,10},{9,11},{10,... | collective-permute-start | bytes 196616 | tf_op jit(solution)/shard_map/ppermute | solution.py:37
  33.3 9.5 %collective-permute-start.10 = (f32[128,128]{1,0:T(8,128)S(1)}, f32[128,128]{1,0:T(8,128)S(1)}, u32[]{:S(2)}, u32[]{:S(2)}) collective-permute-start(f32[128,128]{1,0:T(8,128)S(1)} %get-tuple-element.36.refs_0_), channel_id=1, source_target_pairs={{0,3},{1,2},{2,1},{3,0},{4,7},{5,6},{6,5},{7,4},{8,11},{9,10},{10,... | collective-permute-start | bytes 196616 | tf_op jit(solution)/shard_map/ppermute | solution.py:37
  35.6 7.2 %collective-permute-start.8 = (f32[128,128]{1,0:T(8,128)S(1)}, f32[128,128]{1,0:T(8,128)S(1)}, u32[]{:S(2)}, u32[]{:S(2)}) collective-permute-start(f32[128,128]{1,0:T(8,128)S(1)} %get-tuple-element.36.refs_0_), channel_id=1, source_target_pairs={{0,1},{1,0},{2,3},{3,2},{4,5},{5,4},{6,7},{7,6},{8,9},{9,8},{10,11... | collective-permute-start | bytes 196616 | tf_op jit(solution)/shard_map/ppermute | solution.py:37
  35.7 8.5 %collective-permute-start.9 = (f32[128,128]{1,0:T(8,128)S(1)}, f32[128,128]{1,0:T(8,128)S(1)}, u32[]{:S(2)}, u32[]{:S(2)}) collective-permute-start(f32[128,128]{1,0:T(8,128)S(1)} %get-tuple-element.36.refs_0_), channel_id=1, source_target_pairs={{0,2},{1,3},{2,0},{3,1},{4,6},{5,7},{6,4},{7,5},{8,10},{9,11},{10,... | collective-permute-start | bytes 196616 | tf_op jit(solution)/shard_map/ppermute | solution.py:37
  40.6 5.4 %collective-permute-start.17 = (f32[128,128]{1,0:T(8,128)S(1)}, f32[128,128]{1,0:T(8,128)S(1)}, u32[]{:S(2)}, u32[]{:S(2)}) collective-permute-start(f32[128,128]{1,0:T(8,128)S(1)} %steps.5.refs_0_), channel_id=1, source_target_pairs={{0,8},{4,12},{8,0},{12,4},{16,24},{20,28},{24,16},{28,20},{1,9},{5... | collective-permute-start | bytes 196616 | tf_op jit(solution)/shard_map/ppermute | solution.py:25
  42.2 4.6 %collective-permute-start.18 = (f32[128,128]{1,0:T(8,128)S(1)}, f32[128,128]{1,0:T(8,128)S(1)}, u32[]{:S(2)}, u32[]{:S(2)}) collective-permute-start(f32[128,128]{1,0:T(8,128)S(1)} %steps.5.refs_0_), channel_id=1, source_target_pairs={{0,16},{4,20},{8,24},{12,28},{16,0},{20,4},{24,8},{28,12},{1,17},{... | collective-permute-start | bytes 196616 | tf_op jit(solution)/shard_map/ppermute | solution.py:25
  42.9 9.1 %collective-permute-start.20 = (f32[256,128]{1,0:T(8,128)S(1)}, f32[256,128]{1,0:T(8,128)S(1)}, u32[]{:S(2)}, u32[]{:S(2)}) collective-permute-start(f32[256,128]{1,0:T(8,128)S(1)} %get-tuple-element.38.refs_6_.image_ref), channel_id=1, source_target_pairs={{0,4},{4,0},{8,12},{12,8},{16,20},{20,16},{24,28},{28,24},{1,5},{5... | collective-permute-start | bytes 393224 | tf_op jit(solution)/shard_map/ppermute | solution.py:29
  42.9 5.6 %collective-permute-start.19 = (f32[128,128]{1,0:T(8,128)S(1)}, f32[128,128]{1,0:T(8,128)S(1)}, u32[]{:S(2)}, u32[]{:S(2)}) collective-permute-start(f32[128,128]{1,0:T(8,128)S(1)} %steps.5.refs_0_), channel_id=1, source_target_pairs={{0,24},{4,28},{8,16},{12,20},{16,8},{20,12},{24,0},{28,4},{1,25},{... | collective-permute-start | bytes 196616 | tf_op jit(solution)/shard_map/ppermute | solution.py:25
  44.5 5.0 %collective-permute-start.13 = (f32[128,128]{1,0:T(8,128)S(1)}, f32[128,128]{1,0:T(8,128)S(1)}, u32[]{:S(2)}, u32[]{:S(2)}) collective-permute-start(f32[128,128]{1,0:T(8,128)S(1)} %steps.4.refs_0_), channel_id=1, source_target_pairs={{0,8},{4,12},{8,0},{12,4},{16,24},{20,28},{24,16},{28,20},{1,9},{5... | collective-permute-start | bytes 196616 | tf_op jit(solution)/shard_map/ppermute | solution.py:25
  46.1 5.0 %collective-permute-start.11 = (f32[128,128]{1,0:T(8,128)S(1)}, f32[128,128]{1,0:T(8,128)S(1)}, u32[]{:S(2)}, u32[]{:S(2)}) collective-permute-start(f32[128,128]{1,0:T(8,128)S(1)} %steps.4.refs_0_), channel_id=1, source_target_pairs={{0,16},{4,20},{8,24},{12,28},{16,0},{20,4},{24,8},{28,12},{1,17},{... | collective-permute-start | bytes 196616 | tf_op jit(solution)/shard_map/ppermute | solution.py:25
  46.8 5.2 %collective-permute-start.12 = (f32[128,128]{1,0:T(8,128)S(1)}, f32[128,128]{1,0:T(8,128)S(1)}, u32[]{:S(2)}, u32[]{:S(2)}) collective-permute-start(f32[128,128]{1,0:T(8,128)S(1)} %steps.4.refs_0_), channel_id=1, source_target_pairs={{0,24},{4,28},{8,16},{12,20},{16,8},{20,12},{24,0},{28,4},{1,25},{... | collective-permute-start | bytes 196616 | tf_op jit(solution)/shard_map/ppermute | solution.py:25
  52.3 9.7 %collective-permute-start.21 = (f32[256,128]{1,0:T(8,128)S(1)}, f32[256,128]{1,0:T(8,128)S(1)}, u32[]{:S(2)}, u32[]{:S(2)}) collective-permute-start(f32[256,128]{1,0:T(8,128)S(1)} %get-tuple-element.41), channel_id=1, source_target_pairs={{0,4},{4,0},{8,12},{12,8},{16,20},{20,16},{24,28},{28,24},{1,5},{5... | collective-permute-start | bytes 393224 | tf_op jit(solution)/shard_map/ppermute | solution.py:29
